TPU v7x, 32 devices: a whole 2x2x4 slice. The times are simulated.
32 devices in a mesh: dp: 8 (over y, x, core), seq: 4 (over z).
Axes of the slice: x: 2, y: 2, z: 4, core: 2. Of those that a mesh axis runs over, the one named last changes fastest.
Arguments:
- inputs: bfloat16 [2, 8, 1024, 768], P(None, 'dp', 'seq'), may hold values from -6 to 6
- segments: int32 [2, 8, 1024], P(None, 'dp', 'seq'), may hold values from 0 to 1023, as said below
- attn_params: bfloat16 [2363392], P(('dp', 'seq'))
- mlp_params: bfloat16 [4726784], P(('dp', 'seq'))
- cotangent: bfloat16 [2, 8, 1024, 768], P(None, 'dp', 'seq'), may hold values from -6 to 6
Outputs:
- outputs: bfloat16 [2, 8, 1024, 768], P(None, 'dp', 'seq')
- input_grad: float32 [2, 8, 1024, 768], P(None, 'dp', 'seq')
- attn_grad: float32 [2363392], P(('dp', 'seq'))
- mlp_grad: float32 [4726784], P(('dp', 'seq'))
Inputs may be any that keep to these rules, and one draw needn't show every extreme that they name: `segments`: along each sequence the segment numbers never fall, and equal numbers mark one document. In each micro-batch one sequence, chosen by the seed, is a single document with all numbers 1024 - 1; every other document has at most 512 tokens.
All inputs are finite; a program needn't handle non-finite values.
Results may differ from a plain program's by a relative error of at most 0.012.
The roundings to bfloat16 on the way count: a program that leaves them out, or rounds other values in their place, can miss the bound.
Values may be sent and summed in bfloat16 or wider, within the bound.
A program may use at most 256 MiB of HBM per device.

v0:
```python
import functools
from functools import partial
import math

import jax
import jax.numpy as jnp
from jax import lax
from jax.experimental import pallas as pl
from jax.experimental.pallas import tpu as pltpu
from jax.sharding import PartitionSpec as P

D = 768
H = 12
HD = 64
FF = 3072


norm_eps = 1e-05
score_floor = -1e30
key_block = 512


def attention_layout():
    return [(D,), (D,), (D, 3 * D), (D,), (D,), (D, D), (D,)]


def mlp_layout():
    return [(D,), (D,), (D, FF), (FF,), (FF, D), (D,)]


def unpack_params(flat_vector, layout):
    offset = 0
    result = []
    for dims_entry in layout:
        amount = math.prod(dims_entry)
        result.append(lax.slice_in_dim(flat_vector, offset, offset + amount).reshape(dims_entry))
        offset += amount
    return result


def layer_norm(values, gain, shift):
    average = jnp.mean(values, axis=-1, keepdims=True)
    centred = values - average
    spread = jnp.mean(centred * centred, axis=-1, keepdims=True)
    return centred * lax.rsqrt(spread + norm_eps) * gain + shift


def gelu_tanh(values):
    return jax.nn.gelu(values, approximate=True)


def pack_grads(grad_list, total_size):
    flat_parts = [part_grad.reshape(-1) for part_grad in grad_list]
    used_total = sum((part_grad.size for part_grad in grad_list))
    flat_parts.append(jnp.zeros((total_size - used_total,), jnp.float32))
    return jnp.concatenate(flat_parts)


def fetch_params(attn_params, mlp_params):
    gathered = (
        lax.all_gather(attn_params, ("dp", "seq"), axis=0, tiled=True),
        lax.all_gather(mlp_params, ("dp", "seq"), axis=0, tiled=True),
    )
    return (
        unpack_params(gathered[0], attention_layout()),
        unpack_params(gathered[1], mlp_layout()),
    )


def send_grads(attn_list, mlp_list, attn_total, mlp_total):
    return (
        lax.psum_scatter(
            pack_grads(attn_list, attn_total), ("dp", "seq"), scatter_dimension=0, tiled=True
        ),
        lax.psum_scatter(
            pack_grads(mlp_list, mlp_total), ("dp", "seq"), scatter_dimension=0, tiled=True
        ),
    )


def fold_keys(key_rows, key_segs, fold_step, start_carry):
    return fold_step(
        start_carry,
        (
            lax.all_gather(key_rows, "seq", axis=0, tiled=True),
            lax.all_gather(key_segs, "seq", axis=0, tiled=True),
        ),
        jnp.int32(0),
    )


def over_blocks(block_step, carry_now, key_piece, key_start):
    piece_rows = key_piece[0].shape[0]
    step_rows = math.gcd(piece_rows, key_block)

    def loop_step(index_block, carry_in):
        offset = index_block * step_rows
        sub_piece = tuple(
            (lax.dynamic_slice_in_dim(member, offset, step_rows, 0) for member in key_piece)
        )
        return block_step(carry_in, sub_piece, offset)

    return lax.fori_loop(0, piece_rows // step_rows, loop_step, carry_now)


def block_scores(query_heads, query_segs, query_pos, kv_rows, key_segs, key_start):
    key_heads = kv_rows[:, :D].reshape(-1, H, HD)
    scores = jnp.einsum(
        "qhd,khd->hqk", query_heads, key_heads, preferred_element_type=jnp.float32
    ) * (1.0 / math.sqrt(HD))
    key_pos = key_start + jnp.arange(kv_rows.shape[0], dtype=jnp.int32)
    allowed = (query_segs[:, None] == key_segs[None, :]) & (key_pos[None, :] <= query_pos[:, None])
    return (jnp.where(allowed[None], scores, score_floor), key_heads)


MESH = pl.DeviceIdType.MESH
LANES = 128

def pad_rows(rows):
    return -(-rows // 16) * 16


class Gather:
    def __init__(self, dp_size, seq_size, own, slots, send_sems, recv_sems):
        self.n = seq_size
        self.bits = [b for b in range(1, dp_size.bit_length() - 1)]
        self.dp = lax.axis_index("dp")
        self.z = lax.axis_index("seq")
        self.own, self.slots = own, slots
        self.rows = own.shape[0]
        half = self.rows // 32 * 16
        self.parts = [(0, half), (half, self.rows - half)]
        self.orders = [self.bits, self.bits[::-1]]
        self.send_sems, self.recv_sems = send_sems, recv_sems
        self.started = []

    def peers(self):
        out = [(self.dp, lax.rem(self.z + k, self.n)) for k in range(1, self.n)]
        out += [(self.dp ^ (1 << b), self.z) for b in [0] + self.bits]
        return out

    def slot(self, mask, k):
        return (self.dp ^ mask) * self.n + lax.rem(self.z + self.n - k, self.n)

    def view(self, mask, k, part):
        index = self.slot(mask, k)
        if part is None:
            return self.slots.at[index]
        start, size = self.parts[part]
        return self.slots.at[index, pl.ds(start, size)]

    def source(self, mask, k, part):
        if mask == 0 and k == 0:
            if part is None:
                return self.own
            start, size = self.parts[part]
            return self.own.at[pl.ds(start, size)]
        return self.view(mask, k, part)

    def send(self, mask, k, part, to, kind, recv_index):
        copy = pltpu.make_async_remote_copy(
            src_ref=self.source(mask, k, part),
            dst_ref=self.view(mask, k, part),
            send_sem=self.send_sems.at[len(self.started)],
            recv_sem=self.recv_sems.at[recv_index],
            device_id=to,
            device_id_type=MESH,
        )
        copy.start()
        self.started.append(part)

    def recv_index(self, sibling, part, mask, k):
        part = 0 if part is None else part
        return ((sibling * 2 + part) * (2 << len(self.bits)) // 2 + (mask >> 1)) * self.n + k

    def wait(self, sibling, part, mask, k):
        view = self.view(mask ^ sibling, k, part)
        pltpu.make_async_remote_copy(
            src_ref=view, dst_ref=view, send_sem=self.send_sems.at[0],
            recv_sem=self.recv_sems.at[self.recv_index(sibling, part, mask, k)],
            device_id=(self.dp, self.z), device_id_type=MESH,
        ).wait_recv()

    def forward(self, part, mask, k):
        for p in ((0, 1) if part is None else (part,)):
            order = self.orders[p]
            last = max([order.index(b) for b in self.bits if mask >> b & 1], default=-1)
            for b in order[last + 1 :]:
                self.send(mask, k, p, (self.dp ^ (1 << b), self.z), 0, self.recv_index(0, p, mask | 1 << b, k))
        self.send(mask, k, part, (self.dp ^ 1, self.z), 1, self.recv_index(1, part, mask, k))

    def begin(self):
        for k in range(1, self.n):
            self.send(0, 0, None, (self.dp, lax.rem(self.z + k, self.n)), 0, self.recv_index(0, None, 0, k))
        self.forward(None, 0, 0)

    def events(self):
        out = []
        for k in range(1, self.n):
            out.append((k, None, 0, k))
        for k in range(self.n):
            for p in (0, 1):
                for level in range(len(self.bits)):
                    order = self.orders[p]
                    for low in range(1 << level):
                        mask = 1 << order[level]
                        for i in range(level):
                            if low >> i & 1:
                                mask |= 1 << order[i]
                        out.append(((level + 1) * 4 + k, p, mask, k))
        out.sort(key=lambda e: e[0])
        return [e[1:] for e in out]

    def step(self, event):
        part, mask, k = event
        self.wait(0, part, mask, k)
        self.forward(part, mask, k)

    def sibling_events(self):
        return [(None, 0, 0)] + self.events()

    def finish_sibling(self):
        for part, mask, k in self.sibling_events():
            self.wait(1, part, mask, k)

    def finish_sends(self):
        for index, part in enumerate(self.started):
            start, size = (0, self.rows) if part is None else self.parts[part]
            view = self.slots.at[0, pl.ds(start, size)]
            pltpu.make_async_remote_copy(
                src_ref=view, dst_ref=view, send_sem=self.send_sems.at[index], recv_sem=self.recv_sems.at[0],
                device_id=(self.dp, self.z), device_id_type=MESH,
            ).wait_send()


def gather_counts(dp_size, seq_size):
    bits = dp_size.bit_length() - 2
    recv = 4 * (1 << bits) * seq_size
    send = 0
    send += seq_size - 1
    for p in range(2):
        for mask in range(1 << bits):
            top = mask.bit_length()
            send += (bits - top) * seq_size
    send += seq_size + 2 * ((1 << bits) - 1) * seq_size
    return send, recv


def gather_kernel(dp_size, seq_size, a_own, m_own, a_slots, m_slots, a_send, a_recv, m_send, m_recv, own_sems):
    ga = Gather(dp_size, seq_size, a_own, a_slots, a_send, a_recv)
    gm = Gather(dp_size, seq_size, m_own, m_slots, m_send, m_recv)
    barrier = pltpu.get_barrier_semaphore()
    peers = ga.peers()
    for peer in peers:
        pl.semaphore_signal(barrier, inc=1, device_id=peer, device_id_type=MESH)
    pl.semaphore_wait(barrier, len(peers))
    ca = pltpu.make_async_copy(a_own, a_slots.at[ga.slot(0, 0)], own_sems.at[0])
    cm = pltpu.make_async_copy(m_own, m_slots.at[gm.slot(0, 0)], own_sems.at[1])
    ca.start()
    cm.start()
    ga.begin()
    gm.begin()
    for e in ga.events():
        ga.step(e)
    for e in gm.events():
        gm.step(e)
    ca.wait()
    cm.wait()
    ga.finish_sibling()
    gm.finish_sibling()
    ga.finish_sends()
    gm.finish_sends()


def to_rows(flat):
    rows = flat.shape[0] // LANES
    return jnp.pad(flat.reshape(rows, LANES), ((0, pad_rows(rows) - rows), (0, 0)))


def gather_params(attn, mlp, dp_size, seq_size):
    a, m = to_rows(attn), to_rows(mlp)
    devices = dp_size * seq_size
    send, recv = gather_counts(dp_size, seq_size)
    return pl.pallas_call(
        functools.partial(gather_kernel, dp_size, seq_size),
        out_shape=[jax.ShapeDtypeStruct((devices,) + a.shape, jnp.bfloat16), jax.ShapeDtypeStruct((devices,) + m.shape, jnp.bfloat16)],
        in_specs=[pl.BlockSpec(memory_space=pl.ANY)] * 2,
        out_specs=[pl.BlockSpec(memory_space=pl.ANY)] * 2,
        scratch_shapes=[pltpu.SemaphoreType.DMA((send,)), pltpu.SemaphoreType.DMA((recv,)),
                        pltpu.SemaphoreType.DMA((send,)), pltpu.SemaphoreType.DMA((recv,)), pltpu.SemaphoreType.DMA((2,))],
        compiler_params=pltpu.CompilerParams(collective_id=0, has_side_effects=True),
    )(a, m)


def per_device(inputs, segments, attn_params, mlp_params, cotangent):
    micro_count = inputs.shape[0]
    local_rows = inputs.shape[2]
    seq_length = local_rows * lax.axis_size("seq")
    attn_total = attn_params.shape[0] * lax.axis_size(("dp", "seq"))
    mlp_total = mlp_params.shape[0] * lax.axis_size(("dp", "seq"))
    query_pos = lax.axis_index("seq") * local_rows + jnp.arange(local_rows, dtype=jnp.int32)
    score_scale = 1.0 / math.sqrt(HD)
    out_rows = []
    grad_rows = []
    attn_sums = None
    mlp_sums = None
    shard_sums = None
    attn_slots, mlp_slots = gather_params(attn_params, mlp_params, lax.axis_size("dp"), lax.axis_size("seq"))
    attn_set = unpack_params(
        attn_slots[:, : attn_params.shape[0] // LANES].reshape(-1), attention_layout()
    )
    mlp_set = unpack_params(
        mlp_slots[:, : mlp_params.shape[0] // LANES].reshape(-1), mlp_layout()
    )
    for micro_index in range(micro_count):
        gain_one, shift_one, w_qkv, bias_query, bias_value, w_proj, bias_proj = attn_set
        gain_two, shift_two, w_up, bias_up, w_down, bias_down = mlp_set
        input_rows = inputs[micro_index, 0].astype(jnp.float32)
        query_segs = segments[micro_index, 0]
        normed_one, norm_one_back = jax.vjp(
            layer_norm, input_rows, gain_one.astype(jnp.float32), shift_one.astype(jnp.float32)
        )
        normed_one_low = normed_one.astype(jnp.bfloat16)
        merged_rows = jnp.dot(normed_one_low, w_qkv, preferred_element_type=jnp.float32)
        query_low = (merged_rows[:, :D] + bias_query.astype(jnp.float32)).astype(jnp.bfloat16)
        kv_local = jnp.concatenate(
            [merged_rows[:, D : 2 * D], merged_rows[:, 2 * D :] + bias_value.astype(jnp.float32)],
            axis=1,
        ).astype(jnp.bfloat16)
        query_heads = query_low.reshape(local_rows, H, HD)

        def max_step(carry_in, sub_piece, key_start):
            scores, key_heads = block_scores(
                query_heads, query_segs, query_pos, sub_piece[0], sub_piece[1], key_start
            )
            running_top, running_total = carry_in
            new_top = jnp.maximum(running_top, jnp.max(scores, axis=-1))
            new_total = running_total * jnp.exp(running_top - new_top) + jnp.sum(
                jnp.exp(scores - new_top[..., None]), axis=-1
            )
            return (new_top, new_total)

        top_start = jnp.full((H, local_rows), score_floor, jnp.float32)
        row_top, row_total = fold_keys(
            kv_local,
            query_segs,
            partial(over_blocks, max_step),
            (top_start, jnp.zeros((H, local_rows), jnp.float32)),
        )
        log_total = row_top + jnp.log(row_total)

        def value_step(carry_in, sub_piece, key_start):
            scores, key_heads = block_scores(
                query_heads, query_segs, query_pos, sub_piece[0], sub_piece[1], key_start
            )
            probs = jnp.exp(scores - log_total[..., None])
            probs_low = probs.astype(jnp.bfloat16)
            probs_rest = (probs - probs_low.astype(jnp.float32)).astype(jnp.bfloat16)
            value_heads = sub_piece[0][:, D:].reshape(-1, H, HD)
            main_part, rest_part = carry_in
            main_part = main_part + jnp.einsum(
                "hqk,khd->qhd", probs_low, value_heads, preferred_element_type=jnp.float32
            )
            rest_part = rest_part + jnp.einsum(
                "hqk,khd->qhd", probs_rest, value_heads, preferred_element_type=jnp.float32
            )
            return (main_part, rest_part)

        zero_heads = jnp.zeros((local_rows, H, HD), jnp.float32)
        main_sum, rest_sum = fold_keys(
            kv_local, query_segs, partial(over_blocks, value_step), (zero_heads, zero_heads)
        )
        attended_low = main_sum.reshape(local_rows, D).astype(jnp.bfloat16)
        attended_full = main_sum + rest_sum
        middle = (
            input_rows
            + jnp.dot(attended_low, w_proj, preferred_element_type=jnp.float32)
            + bias_proj.astype(jnp.float32)
        )
        normed_two, norm_two_back = jax.vjp(
            layer_norm, middle, gain_two.astype(jnp.float32), shift_two.astype(jnp.float32)
        )
        normed_two_low = normed_two.astype(jnp.bfloat16)
        hidden = jnp.dot(normed_two_low, w_up, preferred_element_type=jnp.float32) + bias_up.astype(
            jnp.float32
        )
        active, gelu_back = jax.vjp(gelu_tanh, hidden)
        active_low = active.astype(jnp.bfloat16)
        result = (
            middle
            + jnp.dot(active_low, w_down, preferred_element_type=jnp.float32)
            + bias_down.astype(jnp.float32)
        )
        out_rows.append(result.astype(jnp.bfloat16))
        w_qkv, w_proj = (attn_set[2], attn_set[5])
        w_up, w_down = (mlp_set[2], mlp_set[4])
        cot_low = cotangent[micro_index, 0]
        cot_rows = cot_low.astype(jnp.float32)
        grad_w_down = jnp.einsum(
            "rf,rd->fd", active_low, cot_low, preferred_element_type=jnp.float32
        )
        grad_b_down = jnp.sum(cot_rows, axis=0)
        grad_active = jnp.einsum("rd,fd->rf", cot_low, w_down, preferred_element_type=jnp.float32)
        grad_hidden = gelu_back(grad_active)[0].astype(jnp.bfloat16)
        grad_w_up = jnp.einsum(
            "rd,rf->df", normed_two_low, grad_hidden, preferred_element_type=jnp.float32
        )
        grad_b_up = jnp.sum(grad_hidden.astype(jnp.float32), axis=0)
        grad_normed_two = jnp.einsum(
            "rf,df->rd", grad_hidden, w_up, preferred_element_type=jnp.float32
        )
        grad_middle_norm, grad_gain_two, grad_shift_two = norm_two_back(grad_normed_two)
        grad_middle = cot_rows + grad_middle_norm
        grad_branch = grad_middle.astype(jnp.bfloat16)
        grad_w_proj = jnp.einsum(
            "rd,re->de", attended_low, grad_branch, preferred_element_type=jnp.float32
        )
        grad_b_proj = jnp.sum(grad_branch.astype(jnp.float32), axis=0)
        grad_attended = jnp.einsum(
            "re,de->rd", grad_branch, w_proj, preferred_element_type=jnp.float32
        ).astype(jnp.bfloat16)
        grad_heads = grad_attended.reshape(local_rows, H, HD)
        row_delta = jnp.einsum("qhd,qhd->hq", grad_heads.astype(jnp.float32), attended_full)

        def grad_step(carry_in, sub_piece, key_start):
            scores, key_heads = block_scores(
                query_heads, query_segs, query_pos, sub_piece[0], sub_piece[1], key_start
            )
            value_heads = sub_piece[0][:, D:].reshape(-1, H, HD)
            probs = jnp.exp(scores - log_total[..., None])
            grad_probs = jnp.einsum(
                "qhd,khd->hqk", grad_heads, value_heads, preferred_element_type=jnp.float32
            )
            grad_scores = (probs * (grad_probs - row_delta[..., None])).astype(jnp.bfloat16)
            query_part, kv_part = carry_in
            query_part = (
                query_part
                + jnp.einsum(
                    "hqk,khd->qhd", grad_scores, key_heads, preferred_element_type=jnp.float32
                )
                * score_scale
            )
            key_grad = (
                jnp.einsum(
                    "hqk,qhd->khd", grad_scores, query_heads, preferred_element_type=jnp.float32
                )
                * score_scale
            )
            value_grad = jnp.einsum(
                "hqk,qhd->khd",
                probs.astype(jnp.bfloat16),
                grad_heads,
                preferred_element_type=jnp.float32,
            )
            block_grads = jnp.concatenate(
                [key_grad.reshape(-1, D), value_grad.reshape(-1, D)], axis=1
            )
            kv_part = lax.dynamic_update_slice_in_dim(kv_part, block_grads, key_start, 0)
            return (query_part, kv_part)

        query_sum, kv_sums = fold_keys(
            kv_local,
            query_segs,
            partial(over_blocks, grad_step),
            (zero_heads, jnp.zeros((seq_length, 2 * D), jnp.float32)),
        )
        kv_grads = lax.psum_scatter(
            kv_sums.astype(jnp.bfloat16), "seq", scatter_dimension=0, tiled=True
        ).astype(jnp.float32)
        grad_merged = jnp.concatenate([query_sum.reshape(local_rows, D), kv_grads], axis=1).astype(
            jnp.bfloat16
        )
        grad_merged_wide = grad_merged.astype(jnp.float32)
        grad_w_qkv = jnp.einsum(
            "rd,re->de", normed_one_low, grad_merged, preferred_element_type=jnp.float32
        )
        grad_b_query = jnp.sum(grad_merged_wide[:, :D], axis=0)
        grad_b_value = jnp.sum(grad_merged_wide[:, 2 * D :], axis=0)
        grad_normed_one = jnp.einsum(
            "re,de->rd", grad_merged, w_qkv, preferred_element_type=jnp.float32
        )
        grad_input_norm, grad_gain_one, grad_shift_one = norm_one_back(grad_normed_one)
        grad_rows.append(grad_middle + grad_input_norm)
        attn_list = [
            grad_gain_one,
            grad_shift_one,
            grad_w_qkv,
            grad_b_query,
            grad_b_value,
            grad_w_proj,
            grad_b_proj,
        ]
        mlp_list = [grad_gain_two, grad_shift_two, grad_w_up, grad_b_up, grad_w_down, grad_b_down]
        attn_sums = (
            attn_list
            if attn_sums is None
            else [left_sum + right_sum for left_sum, right_sum in zip(attn_sums, attn_list)]
        )
        mlp_sums = (
            mlp_list
            if mlp_sums is None
            else [left_sum + right_sum for left_sum, right_sum in zip(mlp_sums, mlp_list)]
        )
    shard_sums = send_grads(attn_sums, mlp_sums, attn_total, mlp_total)
    outputs = jnp.stack(out_rows)[:, None]
    input_grad = jnp.stack(grad_rows)[:, None]
    return (outputs, input_grad, shard_sums[0], shard_sums[1])


HALF_HEADS = H // 2
HALF_COLS = D // 2
ROW_D = D // LANES
ROW_FF = FF // LANES
ROW_QKV = 3 * ROW_D
ROW_HALF = HALF_COLS // LANES
FF_STEP = 512
VMEM_LIMIT = 62 * 2**20

ATTN_QKV = 2 * ROW_D
ATTN_BQ = ATTN_QKV + D * ROW_QKV
ATTN_BV = ATTN_BQ + ROW_D
ATTN_PROJ = ATTN_BV + ROW_D
ATTN_BPROJ = ATTN_PROJ + D * ROW_D
MLP_UP = 2 * ROW_D
MLP_BUP = MLP_UP + D * ROW_FF
MLP_DOWN = MLP_BUP + ROW_FF
MLP_BDOWN = MLP_DOWN + FF * ROW_D

f32 = jnp.float32
bf16 = jnp.bfloat16


def dot_nn(left, right):
    return jnp.dot(left, right, preferred_element_type=f32)


def dot_nt(left, right):
    return lax.dot_general(left, right, (((1,), (1,)), ((), ())), preferred_element_type=f32)


def dot_tn(left, right):
    return lax.dot_general(left, right, (((0,), (0,)), ((), ())), preferred_element_type=f32)


def remote(src, dst, send_sem, recv_sem, to):
    return pltpu.make_async_remote_copy(
        src_ref=src, dst_ref=dst, send_sem=send_sem, recv_sem=recv_sem, device_id=to, device_id_type=MESH
    )


class Place:
    def __init__(self, seq_size):
        self.n = seq_size
        self.dp = lax.axis_index("dp")
        self.z = lax.axis_index("seq")
        self.core = lax.rem(self.dp, 2)
        self.base = self.dp - self.core
        self.sibling = (self.base + 1 - self.core, self.z)

    def line_peers(self):
        out = [self.sibling]
        for k in range(1, self.n):
            other = lax.rem(self.z + k, self.n)
            out += [(self.base, other), (self.base + 1, other)]
        return out

    def own_block(self, j):
        return 1 - self.core + 2 * j

    def other_block(self, j):
        return self.core + 2 * j

    def worker(self, micro):
        return (self.base + 1 - lax.rem(self.z, 2), 2 * micro + self.core)

    def home(self, j):
        return (self.base + lax.rem(self.z, 2), self.own_block(j)), self.z // 2


def greet(peers):
    barrier = pltpu.get_barrier_semaphore()
    for peer in peers:
        pl.semaphore_signal(barrier, inc=1, device_id=peer, device_id_type=MESH)
    pl.semaphore_wait(barrier, len(peers))


def unflatten(slots, flat, rows):
    def body(s, carry):
        flat[pl.ds(s * rows, rows), :] = slots[s, :rows, :].astype(f32)
        return carry

    lax.fori_loop(0, slots.shape[0], body, 0)


def flatten(flat, slots, rows):
    def body(s, carry):
        slots[s, :rows, :] = flat[pl.ds(s * rows, rows), :].astype(bf16)
        return carry

    lax.fori_loop(0, slots.shape[0], body, 0)


def load_matrix(flat, start, stride, columns, out, step):
    def body(i, carry):
        rows = pl.ds(pl.multiple_of(i * step, step), step)
        for j in range(columns):
            piece = flat[pl.ds(start + j + i * (step * stride), step, stride=stride), :]
            out[rows, j * LANES : (j + 1) * LANES] = piece.astype(bf16)
        return carry

    lax.fori_loop(0, out.shape[0] // step, body, 0)


def load_vector(flat, start, blocks):
    return jnp.concatenate([flat[pl.ds(start + j, 1), :] for j in range(blocks)], axis=1)


def store_vector(flat, start, value):
    for j in range(value.shape[1] // LANES):
        flat[pl.ds(start + j, 1), :] = value[:, j * LANES : (j + 1) * LANES]


def norm_parts(values):
    average = jnp.mean(values, axis=-1, keepdims=True)
    centred = values - average
    spread = jnp.mean(centred * centred, axis=-1, keepdims=True)
    scale = lax.rsqrt(spread + norm_eps)
    return centred * scale, scale


def norm_back(normal, scale, grad, gain):
    scaled = grad * gain
    return scale * (
        scaled
        - jnp.mean(scaled, axis=-1, keepdims=True)
        - normal * jnp.mean(scaled * normal, axis=-1, keepdims=True)
    )


def forward_kernel(
    dp_size, seq_size, a_rows,
    x_in, seg_in, cot_in, a_own, m_own,
    m_slots, cot_own, x_own, n1, wqkv, w_proj, vec, qt, kt, vt, qh, kh, vh, bias, lse, att,
    a_slots, flat, x_all, seg_all, seg_col, scores, ot, att_out,
    a_send, a_recv, m_send, m_recv, own_sems, move_send, move_recv, cot_sems, swap_sems,
):
    place = Place(seq_size)
    block = x_in.shape[1]
    ga = Gather(dp_size, seq_size, a_own, a_slots, a_send, a_recv)
    gm = Gather(dp_size, seq_size, m_own, m_slots, m_send, m_recv)
    greet(place.line_peers() + [(place.dp ^ (1 << b), place.z) for b in ga.bits])

    own_copies = [
        pltpu.make_async_copy(a_own, a_slots.at[ga.slot(0, 0)], own_sems.at[0]),
        pltpu.make_async_copy(m_own, m_slots.at[gm.slot(0, 0)], own_sems.at[1]),
    ]
    for copy in own_copies:
        copy.start()
    sent = []
    for micro in range(2):
        to = place.worker(micro)
        sent.append(
            remote(x_in.at[micro], x_all.at[place.z], move_send.at[0, micro], move_recv.at[0, place.z], to)
        )
        sent.append(
            remote(seg_in.at[micro], seg_all.at[place.z], move_send.at[1, micro], move_recv.at[1, place.z], to)
        )
    for copy in sent:
        copy.start()
    ga.begin()
    for micro in range(2):
        copy = remote(
            cot_in.at[micro], cot_own.at[place.z // 2], cot_sems.at[0, micro], cot_sems.at[1, place.z // 2],
            place.worker(micro),
        )
        copy.start()
        sent.append(copy)
    gm.begin()

    def arrival(t, kind):
        ref = (x_all, seg_all)[kind].at[t]
        return remote(ref, ref, move_send.at[kind, 0], move_recv.at[kind, t], place.sibling)

    for j in range(2):
        t = place.own_block(j)
        for kind in range(2):
            ref = (x_all, seg_all)[kind].at[t]
            arrival(t, kind).wait_recv()
            copy = remote(ref, ref, move_send.at[kind, 2 + j], move_recv.at[kind, t], place.sibling)
            copy.start()
            sent.append(copy)
    for event in ga.events():
        ga.step(event)
    for j in range(2):
        for kind in range(2):
            arrival(place.other_block(j), kind).wait_recv()
        x_own[j] = x_all[place.own_block(j)]

    for t in range(seq_size):
        for r in range(block // LANES):
            row = jnp.broadcast_to(seg_all[t, r : r + 1, :], (LANES, LANES))
            seg_col[pl.ds(t * block + r * LANES, LANES), :] = row.T
    chunks = seq_size * block // LANES
    key_pos = lax.broadcasted_iota(jnp.int32, (LANES, LANES), 0)
    query_pos = lax.broadcasted_iota(jnp.int32, (LANES, LANES), 1)
    for q in range(chunks):
        row = seg_all[q * LANES // block, q % (block // LANES) : q % (block // LANES) + 1, :]
        top = (q * LANES // block + 1) * block // LANES
        for k in range(top):
            rows = slice(k * LANES, (k + 1) * LANES)
            if k > q:
                value = jnp.full((LANES, LANES), score_floor, f32)
            else:
                allowed = seg_col[rows, :] == row
                if k == q:
                    allowed = allowed & (key_pos <= query_pos)
                value = jnp.where(allowed, 0.0, score_floor)
            bias[rows, q * LANES : (q + 1) * LANES] = value

    own_copies[0].wait()
    ga.finish_sibling()
    unflatten(a_slots, flat, a_rows)
    for section in range(3):
        load_matrix(
            flat, ATTN_QKV + section * ROW_D + place.core * ROW_HALF, ROW_QKV, ROW_HALF, wqkv.at[section], LANES
        )
    load_matrix(flat, ATTN_PROJ, ROW_D, ROW_D, w_proj, LANES)
    gain = load_vector(flat, 0, ROW_D)
    shift = load_vector(flat, ROW_D, ROW_D)
    vec[...] = jnp.zeros_like(vec)
    vec[0:1, :] = gain
    vec[1:2, :] = load_vector(flat, ATTN_BPROJ, ROW_D)
    bias_query = load_vector(flat, ATTN_BQ + place.core * ROW_HALF, ROW_HALF)
    bias_value = load_vector(flat, ATTN_BV + place.core * ROW_HALF, ROW_HALF)

    def project(t, carry):
        rows = pl.ds(pl.multiple_of(t * block, block), block)
        normal, _ = norm_parts(x_all[t].astype(f32))
        low = (normal * gain + shift).astype(bf16)
        n1[rows, :] = low
        query = (dot_nn(low, wqkv[0]) + bias_query).astype(bf16).astype(f32) * (1.0 / math.sqrt(HD))
        key = dot_nn(low, wqkv[1])
        value = dot_nn(low, wqkv[2]) + bias_value
        for result, across, heads in ((query, qt, qh), (key, kt, kh), (value, vt, vh)):
            across[:, rows] = result.T.astype(bf16)
            rounded = result.astype(bf16)
            for h in range(HALF_HEADS):
                heads[h, rows, :] = rounded[:, h * HD : (h + 1) * HD]
        return carry

    lax.fori_loop(0, seq_size, project, 0)
    lse[...] = jnp.zeros_like(lse)

    m_events = gm.events()
    per_head = -(-len(m_events) // HALF_HEADS)

    def one_head(h, carry):
        for c in range(HALF_HEADS):

            @pl.when(h == c)
            def _():
                for event in m_events[c * per_head : (c + 1) * per_head]:
                    gm.step(event)

        head_rows = pl.ds(pl.multiple_of(h * HD, HD), HD)
        for i in range(seq_size):
            columns = slice(i * block, (i + 1) * block)
            query = qt[head_rows, columns]
            top = jnp.full((1, block), -jnp.inf, f32)
            for b in range(i + 1):
                rows = slice(b * block, (b + 1) * block)
                piece = dot_nn(kh[h, rows, :], query) + bias[rows, columns]
                scores[rows, :] = piece
                top = jnp.maximum(top, jnp.max(piece, axis=0, keepdims=True))
            total = jnp.zeros((1, block), f32)
            for b in range(i + 1):
                rows = slice(b * block, (b + 1) * block)
                piece = jnp.exp(scores[rows, :] - top)
                scores[rows, :] = piece
                total = total + jnp.sum(piece, axis=0, keepdims=True)
            inverse = 1.0 / total
            result = jnp.zeros((HD, block), f32)
            for b in range(i + 1):
                rows = slice(b * block, (b + 1) * block)
                result = result + dot_nn(vt[head_rows, rows], (scores[rows, :] * inverse).astype(bf16))
            ot[head_rows, columns] = result
            lse[pl.ds(h, 1), columns] = top + jnp.log(total)
        return carry

    lax.fori_loop(0, HALF_HEADS, one_head, 0)

    for j in range(2):
        columns = pl.ds(pl.multiple_of(place.other_block(j) * block, block), block)
        att_out[j] = ot[:, columns].T.astype(bf16)
        copy = remote(
            att_out.at[j], att.at[place.core, j], swap_sems.at[0, j], swap_sems.at[1, j], place.sibling
        )
        copy.start()
        sent.append(copy)
    for j in range(2):
        columns = pl.ds(pl.multiple_of(place.own_block(j) * block, block), block)
        att[place.core, j] = ot[:, columns].T.astype(bf16)
    for j in range(2):
        ref = att.at[1 - place.core, j]
        remote(ref, ref, swap_sems.at[0, j], swap_sems.at[1, j], place.sibling).wait_recv()
        ref = cot_own.at[j]
        remote(ref, ref, cot_sems.at[0, j], cot_sems.at[1, j], place.sibling).wait_recv()
    own_copies[1].wait()
    gm.finish_sibling()
    for copy in sent:
        copy.wait_send()
    ga.finish_sends()
    gm.finish_sends()


def mlp_kernel(
    m_rows,
    m_slots, x_own, cot, att, w_proj, vec,
    out, d_mid, d_att, g_slots, g_proj, g_bias,
    flat, w_up, w_down, mid, n2, d_n2, total, b_up, gb_up, sem,
):
    rows_all = x_own.shape[0]
    half = rows_all // 2
    copy = pltpu.make_async_copy(m_slots, g_slots, sem)
    copy.start()
    blocks = [slice(0, half), slice(half, rows_all)]
    for rows in blocks:
        mid[rows, :] = (
            x_own[rows, :].astype(f32)
            + dot_nn(att[0, rows, :], w_proj[:HALF_COLS, :])
            + dot_nn(att[1, rows, :], w_proj[HALF_COLS:, :])
            + vec[1:2, :]
        )
    copy.wait()
    unflatten(g_slots, flat, m_rows)
    load_matrix(flat, MLP_UP, ROW_FF, ROW_FF, w_up, 64)
    load_matrix(flat, MLP_DOWN, ROW_D, ROW_D, w_down, LANES)
    gain = load_vector(flat, 0, ROW_D)
    shift = load_vector(flat, ROW_D, ROW_D)
    b_down = load_vector(flat, MLP_BDOWN, ROW_D)
    b_up[...] = load_vector(flat, MLP_BUP, ROW_FF)
    for rows in blocks:
        normal, _ = norm_parts(mid[rows, :])
        n2[rows, :] = (normal * gain + shift).astype(bf16)
    total[...] = jnp.zeros_like(total)
    d_n2[...] = jnp.zeros_like(d_n2)
    inner = math.sqrt(2.0 / math.pi)

    def step(f, carry):
        start = pl.multiple_of(f * FF_STEP, FF_STEP)
        columns = pl.ds(start, FF_STEP)
        hidden = dot_nn(n2[...], w_up[:, columns]) + b_up[:, columns]
        square = hidden * hidden
        tanh = jnp.tanh(inner * (hidden + 0.044715 * (square * hidden)))
        cdf = 0.5 * (1.0 + tanh)
        active = (hidden * cdf).astype(bf16)
        slope = cdf + (0.5 * inner) * hidden * (1.0 - tanh * tanh) * (1.0 + (3 * 0.044715) * square)
        d_hidden = dot_nt(cot[...], w_down[columns, :]) * slope
        low = d_hidden.astype(bf16)
        gb_up[:, columns] = jnp.sum(low.astype(f32), axis=0, keepdims=True)
        total[...] += dot_nn(active, w_down[columns, :])
        d_n2[...] += dot_nt(low, w_up[:, columns])
        g_down = dot_tn(active, cot[...])
        for j in range(ROW_D):
            flat[pl.ds(MLP_DOWN + j + f * (FF_STEP * ROW_D), FF_STEP, stride=ROW_D), :] = g_down[
                :, j * LANES : (j + 1) * LANES
            ]
        g_up = dot_tn(n2[...], low)
        for j in range(FF_STEP // LANES):
            flat[pl.ds(MLP_UP + j + f * (FF_STEP // LANES), D, stride=ROW_FF), :] = g_up[
                :, j * LANES : (j + 1) * LANES
            ]
        return carry

    lax.fori_loop(0, FF // FF_STEP, step, 0)

    gain_sum = jnp.zeros((1, D), f32)
    shift_sum = jnp.zeros((1, D), f32)
    down_sum = jnp.zeros((1, D), f32)
    proj_sum = jnp.zeros((1, D), f32)
    for rows in blocks:
        out[rows, :] = (mid[rows, :] + total[rows, :] + b_down).astype(bf16)
        normal, scale = norm_parts(mid[rows, :])
        grad = d_n2[rows, :]
        cot_rows = cot[rows, :].astype(f32)
        gain_sum += jnp.sum(grad * normal, axis=0, keepdims=True)
        shift_sum += jnp.sum(grad, axis=0, keepdims=True)
        down_sum += jnp.sum(cot_rows, axis=0, keepdims=True)
        d_rows = cot_rows + norm_back(normal, scale, grad, gain)
        d_mid[rows, :] = d_rows
        low = d_rows.astype(bf16)
        n2[rows, :] = low
        proj_sum += jnp.sum(low.astype(f32), axis=0, keepdims=True)
        for c in range(2):
            d_att[c, rows, :] = dot_nt(low, w_proj[c * HALF_COLS : (c + 1) * HALF_COLS, :]).astype(bf16)
    for c in range(2):
        g_part = dot_tn(att[c], n2[...])
        for j in range(ROW_D):
            g_proj[pl.ds(c * HALF_COLS * ROW_D + j, HALF_COLS, stride=ROW_D), :] = g_part[
                :, j * LANES : (j + 1) * LANES
            ]
    g_bias[...] = proj_sum
    store_vector(flat, 0, gain_sum)
    store_vector(flat, ROW_D, shift_sum)
    store_vector(flat, MLP_BUP, gb_up[...])
    store_vector(flat, MLP_BDOWN, down_sum)
    used = MLP_BDOWN + ROW_D
    flat[used:, :] = jnp.zeros((flat.shape[0] - used, LANES), f32)
    flatten(flat, g_slots, m_rows)


def backward_kernel(
    seq_size, a_rows,
    out_own, d_mid, d_att, g_proj, g_bias, x_own, n1, wqkv, vec, qt, kt, qh, kh, vh, bias, lse,
    out_back, grad_back, a_grads,
    flat, d_all, dt, dh, p_piece, d_piece, dk, dv, dqt, dm, d_n1, d_n1_in, g_out,
    move_sems, swap_sems, norm_sems, proj_sem,
):
    place = Place(seq_size)
    block = x_own.shape[1]
    length = seq_size * block
    greet(place.line_peers())
    sent = []
    for j in range(2):
        t = place.own_block(j)
        src = d_att.at[1 - place.core, pl.ds(j * block, block)]
        copy = remote(src, d_all.at[t], swap_sems.at[0, j], swap_sems.at[1, j], place.sibling)
        copy.start()
        sent.append(copy)
        to, micro = place.home(j)
        copy = remote(
            out_own.at[pl.ds(j * block, block)], out_back.at[micro], move_sems.at[0, j], move_sems.at[1, micro], to
        )
        copy.start()
        sent.append(copy)
    flat[...] = jnp.zeros_like(flat)
    proj_copy = pltpu.make_async_copy(g_proj, flat.at[pl.ds(ATTN_PROJ, D * ROW_D)], proj_sem)
    proj_copy.start()
    for j in range(2):
        d_all[place.own_block(j)] = d_att[place.core, j * block : (j + 1) * block, :]
    for j in range(2):
        ref = d_all.at[place.other_block(j)]
        remote(ref, ref, swap_sems.at[0, j], swap_sems.at[1, j], place.sibling).wait_recv()

    def spread(t, carry):
        rows = pl.ds(pl.multiple_of(t * block, block), block)
        piece = d_all[t]
        dt[:, rows] = piece.astype(f32).T.astype(bf16)
        for h in range(HALF_HEADS):
            dh[h, rows, :] = piece[:, h * HD : (h + 1) * HD]
        return carry

    lax.fori_loop(0, seq_size, spread, 0)

    def one_head(h, carry):
        head_rows = pl.ds(pl.multiple_of(h * HD, HD), HD)
        for i in range(seq_size):
            columns = slice(i * block, (i + 1) * block)
            query = qt[head_rows, columns]
            d_query = dt[head_rows, columns]
            level = lse[pl.ds(h, 1), columns]
            delta = jnp.zeros((1, block), f32)
            for b in range(i + 1):
                rows = slice(b * block, (b + 1) * block)
                probs = jnp.exp(dot_nn(kh[h, rows, :], query) + bias[rows, columns] - level)
                d_probs = dot_nn(vh[h, rows, :], d_query)
                delta = delta + jnp.sum(probs * d_probs, axis=0, keepdims=True)
                p_piece[rows, :] = probs
                d_piece[rows, :] = d_probs
            result = jnp.zeros((HD, block), f32)
            for b in range(i + 1):
                rows = slice(b * block, (b + 1) * block)
                probs = p_piece[rows, :]
                d_scores = (probs * (d_piece[rows, :] - delta)).astype(bf16)
                key_part = dot_nn(d_scores, qh[h, columns, :])
                value_part = dot_nn(probs.astype(bf16), dh[h, columns, :])
                if b == i:
                    dk[h, rows, :] = key_part
                    dv[h, rows, :] = value_part
                else:
                    dk[h, rows, :] += key_part
                    dv[h, rows, :] += value_part
                result = result + dot_nn(kt[head_rows, rows], d_scores)
            dqt[head_rows, columns] = result * (1.0 / math.sqrt(HD))
        return carry

    lax.fori_loop(0, HALF_HEADS, one_head, 0)

    query_sum = jnp.zeros((1, HALF_COLS), f32)
    value_sum = jnp.zeros((1, HALF_COLS), f32)
    for t in range(seq_size):
        rows = slice(t * block, (t + 1) * block)
        low = dqt[:, rows].T.astype(bf16)
        dm[0, rows, :] = low
        query_sum += jnp.sum(low.astype(f32), axis=0, keepdims=True)
        for section, part in ((1, dk), (2, dv)):
            low = jnp.concatenate([part[h, rows, :] for h in range(HALF_HEADS)], axis=1).astype(bf16)
            dm[section, rows, :] = low
        value_sum += jnp.sum(low.astype(f32), axis=0, keepdims=True)

    def to_norm(t):
        rows = pl.ds(pl.multiple_of(t * block, block), block)
        return dot_nt(dm[0, rows, :], wqkv[0]) + dot_nt(dm[1, rows, :], wqkv[1]) + dot_nt(dm[2, rows, :], wqkv[2])

    for j in range(2):
        d_n1[j] = to_norm(place.other_block(j))
        copy = remote(d_n1.at[j], d_n1_in.at[j], norm_sems.at[0, j], norm_sems.at[1, j], place.sibling)
        copy.start()
        sent.append(copy)
    proj_copy.wait()
    for section in range(3):
        part = dot_tn(n1[...], dm[section])
        for j in range(ROW_HALF):
            start = ATTN_QKV + section * ROW_D + place.core * ROW_HALF + j
            flat[pl.ds(start, D, stride=ROW_QKV), :] = part[:, j * LANES : (j + 1) * LANES]
    store_vector(flat, ATTN_BQ + place.core * ROW_HALF, query_sum)
    store_vector(flat, ATTN_BV + place.core * ROW_HALF, value_sum)
    store_vector(flat, ATTN_BPROJ, g_bias[...])
    gain = vec[0:1, :]
    gain_sum = jnp.zeros((1, D), f32)
    shift_sum = jnp.zeros((1, D), f32)
    for j in range(2):
        grad = to_norm(place.own_block(j))
        ref = d_n1_in.at[j]
        remote(ref, ref, norm_sems.at[0, j], norm_sems.at[1, j], place.sibling).wait_recv()
        grad = grad + d_n1_in[j]
        normal, scale = norm_parts(x_own[j].astype(f32))
        gain_sum += jnp.sum(grad * normal, axis=0, keepdims=True)
        shift_sum += jnp.sum(grad, axis=0, keepdims=True)
        g_out[j] = (d_mid[j * block : (j + 1) * block, :] + norm_back(normal, scale, grad, gain)).astype(bf16)
        to, micro = place.home(j)
        copy = remote(g_out.at[j], grad_back.at[micro], move_sems.at[2, j], move_sems.at[3, micro], to)
        copy.start()
        sent.append(copy)
    store_vector(flat, 0, gain_sum)
    store_vector(flat, ROW_D, shift_sum)
    flatten(flat, a_grads, a_rows)
    for micro in range(2):
        for kind, ref in ((1, out_back), (3, grad_back)):
            remote(
                ref.at[micro], ref.at[micro], move_sems.at[0, micro], move_sems.at[kind, micro], place.sibling
            ).wait_recv()
    for copy in sent:
        copy.wait_send()


class Scatter:
    def __init__(self, dp_size, seq_size, slots, out, acc, core_in, level_in, seq_in, load_sems, send_sems, recv_sems):
        self.n = seq_size
        self.bits = list(range(1, dp_size.bit_length() - 1))
        self.masks = [m << 1 for m in range(1 << len(self.bits))]
        self.dp = lax.axis_index("dp")
        self.z = lax.axis_index("seq")
        self.slots, self.out, self.acc = slots, out, acc
        self.core_in, self.level_in, self.seq_in = core_in, level_in, seq_in
        rows = slots.shape[1]
        half = rows // 32 * 16
        self.parts = [(0, half), (half, rows - half)]
        self.orders = [self.bits[::-1], self.bits]
        self.load_sems, self.send_sems, self.recv_sems = load_sems, send_sems, recv_sems
        self.started = []
        self.indices = {}

    def index(self, *key):
        return self.indices.setdefault(key, len(self.indices))

    def slot(self, mask, k):
        return (self.dp ^ mask) * self.n + lax.rem(self.z + k, self.n)

    def send(self, src, dst, to, key):
        copy = remote(src, dst, self.send_sems.at[len(self.started)], self.recv_sems.at[self.index(*key)], to)
        copy.start()
        self.started.append(copy)

    def wait(self, ref, key):
        remote(ref, ref, self.send_sems.at[0], self.recv_sems.at[self.index(*key)], (self.dp, self.z)).wait_recv()

    def turn(self):
        return list(range(1, self.n)) + [0]

    def begin(self):
        for k in self.turn():
            for mask in self.masks[::-1]:
                i = self.masks.index(mask)
                pltpu.make_async_copy(
                    self.slots.at[self.slot(mask, k)], self.acc.at[i, k], self.load_sems.at[i, k]
                ).start()
                self.send(
                    self.slots.at[self.slot(mask ^ 1, k)], self.core_in.at[i, k], (self.dp ^ 1, self.z), ("c", i, k)
                )

    def cell(self, part, level, mask):
        free = [b for b in self.bits if b not in self.orders[part][: level + 1]]
        return sum(1 << n for n, b in enumerate(free) if mask >> b & 1)

    def pass_on(self, part, level, mask, k):
        order = self.orders[part]
        i = self.masks.index(mask)
        start, size = self.parts[part]
        src = self.acc.at[i, k, pl.ds(start, size)]
        if level == len(order):
            if k:
                to = (self.dp, lax.rem(self.z + k, self.n))
                self.send(src, self.seq_in[part].at[k - 1], to, ("z", part, k))
            return
        bit = 1 << order[level]
        if mask & bit:
            rest = mask ^ bit
            dst = self.level_in[part][level].at[self.cell(part, level, rest), k]
            self.send(src, dst, (self.dp ^ bit, self.z), ("l", part, level, rest, k))

    def events(self):
        out = []
        for turn, k in enumerate(self.turn()):
            for mask in self.masks[::-1]:
                out.append((turn, ("c", mask, k)))
            for level in range(len(self.bits)):
                for part in (0, 1):
                    past = self.orders[part][: level + 1]
                    for mask in self.masks[::-1]:
                        if not any(mask >> b & 1 for b in past):
                            out.append((turn + (level + 1) * 1.0 + 0.5, ("l", part, level, mask, k)))
        out.sort(key=lambda e: e[0])
        return [e[1] for e in out]

    def step(self, event):
        if event[0] == "c":
            _, mask, k = event
            i = self.masks.index(mask)
            pltpu.make_async_copy(
                self.slots.at[self.slot(mask, k)], self.acc.at[i, k], self.load_sems.at[i, k]
            ).wait()
            self.wait(self.core_in.at[i, k], ("c", i, k))
            self.acc[i, k] = (self.acc[i, k].astype(f32) + self.core_in[i, k].astype(f32)).astype(bf16)
            for part in (0, 1):
                self.pass_on(part, 0, mask, k)
            return
        _, part, level, mask, k = event
        i = self.masks.index(mask)
        start, size = self.parts[part]
        cell = self.level_in[part][level].at[self.cell(part, level, mask), k]
        self.wait(cell, ("l", part, level, mask, k))
        rows = pl.ds(start, size)
        self.acc[i, k, rows] = (self.acc[i, k, rows].astype(f32) + cell[...].astype(f32)).astype(bf16)
        self.pass_on(part, level + 1, mask, k)

    def finish(self):
        used = self.out.shape[0]
        for part in (0, 1):
            start, size = self.parts[part]
            size = min(size, used - start)
            total = self.acc[0, 0, pl.ds(start, size)].astype(f32)
            for k in range(1, self.n):
                self.wait(self.seq_in[part].at[k - 1], ("z", part, k))
                total = total + self.seq_in[part][k - 1, :size].astype(f32)
            self.out[start : start + size, :] = total
        for copy in self.started:
            copy.wait_send()

    def peers(self):
        out = [(self.dp, lax.rem(self.z + k, self.n)) for k in range(1, self.n)]
        return out + [(self.dp ^ (1 << b), self.z) for b in [0] + self.bits]


def scatter_scratch(dp_size, seq_size, rows):
    bits = dp_size.bit_length() - 2
    masks = 1 << bits
    half = rows // 32 * 16
    sizes = [half, rows - half]
    shapes = [
        pltpu.VMEM((masks, seq_size, rows, LANES), bf16),
        pltpu.VMEM((masks, seq_size, rows, LANES), bf16),
    ]
    for size in sizes:
        for level in range(bits):
            shapes.append(pltpu.VMEM((masks >> (level + 1), seq_size, size, LANES), bf16))
    for size in sizes:
        shapes.append(pltpu.VMEM((seq_size - 1, size, LANES), bf16))
    count = masks * seq_size + 2 * (masks - 1) * seq_size + 2 * (seq_size - 1)
    shapes += [
        pltpu.SemaphoreType.DMA((masks, seq_size)),
        pltpu.SemaphoreType.DMA((count,)),
        pltpu.SemaphoreType.DMA((count,)),
    ]
    return shapes


def make_scatter(dp_size, seq_size, slots, out, refs):
    bits = dp_size.bit_length() - 2
    acc, core_in, *rest = refs
    level_in = [rest[:bits], rest[bits : 2 * bits]]
    rest = rest[2 * bits :]
    return Scatter(dp_size, seq_size, slots, out, acc, core_in, level_in, rest[:2], *rest[2:])


def scatter_kernel(dp_size, seq_size, a_slots, m_slots, a_out, m_out, *refs):
    count = len(refs) // 2
    sa = make_scatter(dp_size, seq_size, a_slots, a_out, refs[:count])
    sm = make_scatter(dp_size, seq_size, m_slots, m_out, refs[count:])
    greet(sa.peers())
    sm.begin()
    sa.begin()
    for event in sm.events():
        sm.step(event)
    for event in sa.events():
        sa.step(event)
    sm.finish()
    sa.finish()


ANY = pl.BlockSpec(memory_space=pl.ANY)
LOCAL = pl.BlockSpec(memory_space=pltpu.VMEM)


def shape_of(dims, dtype):
    return jax.ShapeDtypeStruct(dims, dtype)


def per_chip_sequence(inputs, segments, attn_params, mlp_params, cotangent):
    dp_size, n = lax.axis_size("dp"), lax.axis_size("seq")
    devices = dp_size * n
    block = inputs.shape[2]
    length = n * block
    a_rows, m_rows = attn_params.shape[0] // LANES, mlp_params.shape[0] // LANES
    a_own, m_own = to_rows(attn_params), to_rows(mlp_params)
    a_pad, m_pad = a_own.shape[0], m_own.shape[0]
    seg_rows = jnp.pad(segments.reshape(2, block // LANES, LANES), ((0, 0), (0, 8 - block // LANES), (0, 0)))
    send, recv = gather_counts(dp_size, n)
    dma = pltpu.SemaphoreType.DMA
    across = shape_of((HALF_COLS, length), bf16)
    heads = shape_of((HALF_HEADS, length, HD), bf16)
    own = shape_of((2, block, D), bf16)
    (
        m_slots, cot_own, x_own, n1, wqkv, w_proj, vec, qt, kt, vt, qh, kh, vh, bias, lse, att,
    ) = pl.pallas_call(
        functools.partial(forward_kernel, dp_size, n, a_rows),
        out_shape=[
            shape_of((devices, m_pad, LANES), bf16), own, own, shape_of((length, D), bf16),
            shape_of((3, D, HALF_COLS), bf16), shape_of((D, D), bf16), shape_of((8, D), f32),
            across, across, across, heads, heads, heads,
            shape_of((length, length), f32), shape_of((8, length), f32), shape_of((2, 2, block, HALF_COLS), bf16),
        ],
        in_specs=[ANY] * 5,
        out_specs=[ANY] * 2 + [LOCAL] * 14,
        scratch_shapes=[
            pltpu.VMEM((devices, a_pad, LANES), bf16),
            pltpu.VMEM((devices * a_rows, LANES), f32),
            pltpu.VMEM((n, block, D), bf16),
            pltpu.VMEM((n, 8, LANES), jnp.int32),
            pltpu.VMEM((length, LANES), jnp.int32),
            pltpu.VMEM((length, block), f32),
            pltpu.VMEM((HALF_COLS, length), f32),
            pltpu.VMEM((2, block, HALF_COLS), bf16),
            dma((send,)), dma((recv,)), dma((send,)), dma((recv,)), dma((2,)),
            dma((2, 4)), dma((2, n)), dma((2, 2)), dma((2, 2)),
        ],
        compiler_params=pltpu.CompilerParams(collective_id=0, has_side_effects=True, vmem_limit_bytes=VMEM_LIMIT),
    )(inputs[:, 0], seg_rows, cotangent[:, 0], a_own, m_own)

    tokens = 2 * block
    out_own, d_mid, d_att, m_grads, g_proj, g_bias = pl.pallas_call(
        functools.partial(mlp_kernel, m_rows),
        out_shape=[
            shape_of((tokens, D), bf16), shape_of((tokens, D), f32), shape_of((2, tokens, HALF_COLS), bf16),
            shape_of((devices, m_pad, LANES), bf16), shape_of((D * ROW_D, LANES), f32), shape_of((1, D), f32),
        ],
        in_specs=[ANY] + [LOCAL] * 5,
        out_specs=[LOCAL] * 6,
        scratch_shapes=[
            pltpu.VMEM((devices * m_rows, LANES), f32),
            pltpu.VMEM((D, FF), bf16), pltpu.VMEM((FF, D), bf16),
            pltpu.VMEM((tokens, D), f32), pltpu.VMEM((tokens, D), bf16),
            pltpu.VMEM((tokens, D), f32), pltpu.VMEM((tokens, D), f32),
            pltpu.VMEM((1, FF), f32), pltpu.VMEM((1, FF), f32),
            dma(()),
        ],
        compiler_params=pltpu.CompilerParams(vmem_limit_bytes=VMEM_LIMIT),
    )(m_slots, x_own.reshape(tokens, D), cot_own.reshape(tokens, D), att.reshape(2, tokens, HALF_COLS), w_proj, vec)

    out_back, grad_back, a_grads = pl.pallas_call(
        functools.partial(backward_kernel, n, a_rows),
        out_shape=[own, own, shape_of((devices, a_pad, LANES), bf16)],
        in_specs=[ANY] + [LOCAL] * 2 + [ANY] + [LOCAL] * 12,
        out_specs=[ANY] * 2 + [LOCAL],
        scratch_shapes=[
            pltpu.VMEM((devices * a_rows, LANES), f32),
            pltpu.VMEM((n, block, HALF_COLS), bf16),
            pltpu.VMEM((HALF_COLS, length), bf16),
            pltpu.VMEM((HALF_HEADS, length, HD), bf16),
            pltpu.VMEM((length, block), f32),
            pltpu.VMEM((length, block), f32),
            pltpu.VMEM((HALF_HEADS, length, HD), f32),
            pltpu.VMEM((HALF_HEADS, length, HD), f32),
            pltpu.VMEM((HALF_COLS, length), f32),
            pltpu.VMEM((3, length, HALF_COLS), bf16),
            pltpu.VMEM((2, block, D), f32),
            pltpu.VMEM((2, block, D), f32),
            pltpu.VMEM((2, block, D), bf16),
            dma((4, 2)), dma((2, 2)), dma((2, 2)), dma(()),
        ],
        compiler_params=pltpu.CompilerParams(collective_id=1, has_side_effects=True, vmem_limit_bytes=VMEM_LIMIT),
    )(out_own, d_mid, d_att, g_proj, g_bias, x_own, n1, wqkv, vec, qt, kt, qh, kh, vh, bias, lse)

    a_sum, m_sum = pl.pallas_call(
        functools.partial(scatter_kernel, dp_size, n),
        out_shape=[shape_of((a_rows, LANES), f32), shape_of((m_rows, LANES), f32)],
        in_specs=[ANY] * 2,
        out_specs=[LOCAL] * 2,
        scratch_shapes=scatter_scratch(dp_size, n, a_pad) + scatter_scratch(dp_size, n, m_pad),
        compiler_params=pltpu.CompilerParams(collective_id=2, has_side_effects=True, vmem_limit_bytes=VMEM_LIMIT),
    )(a_grads, m_grads)
    return (
        out_back[:, None],
        grad_back.astype(f32)[:, None],
        a_sum.reshape(-1),
        m_sum.reshape(-1),
    )


def solution(mesh):
    in_specs = (
        P(None, "dp", "seq", None),
        P(None, "dp", "seq"),
        P(("dp", "seq")),
        P(("dp", "seq")),
        P(None, "dp", "seq", None),
    )
    out_specs = (
        P(None, "dp", "seq", None),
        P(None, "dp", "seq", None),
        P(("dp", "seq")),
        P(("dp", "seq")),
    )
    one_each = mesh.shape["seq"] == 4 and mesh.shape["dp"] % 2 == 0
    return jax.shard_map(
        per_chip_sequence if one_each else per_device, mesh=mesh, in_specs=in_specs, out_specs=out_specs, check_vma=False
    )
```

profile of v0, /device:TPU:0, one launch (start us, length us, event | category | flops | bytes accessed | tf_op | source)
XLA Modules:
  0.0 295.2 jit_solution(11891009309573866251)
XLA Ops:
  0.6 1.3 pad.12.seg_in
  1.9 1.6 pad.13.a_own
  3.5 1.7 pad.14.m_own
  5.2 119.8 %shard_map.84 = (bf16[32,1168,128]{2,1,0:T(8,128)(2,1)}, bf16[2,256,768]{2,1,0:T(8,128)(2,1)}, bf16[2,256,768]{2,1,0:T(8,128)(2,1)}, bf16[1024,768]{1,0:T(8,128)...) custom-call(bf16[2,256,768]{2,1,0:T(8,128)(2,1)} %bitcast.23, ...), custom_call_target="tpu_custom_call" | custom-call | tf_op jit(solution)/shard_map/pallas_call | solution.py:1235
  125.0 36.6 %shard_map.85 = (bf16[512,768]{1,0:T(8,128)(2,1)}, f32[512,768]{1,0:T(8,128)}, bf16[2,512,384]{2,1,0:T(8,128)(2,1)}, bf16[32,1168,128]{2,1,0:T(8,128)(2,1)}, f32[4608,128]{1,0:T(8,128)}, /*index=5*/f32[1,768]{1,0:T(1,128)}) custom-call(bf16[32,1168,128]{2,1,0:T(8,128)(2,1)} %get-tuple-element.30.m_slots, bf16[512,768]{1,0:T(8,128)(2,1)} %bitcast.19, ...), custom_call_target="tpu_custom_call" | custom-call | tf_op jit(solution)/shard_map/pallas_call | solution.py:1261
  161.6 55.5 %shard_map.86 = (bf16[2,256,768]{2,1,0:T(8,128)(2,1)}, bf16[2,256,768]{2,1,0:T(8,128)(2,1)}, bf16[32,592,128]{2,1,0:T(8,128)(2,1)}) custom-call(bf16[512,768]{1,0:T(8,128)(2,1)} %get-tuple-element.36.out_own, f32[512,768]{1,0:T(8,128)} %get-tuple-element.37.d_mid, bf16[2,512,384]{2,1,0:T(8,128)(2,1)} %get-tuple-element.38.d_att, ...), custom_call_target="tpu_custom_call" | custom-call | tf_op jit(solution)/shard_map/pallas_call | solution.py:1280
  217.2 0.0 copy-start.1
  217.2 74.2 %shard_map.87 = (f32[577,128]{1,0:T(8,128)}, f32[1154,128]{1,0:T(8,128)}) custom-call(bf16[32,592,128]{2,1,0:T(8,128)(2,1)} %get-tuple-element.52.a_slots, bf16[32,1168,128]{2,1,0:T(8,128)(2,1)} %get-tuple-element.53.m_slots), custom_call_target="tpu_custom_call" | custom-call | tf_op jit(solution)/shard_map/pallas_call | solution.py:1304
  291.3 0.0 copy-start
  291.4 0.0 copy-done.1
  291.4 0.0 copy-start.3
  291.4 1.3 bitcast_convert_fusion
  292.6 0.0 copy-done
  292.7 0.0 copy-start.2
  292.7 0.9 copy.14
  293.6 0.0 copy-done.3
  293.6 0.7 copy.15
  294.3 0.0 copy-done.2
  294.3 0.9 copy.16
Async XLA Ops:
  217.2 74.2 %copy-start.1 = (bf16[2,256,768]{2,1,0:T(8,128)(2,1)S(1)}, bf16[2,256,768]{2,1,0:T(8,128)(2,1)}, u32[]{:S(2)}) copy-start(bf16[2,256,768]{2,1,0:T(8,128)(2,1)} %get-tuple-element.51) | copy-start | bytes 2359300
  291.3 1.3 copy-start
  291.4 2.2 copy-start.3
  292.7 1.6 copy-start.2
where the time goes:
time: 295 us
  Pallas kernels  286 us (97%)
  local copies, waits for them, and re-layouts  7.09 us (2%)
    pallas_call x1, Pallas kernels, per_chip_sequence(): pl.pallas_call(functools.partial(forward_kernel, dp_size, n, a_rows), out...  120 us
    pallas_call x1, Pallas kernels, per_chip_sequence(): pl.pallas_call(functools.partial(scatter_kernel, dp_size, n), out_shape=[...  74.2 us
    pallas_call x1, Pallas kernels, per_chip_sequence(): pl.pallas_call(functools.partial(backward_kernel, n, a_rows), out_shape=[...  55.5 us
    pallas_call x1, Pallas kernels, per_chip_sequence(): pl.pallas_call(functools.partial(mlp_kernel, m_rows), out_shape=[shape_of...  36.6 us

commit v1 on v0

--- a/solution.py
+++ b/solution.py
@@ -123,7 +123,7 @@
 class Gather:
     def __init__(self, dp_size, seq_size, own, slots, send_sems, recv_sems):
         self.n = seq_size
-        self.bits = [b for b in range(1, dp_size.bit_length() - 1)]
+        self.bits = list(range(1, dp_size.bit_length() - 1))
         self.dp = lax.axis_index("dp")
         self.z = lax.axis_index("seq")
         self.own, self.slots = own, slots
@@ -136,113 +136,142 @@
 
     def peers(self):
         out = [(self.dp, lax.rem(self.z + k, self.n)) for k in range(1, self.n)]
-        out += [(self.dp ^ (1 << b), self.z) for b in [0] + self.bits]
-        return out
-
-    def slot(self, mask, k):
-        return (self.dp ^ mask) * self.n + lax.rem(self.z + self.n - k, self.n)
-
-    def view(self, mask, k, part):
-        index = self.slot(mask, k)
+        return out + [(self.dp ^ (1 << b), self.z) for b in [0] + self.bits]
+
+    def place(self, i):
+        last = self.n - 1
+        high = self.z > last - self.z
+        near = jnp.where(high, last - self.z, self.z)
+        step = (i // 2) if i % 2 == 0 else -((i + 1) // 2)
+        found = jnp.where(i <= 2 * near, near + step, i)
+        return jnp.where(high, last - found, found)
+
+    def view(self, mask, i, part):
+        index = (self.dp ^ mask) * self.n + self.place(i)
         if part is None:
             return self.slots.at[index]
         start, size = self.parts[part]
         return self.slots.at[index, pl.ds(start, size)]
 
-    def source(self, mask, k, part):
-        if mask == 0 and k == 0:
+    def source(self, mask, i, part):
+        if mask == 0 and i == 0:
             if part is None:
                 return self.own
             start, size = self.parts[part]
             return self.own.at[pl.ds(start, size)]
-        return self.view(mask, k, part)
-
-    def send(self, mask, k, part, to, kind, recv_index):
-        copy = pltpu.make_async_remote_copy(
-            src_ref=self.source(mask, k, part),
-            dst_ref=self.view(mask, k, part),
-            send_sem=self.send_sems.at[len(self.started)],
-            recv_sem=self.recv_sems.at[recv_index],
-            device_id=to,
-            device_id_type=MESH,
-        )
-        copy.start()
-        self.started.append(part)
-
-    def recv_index(self, sibling, part, mask, k):
+        return self.view(mask, i, part)
+
+    def recv_sem(self, sibling, part, mask, i):
         part = 0 if part is None else part
-        return ((sibling * 2 + part) * (2 << len(self.bits)) // 2 + (mask >> 1)) * self.n + k
-
-    def wait(self, sibling, part, mask, k):
-        view = self.view(mask ^ sibling, k, part)
+        count = 1 << len(self.bits)
+        return self.recv_sems.at[((sibling * 2 + part) * count + (mask >> 1)) * self.n + self.place(i)]
+
+    def send(self, mask, i, part, to, recv_sem, when=None):
+        index = len(self.started)
+        self.started.append((part, when))
+
+        def start():
+            pltpu.make_async_remote_copy(
+                src_ref=self.source(mask, i, part), dst_ref=self.view(mask, i, part),
+                send_sem=self.send_sems.at[index], recv_sem=recv_sem, device_id=to, device_id_type=MESH,
+            ).start()
+
+        if when is None:
+            start()
+        else:
+            pl.when(when())(start)
+
+    def wait(self, sibling, part, mask, i):
+        view = self.view(mask ^ sibling, i, part)
         pltpu.make_async_remote_copy(
             src_ref=view, dst_ref=view, send_sem=self.send_sems.at[0],
-            recv_sem=self.recv_sems.at[self.recv_index(sibling, part, mask, k)],
+            recv_sem=self.recv_sem(sibling, part, mask, i),
             device_id=(self.dp, self.z), device_id_type=MESH,
         ).wait_recv()
 
-    def forward(self, part, mask, k):
-        for p in ((0, 1) if part is None else (part,)):
+    def along(self, i, up):
+        if i == 0:
+            to = self.z + 1 if up else self.z - 1
+        else:
+            to = jnp.where(self.place(i) < self.z, self.z + 1, self.z - 1)
+
+        def when():
+            if i == 0:
+                return (self.z < self.n - 1) if up else (self.z > 0)
+            below = self.place(i) < self.z
+            return (below & (self.z < self.n - 1)) | (jnp.logical_not(below) & (self.z > 0))
+
+        self.send(0, i, None, (self.dp, to), self.recv_sem(0, None, 0, i), when)
+
+    def forward(self, part, mask, i, seq=True):
+        if mask == 0 and seq:
+            self.along(i, True)
+        for p in (0, 1) if part is None else (part,):
             order = self.orders[p]
             last = max([order.index(b) for b in self.bits if mask >> b & 1], default=-1)
             for b in order[last + 1 :]:
-                self.send(mask, k, p, (self.dp ^ (1 << b), self.z), 0, self.recv_index(0, p, mask | 1 << b, k))
-        self.send(mask, k, part, (self.dp ^ 1, self.z), 1, self.recv_index(1, part, mask, k))
+                self.send(mask, i, p, (self.dp ^ (1 << b), self.z), self.recv_sem(0, p, mask | 1 << b, i))
+        self.send(mask, i, part, (self.dp ^ 1, self.z), self.recv_sem(1, part, mask, i))
+
+    def begin_seq(self):
+        self.along(0, True)
+        self.along(0, False)
+
+    def begin_bits(self):
+        self.forward(None, 0, 0, False)
 
     def begin(self):
-        for k in range(1, self.n):
-            self.send(0, 0, None, (self.dp, lax.rem(self.z + k, self.n)), 0, self.recv_index(0, None, 0, k))
-        self.forward(None, 0, 0)
+        self.begin_seq()
+        self.begin_bits()
 
     def events(self):
         out = []
-        for k in range(1, self.n):
-            out.append((k, None, 0, k))
-        for k in range(self.n):
-            for p in (0, 1):
-                for level in range(len(self.bits)):
-                    order = self.orders[p]
-                    for low in range(1 << level):
+        for i in range(1, self.n):
+            out.append((i, None, 0, i))
+        for i in range(self.n):
+            for level in range(len(self.bits)):
+                for low in range(1 << level):
+                    for p in (0, 1):
+                        order = self.orders[p]
                         mask = 1 << order[level]
-                        for i in range(level):
-                            if low >> i & 1:
-                                mask |= 1 << order[i]
-                        out.append(((level + 1) * 4 + k, p, mask, k))
+                        for n in range(level):
+                            if low >> n & 1:
+                                mask |= 1 << order[n]
+                        out.append((i + level + 1, p, mask, i))
         out.sort(key=lambda e: e[0])
         return [e[1:] for e in out]
 
     def step(self, event):
-        part, mask, k = event
-        self.wait(0, part, mask, k)
-        self.forward(part, mask, k)
-
-    def sibling_events(self):
-        return [(None, 0, 0)] + self.events()
+        part, mask, i = event
+        self.wait(0, part, mask, i)
+        self.forward(part, mask, i)
 
     def finish_sibling(self):
-        for part, mask, k in self.sibling_events():
-            self.wait(1, part, mask, k)
+        for part, mask, i in [(None, 0, 0)] + self.events():
+            self.wait(1, part, mask, i)
 
     def finish_sends(self):
-        for index, part in enumerate(self.started):
-            start, size = (0, self.rows) if part is None else self.parts[part]
-            view = self.slots.at[0, pl.ds(start, size)]
-            pltpu.make_async_remote_copy(
-                src_ref=view, dst_ref=view, send_sem=self.send_sems.at[index], recv_sem=self.recv_sems.at[0],
-                device_id=(self.dp, self.z), device_id_type=MESH,
-            ).wait_send()
+        for index, (part, when) in enumerate(self.started):
+
+            def wait(index=index, part=part):
+                start, size = (0, self.rows) if part is None else self.parts[part]
+                view = self.slots.at[0, pl.ds(start, size)]
+                pltpu.make_async_remote_copy(
+                    src_ref=view, dst_ref=view, send_sem=self.send_sems.at[index], recv_sem=self.recv_sems.at[0],
+                    device_id=(self.dp, self.z), device_id_type=MESH,
+                ).wait_send()
+
+            if when is None:
+                wait()
+            else:
+                pl.when(when())(wait)
 
 
 def gather_counts(dp_size, seq_size):
     bits = dp_size.bit_length() - 2
-    recv = 4 * (1 << bits) * seq_size
-    send = 0
-    send += seq_size - 1
-    for p in range(2):
-        for mask in range(1 << bits):
-            top = mask.bit_length()
-            send += (bits - top) * seq_size
-    send += seq_size + 2 * ((1 << bits) - 1) * seq_size
+    masks = 1 << bits
+    recv = 4 * masks * seq_size
+    send = seq_size + 1 + seq_size * 2 * (masks - 1) + seq_size * (1 + 2 * (masks - 1))
     return send, recv
 
 
@@ -254,8 +283,8 @@
     for peer in peers:
         pl.semaphore_signal(barrier, inc=1, device_id=peer, device_id_type=MESH)
     pl.semaphore_wait(barrier, len(peers))
-    ca = pltpu.make_async_copy(a_own, a_slots.at[ga.slot(0, 0)], own_sems.at[0])
-    cm = pltpu.make_async_copy(m_own, m_slots.at[gm.slot(0, 0)], own_sems.at[1])
+    ca = pltpu.make_async_copy(a_own, a_slots.at[ga.dp * ga.n + ga.z], own_sems.at[0])
+    cm = pltpu.make_async_copy(m_own, m_slots.at[ga.dp * ga.n + ga.z], own_sems.at[1])
     ca.start()
     cm.start()
     ga.begin()
@@ -514,7 +543,9 @@
 ROW_QKV = 3 * ROW_D
 ROW_HALF = HALF_COLS // LANES
 FF_STEP = 512
-VMEM_LIMIT = 62 * 2**20
+VMEM_LIMIT = 63 * 2**20
+A_FIRST = 7
+PUMP = (4, 3, 3)
 
 ATTN_QKV = 2 * ROW_D
 ATTN_BQ = ATTN_QKV + D * ROW_QKV
@@ -637,11 +668,31 @@
     )
 
 
+def keep_allowed(scores, seg_col, seg_all, b, i, block):
+    parts = []
+    for r in range(block // LANES):
+        row = seg_all[i, r : r + 1, :]
+        allowed = seg_col[b * block : (b + 1) * block, :] == row
+        if b == i:
+            key_pos = lax.broadcasted_iota(jnp.int32, (block, LANES), 0)
+            query_pos = lax.broadcasted_iota(jnp.int32, (block, LANES), 1) + r * LANES
+            allowed = allowed & (key_pos <= query_pos)
+        parts.append(jnp.where(allowed, scores[:, r * LANES : (r + 1) * LANES], score_floor))
+    return jnp.concatenate(parts, axis=1)
+
+
+def segment_columns(seg_all, seg_col, block):
+    for t in range(seg_all.shape[0]):
+        for r in range(block // LANES):
+            row = jnp.broadcast_to(seg_all[t, r : r + 1, :], (LANES, LANES))
+            seg_col[pl.ds(t * block + r * LANES, LANES), :] = row.T
+
+
 def forward_kernel(
     dp_size, seq_size, a_rows,
     x_in, seg_in, cot_in, a_own, m_own,
-    m_slots, cot_own, x_own, n1, wqkv, w_proj, vec, qt, kt, vt, qh, kh, vh, bias, lse, att,
-    a_slots, flat, x_all, seg_all, seg_col, scores, ot, att_out,
+    m_slots, cot_own, x_own, n1, wqkv, w_proj, vec, qt, kt, qh, kh, vh, seg_all, lse, att,
+    a_slots, flat, x_all, vt, seg_col, scores, ot, att_out,
     a_send, a_recv, m_send, m_recv, own_sems, move_send, move_recv, cot_sems, swap_sems,
 ):
     place = Place(seq_size)
@@ -650,37 +701,37 @@
     gm = Gather(dp_size, seq_size, m_own, m_slots, m_send, m_recv)
     greet(place.line_peers() + [(place.dp ^ (1 << b), place.z) for b in ga.bits])
 
+    mine = place.dp * seq_size + place.z
     own_copies = [
-        pltpu.make_async_copy(a_own, a_slots.at[ga.slot(0, 0)], own_sems.at[0]),
-        pltpu.make_async_copy(m_own, m_slots.at[gm.slot(0, 0)], own_sems.at[1]),
+        pltpu.make_async_copy(a_own, a_slots.at[mine], own_sems.at[0]),
+        pltpu.make_async_copy(m_own, m_slots.at[mine], own_sems.at[1]),
     ]
-    for copy in own_copies:
-        copy.start()
+    ga.begin()
     sent = []
     for micro in range(2):
         to = place.worker(micro)
         sent.append(
+            remote(seg_in.at[micro], seg_all.at[place.z], move_send.at[1, micro], move_recv.at[1, place.z], to)
+        )
+        sent.append(
             remote(x_in.at[micro], x_all.at[place.z], move_send.at[0, micro], move_recv.at[0, place.z], to)
-        )
-        sent.append(
-            remote(seg_in.at[micro], seg_all.at[place.z], move_send.at[1, micro], move_recv.at[1, place.z], to)
         )
     for copy in sent:
         copy.start()
-    ga.begin()
-    for micro in range(2):
-        copy = remote(
-            cot_in.at[micro], cot_own.at[place.z // 2], cot_sems.at[0, micro], cot_sems.at[1, place.z // 2],
-            place.worker(micro),
-        )
+    gm.begin_bits()
+    for copy in own_copies:
         copy.start()
-        sent.append(copy)
-    gm.begin()
 
     def arrival(t, kind):
         ref = (x_all, seg_all)[kind].at[t]
         return remote(ref, ref, move_send.at[kind, 0], move_recv.at[kind, t], place.sibling)
 
+    events = ga.events()
+    for event in events[:A_FIRST]:
+        ga.step(event)
+    gm.begin_seq()
+    for event in events[A_FIRST:]:
+        ga.step(event)
     for j in range(2):
         t = place.own_block(j)
         for kind in range(2):
@@ -689,37 +740,27 @@
             copy = remote(ref, ref, move_send.at[kind, 2 + j], move_recv.at[kind, t], place.sibling)
             copy.start()
             sent.append(copy)
-    for event in ga.events():
-        ga.step(event)
-    for j in range(2):
-        for kind in range(2):
-            arrival(place.other_block(j), kind).wait_recv()
-        x_own[j] = x_all[place.own_block(j)]
-
-    for t in range(seq_size):
-        for r in range(block // LANES):
-            row = jnp.broadcast_to(seg_all[t, r : r + 1, :], (LANES, LANES))
-            seg_col[pl.ds(t * block + r * LANES, LANES), :] = row.T
-    chunks = seq_size * block // LANES
-    key_pos = lax.broadcasted_iota(jnp.int32, (LANES, LANES), 0)
-    query_pos = lax.broadcasted_iota(jnp.int32, (LANES, LANES), 1)
-    for q in range(chunks):
-        row = seg_all[q * LANES // block, q % (block // LANES) : q % (block // LANES) + 1, :]
-        top = (q * LANES // block + 1) * block // LANES
-        for k in range(top):
-            rows = slice(k * LANES, (k + 1) * LANES)
-            if k > q:
-                value = jnp.full((LANES, LANES), score_floor, f32)
-            else:
-                allowed = seg_col[rows, :] == row
-                if k == q:
-                    allowed = allowed & (key_pos <= query_pos)
-                value = jnp.where(allowed, 0.0, score_floor)
-            bias[rows, q * LANES : (q + 1) * LANES] = value
-
+    for micro in range(2):
+        copy = remote(
+            cot_in.at[micro], cot_own.at[place.z // 2], cot_sems.at[0, micro], cot_sems.at[1, place.z // 2],
+            place.worker(micro),
+        )
+        copy.start()
+        sent.append(copy)
+
+    m_events = gm.events()
+    pumped = [0]
+
+    def pump(count):
+        for event in m_events[pumped[0] : pumped[0] + count]:
+            gm.step(event)
+        pumped[0] += count
+
+    pump(PUMP[0])
     own_copies[0].wait()
     ga.finish_sibling()
     unflatten(a_slots, flat, a_rows)
+    pump(PUMP[1])
     for section in range(3):
         load_matrix(
             flat, ATTN_QKV + section * ROW_D + place.core * ROW_HALF, ROW_QKV, ROW_HALF, wqkv.at[section], LANES
@@ -732,6 +773,12 @@
     vec[1:2, :] = load_vector(flat, ATTN_BPROJ, ROW_D)
     bias_query = load_vector(flat, ATTN_BQ + place.core * ROW_HALF, ROW_HALF)
     bias_value = load_vector(flat, ATTN_BV + place.core * ROW_HALF, ROW_HALF)
+    pump(PUMP[2])
+    for j in range(2):
+        for kind in range(2):
+            arrival(place.other_block(j), kind).wait_recv()
+        x_own[j] = x_all[place.own_block(j)]
+    segment_columns(seg_all, seg_col, block)
 
     def project(t, carry):
         rows = pl.ds(pl.multiple_of(t * block, block), block)
@@ -751,16 +798,15 @@
     lax.fori_loop(0, seq_size, project, 0)
     lse[...] = jnp.zeros_like(lse)
 
-    m_events = gm.events()
-    per_head = -(-len(m_events) // HALF_HEADS)
+    rest = len(m_events) - pumped[0]
+    per_head = -(-rest // HALF_HEADS)
 
     def one_head(h, carry):
         for c in range(HALF_HEADS):
 
             @pl.when(h == c)
             def _():
-                for event in m_events[c * per_head : (c + 1) * per_head]:
-                    gm.step(event)
+                pump(per_head)
 
         head_rows = pl.ds(pl.multiple_of(h * HD, HD), HD)
         for i in range(seq_size):
@@ -769,7 +815,7 @@
             top = jnp.full((1, block), -jnp.inf, f32)
             for b in range(i + 1):
                 rows = slice(b * block, (b + 1) * block)
-                piece = dot_nn(kh[h, rows, :], query) + bias[rows, columns]
+                piece = keep_allowed(dot_nn(kh[h, rows, :], query), seg_col, seg_all, b, i, block)
                 scores[rows, :] = piece
                 top = jnp.maximum(top, jnp.max(piece, axis=0, keepdims=True))
             total = jnp.zeros((1, block), f32)
@@ -910,16 +956,18 @@
 
 
 def backward_kernel(
-    seq_size, a_rows,
-    out_own, d_mid, d_att, g_proj, g_bias, x_own, n1, wqkv, vec, qt, kt, qh, kh, vh, bias, lse,
-    out_back, grad_back, a_grads,
-    flat, d_all, dt, dh, p_piece, d_piece, dk, dv, dqt, dm, d_n1, d_n1_in, g_out,
-    move_sems, swap_sems, norm_sems, proj_sem,
+    dp_size, seq_size, a_rows,
+    out_own, m_grads, d_mid, d_att, g_proj, g_bias, x_own, n1, wqkv, vec, qt, kt, qh, kh, vh, seg_all, lse,
+    out_back, grad_back, a_out, m_out,
+    flat, d_all, dt, dh, seg_col, p_piece, d_piece, dk, dv, dqt, dm, d_n1, d_n1_in, g_out, core_out,
+    move_sems, swap_sems, norm_sems, proj_sem, *refs,
 ):
     place = Place(seq_size)
     block = x_own.shape[1]
-    length = seq_size * block
-    greet(place.line_peers())
+    count = len(refs) // 2
+    sm = make_scatter(dp_size, seq_size, m_out, refs[:count])
+    sa = make_scatter(dp_size, seq_size, a_out, refs[count:])
+    greet(place.line_peers() + [(place.dp ^ (1 << b), place.z) for b in sm.bits])
     sent = []
     for j in range(2):
         t = place.own_block(j)
@@ -927,6 +975,8 @@
         copy = remote(src, d_all.at[t], swap_sems.at[0, j], swap_sems.at[1, j], place.sibling)
         copy.start()
         sent.append(copy)
+    sm.begin(m_grads)
+    for j in range(2):
         to, micro = place.home(j)
         copy = remote(
             out_own.at[pl.ds(j * block, block)], out_back.at[micro], move_sems.at[0, j], move_sems.at[1, micro], to
@@ -938,6 +988,7 @@
     proj_copy.start()
     for j in range(2):
         d_all[place.own_block(j)] = d_att[place.core, j * block : (j + 1) * block, :]
+    segment_columns(seg_all, seg_col, block)
     for j in range(2):
         ref = d_all.at[place.other_block(j)]
         remote(ref, ref, swap_sems.at[0, j], swap_sems.at[1, j], place.sibling).wait_recv()
@@ -952,39 +1003,67 @@
 
     lax.fori_loop(0, seq_size, spread, 0)
 
-    def one_head(h, carry):
-        head_rows = pl.ds(pl.multiple_of(h * HD, HD), HD)
-        for i in range(seq_size):
-            columns = slice(i * block, (i + 1) * block)
-            query = qt[head_rows, columns]
-            d_query = dt[head_rows, columns]
-            level = lse[pl.ds(h, 1), columns]
-            delta = jnp.zeros((1, block), f32)
-            for b in range(i + 1):
-                rows = slice(b * block, (b + 1) * block)
-                probs = jnp.exp(dot_nn(kh[h, rows, :], query) + bias[rows, columns] - level)
-                d_probs = dot_nn(vh[h, rows, :], d_query)
-                delta = delta + jnp.sum(probs * d_probs, axis=0, keepdims=True)
-                p_piece[rows, :] = probs
-                d_piece[rows, :] = d_probs
-            result = jnp.zeros((HD, block), f32)
-            for b in range(i + 1):
-                rows = slice(b * block, (b + 1) * block)
-                probs = p_piece[rows, :]
-                d_scores = (probs * (d_piece[rows, :] - delta)).astype(bf16)
-                key_part = dot_nn(d_scores, qh[h, columns, :])
-                value_part = dot_nn(probs.astype(bf16), dh[h, columns, :])
-                if b == i:
-                    dk[h, rows, :] = key_part
-                    dv[h, rows, :] = value_part
-                else:
-                    dk[h, rows, :] += key_part
-                    dv[h, rows, :] += value_part
-                result = result + dot_nn(kt[head_rows, rows], d_scores)
-            dqt[head_rows, columns] = result * (1.0 / math.sqrt(HD))
+    m_events = sm.events()
+    first = len(m_events) - len([e for e in m_events if e[0] != "c"])
+    pumped = [0]
+
+    def pump(count):
+        for event in m_events[pumped[0] : pumped[0] + count]:
+            sm.step(event)
+        pumped[0] += count
+
+    pump(first)
+    per_head = -(-(len(m_events) - first) // HALF_HEADS)
+
+    def one_pair(pair, carry):
+        for side in range(2):
+            for c in range(HALF_HEADS // 2):
+
+                @pl.when(pair == c)
+                def _():
+                    begin = first + (2 * c + side) * per_head
+                    for event in m_events[begin : begin + per_head]:
+                        sm.step(event)
+
+            h = 2 * pair + side
+            head_rows = pl.ds(pl.multiple_of(h * HD, HD), HD)
+            for i in range(seq_size):
+                columns = slice(i * block, (i + 1) * block)
+                query = qt[head_rows, columns]
+                d_query = dt[head_rows, columns]
+                level = lse[pl.ds(h, 1), columns]
+                delta = jnp.zeros((1, block), f32)
+                for b in range(i + 1):
+                    rows = slice(b * block, (b + 1) * block)
+                    probs = jnp.exp(
+                        keep_allowed(dot_nn(kh[h, rows, :], query), seg_col, seg_all, b, i, block) - level
+                    )
+                    d_probs = dot_nn(vh[h, rows, :], d_query)
+                    delta = delta + jnp.sum(probs * d_probs, axis=0, keepdims=True)
+                    p_piece[rows, :] = probs
+                    d_piece[rows, :] = d_probs
+                result = jnp.zeros((HD, block), f32)
+                for b in range(i + 1):
+                    rows = slice(b * block, (b + 1) * block)
+                    probs = p_piece[rows, :]
+                    d_scores = (probs * (d_piece[rows, :] - delta)).astype(bf16)
+                    key_part = dot_nn(d_scores, qh[h, columns, :])
+                    value_part = dot_nn(probs.astype(bf16), dh[h, columns, :])
+                    if b == i:
+                        dk[side, rows, :] = key_part
+                        dv[side, rows, :] = value_part
+                    else:
+                        dk[side, rows, :] += key_part
+                        dv[side, rows, :] += value_part
+                    result = result + dot_nn(kt[head_rows, rows], d_scores)
+                dqt[head_rows, columns] = result * (1.0 / math.sqrt(HD))
+        lanes = pl.ds(pl.multiple_of(pair * LANES, LANES), LANES)
+        for section, part in ((1, dk), (2, dv)):
+            dm[section, :, lanes] = jnp.concatenate([part[0], part[1]], axis=1).astype(bf16)
         return carry
 
-    lax.fori_loop(0, HALF_HEADS, one_head, 0)
+    lax.fori_loop(0, HALF_HEADS // 2, one_pair, 0)
+    pumped[0] = len(m_events)
 
     query_sum = jnp.zeros((1, HALF_COLS), f32)
     value_sum = jnp.zeros((1, HALF_COLS), f32)
@@ -993,10 +1072,7 @@
         low = dqt[:, rows].T.astype(bf16)
         dm[0, rows, :] = low
         query_sum += jnp.sum(low.astype(f32), axis=0, keepdims=True)
-        for section, part in ((1, dk), (2, dv)):
-            low = jnp.concatenate([part[h, rows, :] for h in range(HALF_HEADS)], axis=1).astype(bf16)
-            dm[section, rows, :] = low
-        value_sum += jnp.sum(low.astype(f32), axis=0, keepdims=True)
+        value_sum += jnp.sum(dm[2, rows, :].astype(f32), axis=0, keepdims=True)
 
     def to_norm(t):
         rows = pl.ds(pl.multiple_of(t * block, block), block)
@@ -1028,13 +1104,18 @@
         gain_sum += jnp.sum(grad * normal, axis=0, keepdims=True)
         shift_sum += jnp.sum(grad, axis=0, keepdims=True)
         g_out[j] = (d_mid[j * block : (j + 1) * block, :] + norm_back(normal, scale, grad, gain)).astype(bf16)
+    store_vector(flat, 0, gain_sum)
+    store_vector(flat, ROW_D, shift_sum)
+    sa.begin_flat(flat, a_rows, core_out)
+    for j in range(2):
         to, micro = place.home(j)
         copy = remote(g_out.at[j], grad_back.at[micro], move_sems.at[2, j], move_sems.at[3, micro], to)
         copy.start()
         sent.append(copy)
-    store_vector(flat, 0, gain_sum)
-    store_vector(flat, ROW_D, shift_sum)
-    flatten(flat, a_grads, a_rows)
+    for event in sa.events():
+        sa.step(event)
+    sm.finish()
+    sa.finish()
     for micro in range(2):
         for kind, ref in ((1, out_back), (3, grad_back)):
             remote(
@@ -1045,15 +1126,16 @@
 
 
 class Scatter:
-    def __init__(self, dp_size, seq_size, slots, out, acc, core_in, level_in, seq_in, load_sems, send_sems, recv_sems):
+    def __init__(self, dp_size, seq_size, out, acc, core_in, level_in, seq_in, load_sems, send_sems, recv_sems):
         self.n = seq_size
         self.bits = list(range(1, dp_size.bit_length() - 1))
         self.masks = [m << 1 for m in range(1 << len(self.bits))]
         self.dp = lax.axis_index("dp")
         self.z = lax.axis_index("seq")
-        self.slots, self.out, self.acc = slots, out, acc
+        self.out, self.acc = out, acc
+        self.loads = []
         self.core_in, self.level_in, self.seq_in = core_in, level_in, seq_in
-        rows = slots.shape[1]
+        rows = acc.shape[2]
         half = rows // 32 * 16
         self.parts = [(0, half), (half, rows - half)]
         self.orders = [self.bits[::-1], self.bits]
@@ -1067,10 +1149,9 @@
     def slot(self, mask, k):
         return (self.dp ^ mask) * self.n + lax.rem(self.z + k, self.n)
 
-    def send(self, src, dst, to, key):
-        copy = remote(src, dst, self.send_sems.at[len(self.started)], self.recv_sems.at[self.index(*key)], to)
-        copy.start()
-        self.started.append(copy)
+    def send(self, src, dst, to, key, part=None):
+        remote(src, dst, self.send_sems.at[len(self.started)], self.recv_sems.at[self.index(*key)], to).start()
+        self.started.append(part)
 
     def wait(self, ref, key):
         remote(ref, ref, self.send_sems.at[0], self.recv_sems.at[self.index(*key)], (self.dp, self.z)).wait_recv()
@@ -1078,16 +1159,27 @@
     def turn(self):
         return list(range(1, self.n)) + [0]
 
-    def begin(self):
+    def begin(self, slots):
         for k in self.turn():
             for mask in self.masks[::-1]:
                 i = self.masks.index(mask)
-                pltpu.make_async_copy(
-                    self.slots.at[self.slot(mask, k)], self.acc.at[i, k], self.load_sems.at[i, k]
-                ).start()
+                load = pltpu.make_async_copy(
+                    slots.at[self.slot(mask, k)], self.acc.at[i, k], self.load_sems.at[i, k]
+                )
+                load.start()
+                self.loads.append(load)
                 self.send(
-                    self.slots.at[self.slot(mask ^ 1, k)], self.core_in.at[i, k], (self.dp ^ 1, self.z), ("c", i, k)
+                    slots.at[self.slot(mask ^ 1, k)], self.core_in.at[i, k], (self.dp ^ 1, self.z), ("c", i, k)
                 )
+
+    def begin_flat(self, flat, rows, core_out):
+        for k in self.turn():
+            for mask in self.masks[::-1]:
+                i = self.masks.index(mask)
+                for target, which in ((core_out, mask ^ 1), (self.acc, mask)):
+                    target[i, k, :rows, :] = flat[pl.ds(self.slot(which, k) * rows, rows), :].astype(bf16)
+                    target[i, k, rows:, :] = jnp.zeros((target.shape[2] - rows, LANES), bf16)
+                self.send(core_out.at[i, k], self.core_in.at[i, k], (self.dp ^ 1, self.z), ("c", i, k))
 
     def cell(self, part, level, mask):
         free = [b for b in self.bits if b not in self.orders[part][: level + 1]]
@@ -1101,19 +1193,19 @@
         if level == len(order):
             if k:
                 to = (self.dp, lax.rem(self.z + k, self.n))
-                self.send(src, self.seq_in[part].at[k - 1], to, ("z", part, k))
+                self.send(src, self.seq_in[part].at[k - 1], to, ("z", part, k), part)
             return
         bit = 1 << order[level]
         if mask & bit:
             rest = mask ^ bit
             dst = self.level_in[part][level].at[self.cell(part, level, rest), k]
-            self.send(src, dst, (self.dp ^ bit, self.z), ("l", part, level, rest, k))
+            self.send(src, dst, (self.dp ^ bit, self.z), ("l", part, level, rest, k), part)
 
     def events(self):
         out = []
         for turn, k in enumerate(self.turn()):
             for mask in self.masks[::-1]:
-                out.append((turn, ("c", mask, k)))
+                out.append((turn * 0.1, ("c", mask, k)))
             for level in range(len(self.bits)):
                 for part in (0, 1):
                     past = self.orders[part][: level + 1]
@@ -1127,9 +1219,8 @@
         if event[0] == "c":
             _, mask, k = event
             i = self.masks.index(mask)
-            pltpu.make_async_copy(
-                self.slots.at[self.slot(mask, k)], self.acc.at[i, k], self.load_sems.at[i, k]
-            ).wait()
+            if self.loads:
+                pltpu.make_async_copy(self.acc.at[i, k], self.acc.at[i, k], self.load_sems.at[i, k]).wait()
             self.wait(self.core_in.at[i, k], ("c", i, k))
             self.acc[i, k] = (self.acc[i, k].astype(f32) + self.core_in[i, k].astype(f32)).astype(bf16)
             for part in (0, 1):
@@ -1154,12 +1245,10 @@
                 self.wait(self.seq_in[part].at[k - 1], ("z", part, k))
                 total = total + self.seq_in[part][k - 1, :size].astype(f32)
             self.out[start : start + size, :] = total
-        for copy in self.started:
-            copy.wait_send()
-
-    def peers(self):
-        out = [(self.dp, lax.rem(self.z + k, self.n)) for k in range(1, self.n)]
-        return out + [(self.dp ^ (1 << b), self.z) for b in [0] + self.bits]
+        for index, part in enumerate(self.started):
+            start, size = (0, self.acc.shape[2]) if part is None else self.parts[part]
+            ref = self.acc.at[0, 0, pl.ds(start, size)]
+            remote(ref, ref, self.send_sems.at[index], self.recv_sems.at[0], (self.dp, self.z)).wait_send()
 
 
 def scatter_scratch(dp_size, seq_size, rows):
@@ -1185,27 +1274,12 @@
     return shapes
 
 
-def make_scatter(dp_size, seq_size, slots, out, refs):
+def make_scatter(dp_size, seq_size, out, refs):
     bits = dp_size.bit_length() - 2
     acc, core_in, *rest = refs
     level_in = [rest[:bits], rest[bits : 2 * bits]]
     rest = rest[2 * bits :]
-    return Scatter(dp_size, seq_size, slots, out, acc, core_in, level_in, rest[:2], *rest[2:])
-
-
-def scatter_kernel(dp_size, seq_size, a_slots, m_slots, a_out, m_out, *refs):
-    count = len(refs) // 2
-    sa = make_scatter(dp_size, seq_size, a_slots, a_out, refs[:count])
-    sm = make_scatter(dp_size, seq_size, m_slots, m_out, refs[count:])
-    greet(sa.peers())
-    sm.begin()
-    sa.begin()
-    for event in sm.events():
-        sm.step(event)
-    for event in sa.events():
-        sa.step(event)
-    sm.finish()
-    sa.finish()
+    return Scatter(dp_size, seq_size, out, acc, core_in, level_in, rest[:2], *rest[2:])
 
 
 ANY = pl.BlockSpec(memory_space=pl.ANY)
@@ -1231,22 +1305,22 @@
     heads = shape_of((HALF_HEADS, length, HD), bf16)
     own = shape_of((2, block, D), bf16)
     (
-        m_slots, cot_own, x_own, n1, wqkv, w_proj, vec, qt, kt, vt, qh, kh, vh, bias, lse, att,
+        m_slots, cot_own, x_own, n1, wqkv, w_proj, vec, qt, kt, qh, kh, vh, seg_all, lse, att,
     ) = pl.pallas_call(
         functools.partial(forward_kernel, dp_size, n, a_rows),
         out_shape=[
             shape_of((devices, m_pad, LANES), bf16), own, own, shape_of((length, D), bf16),
             shape_of((3, D, HALF_COLS), bf16), shape_of((D, D), bf16), shape_of((8, D), f32),
-            across, across, across, heads, heads, heads,
-            shape_of((length, length), f32), shape_of((8, length), f32), shape_of((2, 2, block, HALF_COLS), bf16),
+            across, across, heads, heads, heads,
+            shape_of((n, 8, LANES), jnp.int32), shape_of((8, length), f32), shape_of((2, 2, block, HALF_COLS), bf16),
         ],
         in_specs=[ANY] * 5,
-        out_specs=[ANY] * 2 + [LOCAL] * 14,
+        out_specs=[ANY] * 2 + [LOCAL] * 13,
         scratch_shapes=[
             pltpu.VMEM((devices, a_pad, LANES), bf16),
             pltpu.VMEM((devices * a_rows, LANES), f32),
             pltpu.VMEM((n, block, D), bf16),
-            pltpu.VMEM((n, 8, LANES), jnp.int32),
+            pltpu.VMEM((HALF_COLS, length), bf16),
             pltpu.VMEM((length, LANES), jnp.int32),
             pltpu.VMEM((length, block), f32),
             pltpu.VMEM((HALF_COLS, length), f32),
@@ -1277,38 +1351,34 @@
         compiler_params=pltpu.CompilerParams(vmem_limit_bytes=VMEM_LIMIT),
     )(m_slots, x_own.reshape(tokens, D), cot_own.reshape(tokens, D), att.reshape(2, tokens, HALF_COLS), w_proj, vec)
 
-    out_back, grad_back, a_grads = pl.pallas_call(
-        functools.partial(backward_kernel, n, a_rows),
-        out_shape=[own, own, shape_of((devices, a_pad, LANES), bf16)],
-        in_specs=[ANY] + [LOCAL] * 2 + [ANY] + [LOCAL] * 12,
-        out_specs=[ANY] * 2 + [LOCAL],
+    masks = dp_size // 2
+    out_back, grad_back, a_sum, m_sum = pl.pallas_call(
+        functools.partial(backward_kernel, dp_size, n, a_rows),
+        out_shape=[own, own, shape_of((a_rows, LANES), f32), shape_of((m_rows, LANES), f32)],
+        in_specs=[ANY] * 2 + [LOCAL] * 2 + [ANY] + [LOCAL] * 12,
+        out_specs=[ANY] * 2 + [LOCAL] * 2,
         scratch_shapes=[
             pltpu.VMEM((devices * a_rows, LANES), f32),
             pltpu.VMEM((n, block, HALF_COLS), bf16),
             pltpu.VMEM((HALF_COLS, length), bf16),
             pltpu.VMEM((HALF_HEADS, length, HD), bf16),
+            pltpu.VMEM((length, LANES), jnp.int32),
             pltpu.VMEM((length, block), f32),
             pltpu.VMEM((length, block), f32),
-            pltpu.VMEM((HALF_HEADS, length, HD), f32),
-            pltpu.VMEM((HALF_HEADS, length, HD), f32),
+            pltpu.VMEM((2, length, HD), f32),
+            pltpu.VMEM((2, length, HD), f32),
             pltpu.VMEM((HALF_COLS, length), f32),
             pltpu.VMEM((3, length, HALF_COLS), bf16),
             pltpu.VMEM((2, block, D), f32),
             pltpu.VMEM((2, block, D), f32),
             pltpu.VMEM((2, block, D), bf16),
+            pltpu.VMEM((masks, n, a_pad, LANES), bf16),
             dma((4, 2)), dma((2, 2)), dma((2, 2)), dma(()),
-        ],
+        ]
+        + scatter_scratch(dp_size, n, m_pad)
+        + scatter_scratch(dp_size, n, a_pad),
         compiler_params=pltpu.CompilerParams(collective_id=1, has_side_effects=True, vmem_limit_bytes=VMEM_LIMIT),
-    )(out_own, d_mid, d_att, g_proj, g_bias, x_own, n1, wqkv, vec, qt, kt, qh, kh, vh, bias, lse)
-
-    a_sum, m_sum = pl.pallas_call(
-        functools.partial(scatter_kernel, dp_size, n),
-        out_shape=[shape_of((a_rows, LANES), f32), shape_of((m_rows, LANES), f32)],
-        in_specs=[ANY] * 2,
-        out_specs=[LOCAL] * 2,
-        scratch_shapes=scatter_scratch(dp_size, n, a_pad) + scatter_scratch(dp_size, n, m_pad),
-        compiler_params=pltpu.CompilerParams(collective_id=2, has_side_effects=True, vmem_limit_bytes=VMEM_LIMIT),
-    )(a_grads, m_grads)
+    )(out_own, m_grads, d_mid, d_att, g_proj, g_bias, x_own, n1, wqkv, vec, qt, kt, qh, kh, vh, seg_all, lse)
     return (
         out_back[:, None],
         grad_back.astype(f32)[:, None],

time: 295 us -> 252 us (0.85)
  Pallas kernels: 286 us -> 242 us
    pallas_call x1, Pallas kernels: 120 us -> 95.8 us  [per_chip_sequence(): pl.pallas_call(functools.partial(forward_kernel, dp_size, n, a_rows), out...]
    pallas_call x2 -> x1, Pallas kernels: 130 us -> 109 us  [per_chip_sequence(): pl.pallas_call(functools.partial(backward_kernel, dp_size, n, a_rows), ou...]
where the time goes in v1:
time: 252 us
  Pallas kernels  242 us (96%)
  local copies, waits for them, and re-layouts  7.05 us (3%)
    pallas_call x1, Pallas kernels, per_chip_sequence(): pl.pallas_call(functools.partial(backward_kernel, dp_size, n, a_rows), ou...  109 us
    pallas_call x1, Pallas kernels, per_chip_sequence(): pl.pallas_call(functools.partial(forward_kernel, dp_size, n, a_rows), out...  95.8 us
    pallas_call x1, Pallas kernels, per_chip_sequence(): pl.pallas_call(functools.partial(mlp_kernel, m_rows), out_shape=[shape_of...  36.7 us

profile of v1, /device:TPU:0, one launch (start us, length us, event | category | flops | bytes accessed | tf_op | source)
XLA Modules:
  0.0 251.9 jit_solution(13963586819942640549)
XLA Ops:
  0.6 1.3 pad.12.seg_in
  1.9 1.6 pad.13.a_own
  3.5 1.7 pad.14.m_own
  5.2 95.8 %shard_map.84 = (bf16[32,1168,128]{2,1,0:T(8,128)(2,1)}, bf16[2,256,768]{2,1,0:T(8,128)(2,1)}, bf16[2,256,768]{2,1,0:T(8,128)(2,1)}, bf16[1024,768]{1,0:T(8,128)...) custom-call(bf16[2,256,768]{2,1,0:T(8,128)(2,1)} %bitcast.23, ...), custom_call_target="tpu_custom_call" | custom-call | tf_op jit(solution)/shard_map/pallas_call | solution.py:1309
  101.0 36.7 %shard_map.85 = (bf16[512,768]{1,0:T(8,128)(2,1)}, f32[512,768]{1,0:T(8,128)}, bf16[2,512,384]{2,1,0:T(8,128)(2,1)}, bf16[32,1168,128]{2,1,0:T(8,128)(2,1)}, f32[4608,128]{1,0:T(8,128)}, /*index=5*/f32[1,768]{1,0:T(1,128)}) custom-call(bf16[32,1168,128]{2,1,0:T(8,128)(2,1)} %get-tuple-element.29.m_slots, bf16[512,768]{1,0:T(8,128)(2,1)} %bitcast.19, ...), custom_call_target="tpu_custom_call" | custom-call | tf_op jit(solution)/shard_map/pallas_call | solution.py:1335
  137.7 109.2 %shard_map.86 = (bf16[2,256,768]{2,1,0:T(8,128)(2,1)}, bf16[2,256,768]{2,1,0:T(8,128)(2,1)}, f32[577,128]{1,0:T(8,128)}, f32[1154,128]{1,0:T(8,128)}) custom-call(bf16[512,768]{1,0:T(8,128)(2,1)} %get-tuple-element.35.out_own, bf16[32,1168,128]{2,1,0:T(8,128)(2,1)} %get-tuple-element.36.m_grads, f32[512,768]{1,0:T(8,128)} %get-tuple-element.37.d_mid, ...), custom_call_target="tpu_custom_call" | custom-call | tf_op jit(solution)/shard_map/pallas_call | solution.py:1355
  246.9 0.0 copy-start
  247.0 0.0 copy-start.2
  247.0 2.5 bitcast_convert_fusion
  249.4 0.0 copy-done
  249.4 0.0 copy-start.1
  249.4 0.9 copy.14
  250.3 0.0 copy-done.2
  250.3 0.7 copy.15
  251.1 0.0 copy-done.1
  251.1 0.9 copy.16
Async XLA Ops:
  246.9 2.5 copy-start
  247.0 3.4 %copy-start.2 = (f32[577,128]{1,0:T(8,128)S(1)}, f32[577,128]{1,0:T(8,128)}, u32[]{:S(2)}) copy-start(f32[577,128]{1,0:T(8,128)} %get-tuple-element.52) | copy-start | bytes 886276
  249.4 1.6 copy-start.1

commit v2 on v1

--- a/solution.py
+++ b/solution.py
@@ -118,6 +118,15 @@
 
 def pad_rows(rows):
     return -(-rows // 16) * 16
+
+
+def nearest(z, n, i):
+    last = n - 1
+    high = z > last - z
+    near = jnp.where(high, last - z, z)
+    step = (i // 2) if i % 2 == 0 else -((i + 1) // 2)
+    found = jnp.where(i <= 2 * near, near + step, i)
+    return jnp.where(high, last - found, found)
 
 
 class Gather:
@@ -139,30 +148,20 @@
         return out + [(self.dp ^ (1 << b), self.z) for b in [0] + self.bits]
 
     def place(self, i):
-        last = self.n - 1
-        high = self.z > last - self.z
-        near = jnp.where(high, last - self.z, self.z)
-        step = (i // 2) if i % 2 == 0 else -((i + 1) // 2)
-        found = jnp.where(i <= 2 * near, near + step, i)
-        return jnp.where(high, last - found, found)
+        return nearest(self.z, self.n, i)
 
     def view(self, mask, i, part):
         index = (self.dp ^ mask) * self.n + self.place(i)
-        if part is None:
-            return self.slots.at[index]
         start, size = self.parts[part]
         return self.slots.at[index, pl.ds(start, size)]
 
     def source(self, mask, i, part):
         if mask == 0 and i == 0:
-            if part is None:
-                return self.own
             start, size = self.parts[part]
             return self.own.at[pl.ds(start, size)]
         return self.view(mask, i, part)
 
     def recv_sem(self, sibling, part, mask, i):
-        part = 0 if part is None else part
         count = 1 << len(self.bits)
         return self.recv_sems.at[((sibling * 2 + part) * count + (mask >> 1)) * self.n + self.place(i)]
 
@@ -189,7 +188,7 @@
             device_id=(self.dp, self.z), device_id_type=MESH,
         ).wait_recv()
 
-    def along(self, i, up):
+    def along(self, i, part, up):
         if i == 0:
             to = self.z + 1 if up else self.z - 1
         else:
@@ -201,45 +200,51 @@
             below = self.place(i) < self.z
             return (below & (self.z < self.n - 1)) | (jnp.logical_not(below) & (self.z > 0))
 
-        self.send(0, i, None, (self.dp, to), self.recv_sem(0, None, 0, i), when)
-
-    def forward(self, part, mask, i, seq=True):
-        if mask == 0 and seq:
-            self.along(i, True)
-        for p in (0, 1) if part is None else (part,):
-            order = self.orders[p]
-            last = max([order.index(b) for b in self.bits if mask >> b & 1], default=-1)
-            for b in order[last + 1 :]:
-                self.send(mask, i, p, (self.dp ^ (1 << b), self.z), self.recv_sem(0, p, mask | 1 << b, i))
+        self.send(0, i, part, (self.dp, to), self.recv_sem(0, part, 0, i), when)
+
+    def forward(self, part, mask, i):
+        if mask == 0 and i:
+            self.along(i, part, True)
+        order = self.orders[part]
+        for level in range(len(order)):
+            if not any(mask >> b & 1 for b in order[level:]):
+                bit = 1 << order[level]
+                self.send(mask, i, part, (self.dp ^ bit, self.z), self.recv_sem(0, part, mask | bit, i))
         self.send(mask, i, part, (self.dp ^ 1, self.z), self.recv_sem(1, part, mask, i))
 
     def begin_seq(self):
-        self.along(0, True)
-        self.along(0, False)
+        for part in (0, 1):
+            for up in (True, False):
+                self.along(0, part, up)
 
     def begin_bits(self):
-        self.forward(None, 0, 0, False)
+        for level in range(len(self.bits)):
+            for part in (0, 1):
+                bit = 1 << self.orders[part][level]
+                self.send(0, 0, part, (self.dp ^ bit, self.z), self.recv_sem(0, part, bit, 0))
+        for part in (0, 1):
+            self.send(0, 0, part, (self.dp ^ 1, self.z), self.recv_sem(1, part, 0, 0))
 
     def begin(self):
         self.begin_seq()
         self.begin_bits()
 
-    def events(self):
+    def events(self, begin=0, seq_gap=1, level_gap=1):
         out = []
-        for i in range(1, self.n):
-            out.append((i, None, 0, i))
         for i in range(self.n):
-            for level in range(len(self.bits)):
-                for low in range(1 << level):
-                    for p in (0, 1):
-                        order = self.orders[p]
+            for part in (0, 1):
+                at = begin + (i + 0.5 * part - 0.5) * seq_gap if i else 0
+                if i:
+                    out.append((at, (part, 0, i)))
+                order = self.orders[part]
+                for level in range(len(order)):
+                    for low in range(1 << level):
                         mask = 1 << order[level]
                         for n in range(level):
                             if low >> n & 1:
                                 mask |= 1 << order[n]
-                        out.append((i + level + 1, p, mask, i))
-        out.sort(key=lambda e: e[0])
-        return [e[1:] for e in out]
+                        out.append((at + (level + 1) * level_gap, (part, mask, i)))
+        return sorted(out, key=lambda e: e[0])
 
     def step(self, event):
         part, mask, i = event
@@ -247,14 +252,14 @@
         self.forward(part, mask, i)
 
     def finish_sibling(self):
-        for part, mask, i in [(None, 0, 0)] + self.events():
+        for part, mask, i in [(0, 0, 0), (1, 0, 0)] + [event for _, event in self.events()]:
             self.wait(1, part, mask, i)
 
     def finish_sends(self):
         for index, (part, when) in enumerate(self.started):
 
             def wait(index=index, part=part):
-                start, size = (0, self.rows) if part is None else self.parts[part]
+                start, size = self.parts[part]
                 view = self.slots.at[0, pl.ds(start, size)]
                 pltpu.make_async_remote_copy(
                     src_ref=view, dst_ref=view, send_sem=self.send_sems.at[index], recv_sem=self.recv_sems.at[0],
@@ -271,7 +276,7 @@
     bits = dp_size.bit_length() - 2
     masks = 1 << bits
     recv = 4 * masks * seq_size
-    send = seq_size + 1 + seq_size * 2 * (masks - 1) + seq_size * (1 + 2 * (masks - 1))
+    send = 2 * (seq_size + 1 + seq_size * (masks - 1) + seq_size * masks)
     return send, recv
 
 
@@ -289,10 +294,10 @@
     cm.start()
     ga.begin()
     gm.begin()
-    for e in ga.events():
-        ga.step(e)
-    for e in gm.events():
-        gm.step(e)
+    for _, event in ga.events():
+        ga.step(event)
+    for _, event in gm.events():
+        gm.step(event)
     ca.wait()
     cm.wait()
     ga.finish_sibling()
@@ -544,8 +549,19 @@
 ROW_HALF = HALF_COLS // LANES
 FF_STEP = 512
 VMEM_LIMIT = 63 * 2**20
-A_FIRST = 7
-PUMP = (4, 3, 3)
+
+A_TIMES = (3.0, 6.0, 4.0)
+M_TIMES = (12.0, 9.0, 6.0)
+M_OWN = 8.0
+M_SEQ = 0.0
+M_BITS = 4.0
+SEND_X = 6.0
+SHARE_X = 28.0
+SEND_COT = 45.0
+FORWARD_START = 30.0
+HEAD_FORWARD = 3.3
+BACKWARD_START = 8.0
+HEAD_BACKWARD = 5.8
 
 ATTN_QKV = 2 * ROW_D
 ATTN_BQ = ATTN_QKV + D * ROW_QKV
@@ -608,6 +624,49 @@
         return (self.base + lax.rem(self.z, 2), self.own_block(j)), self.z // 2
 
 
+def split_heads(piece, heads, rows):
+    lane = lax.broadcasted_iota(jnp.int32, (piece.shape[0], LANES), 1)
+    for h in range(HALF_HEADS):
+        pair = piece[:, h // 2 * LANES : (h // 2 + 1) * LANES]
+        heads[h, rows, :] = jnp.where(lane // HD == h % 2, pair, jnp.zeros_like(pair))
+
+
+class Action:
+    def step(self, action):
+        action()
+
+
+class Steps:
+    def __init__(self, timed):
+        self.queue = sorted(timed, key=lambda e: e[0])
+
+    def take(self, time):
+        out = [event for at, event in self.queue if at <= time]
+        self.queue = [e for e in self.queue if e[0] > time]
+        return out
+
+    def until(self, time):
+        for owner, event in self.take(time):
+            owner.step(event)
+
+    def plan(self, start, points):
+        out = {}
+        for point, length in points:
+            out[point] = self.take(start)
+            start += length
+        return out
+
+
+def handle(plan, index):
+    for turn, events in enumerate(plan):
+        if events:
+
+            @pl.when(index == turn)
+            def _():
+                for owner, event in events:
+                    owner.step(event)
+
+
 def greet(peers):
     barrier = pltpu.get_barrier_semaphore()
     for peer in peers:
@@ -618,14 +677,6 @@
 def unflatten(slots, flat, rows):
     def body(s, carry):
         flat[pl.ds(s * rows, rows), :] = slots[s, :rows, :].astype(f32)
-        return carry
-
-    lax.fori_loop(0, slots.shape[0], body, 0)
-
-
-def flatten(flat, slots, rows):
-    def body(s, carry):
-        slots[s, :rows, :] = flat[pl.ds(s * rows, rows), :].astype(bf16)
         return carry
 
     lax.fori_loop(0, slots.shape[0], body, 0)
@@ -691,9 +742,11 @@
 def forward_kernel(
     dp_size, seq_size, a_rows,
     x_in, seg_in, cot_in, a_own, m_own,
-    m_slots, cot_own, x_own, n1, wqkv, w_proj, vec, qt, kt, qh, kh, vh, seg_all, lse, att,
+    m_slots, cot_own, n1_out, wqkv_out, qt_out, kt_out, qh_out, kh_out, vh_out,
+    x_own, w_proj, vec, seg_all, lse, att,
+    n1, wqkv, qt, kt, qh, kh, vh,
     a_slots, flat, x_all, vt, seg_col, scores, ot, att_out,
-    a_send, a_recv, m_send, m_recv, own_sems, move_send, move_recv, cot_sems, swap_sems,
+    a_send, a_recv, m_send, m_recv, own_sems, move_send, move_recv, cot_sems, swap_sems, keep_sems,
 ):
     place = Place(seq_size)
     block = x_in.shape[1]
@@ -707,60 +760,54 @@
         pltpu.make_async_copy(m_own, m_slots.at[mine], own_sems.at[1]),
     ]
     ga.begin()
-    sent = []
-    for micro in range(2):
-        to = place.worker(micro)
-        sent.append(
-            remote(seg_in.at[micro], seg_all.at[place.z], move_send.at[1, micro], move_recv.at[1, place.z], to)
-        )
-        sent.append(
-            remote(x_in.at[micro], x_all.at[place.z], move_send.at[0, micro], move_recv.at[0, place.z], to)
-        )
-    for copy in sent:
-        copy.start()
-    gm.begin_bits()
     for copy in own_copies:
         copy.start()
+    sent = []
+
+    def launch(copy):
+        copy.start()
+        sent.append(copy)
+
+    def send_inputs():
+        for micro in range(2):
+            to = place.worker(micro)
+            launch(remote(seg_in.at[micro], seg_all.at[place.z], move_send.at[1, micro], move_recv.at[1, place.z], to))
+            launch(remote(x_in.at[micro], x_all.at[place.z], move_send.at[0, micro], move_recv.at[0, place.z], to))
 
     def arrival(t, kind):
         ref = (x_all, seg_all)[kind].at[t]
         return remote(ref, ref, move_send.at[kind, 0], move_recv.at[kind, t], place.sibling)
 
-    events = ga.events()
-    for event in events[:A_FIRST]:
-        ga.step(event)
-    gm.begin_seq()
-    for event in events[A_FIRST:]:
-        ga.step(event)
-    for j in range(2):
-        t = place.own_block(j)
-        for kind in range(2):
-            ref = (x_all, seg_all)[kind].at[t]
-            arrival(t, kind).wait_recv()
-            copy = remote(ref, ref, move_send.at[kind, 2 + j], move_recv.at[kind, t], place.sibling)
-            copy.start()
-            sent.append(copy)
-    for micro in range(2):
-        copy = remote(
-            cot_in.at[micro], cot_own.at[place.z // 2], cot_sems.at[0, micro], cot_sems.at[1, place.z // 2],
-            place.worker(micro),
-        )
-        copy.start()
-        sent.append(copy)
-
-    m_events = gm.events()
-    pumped = [0]
-
-    def pump(count):
-        for event in m_events[pumped[0] : pumped[0] + count]:
-            gm.step(event)
-        pumped[0] += count
-
-    pump(PUMP[0])
+    def share_inputs():
+        for j in range(2):
+            t = place.own_block(j)
+            for kind in range(2):
+                ref = (x_all, seg_all)[kind].at[t]
+                arrival(t, kind).wait_recv()
+                launch(remote(ref, ref, move_send.at[kind, 2 + j], move_recv.at[kind, t], place.sibling))
+
+    def send_cotangent():
+        for micro in range(2):
+            remote(
+                cot_in.at[micro], cot_own.at[place.z // 2], cot_sems.at[0, micro], cot_sems.at[1, place.z // 2],
+                place.worker(micro),
+            ).start()
+
+    timed = [(time, (ga, event)) for time, event in ga.events(*A_TIMES)]
+    timed += [(time + (0 if event[2] else M_OWN), (gm, event)) for time, event in gm.events(*M_TIMES)]
+    timed += [
+        (at, (Action(), action))
+        for at, action in (
+            (SEND_X, send_inputs), (SHARE_X, share_inputs), (SEND_COT, send_cotangent),
+            (M_SEQ, gm.begin_seq), (M_BITS, gm.begin_bits),
+        )
+    ]
+    both = Steps(timed)
+    both.until(FORWARD_START)
     own_copies[0].wait()
     ga.finish_sibling()
     unflatten(a_slots, flat, a_rows)
-    pump(PUMP[1])
+    both.until(FORWARD_START + 3)
     for section in range(3):
         load_matrix(
             flat, ATTN_QKV + section * ROW_D + place.core * ROW_HALF, ROW_QKV, ROW_HALF, wqkv.at[section], LANES
@@ -773,7 +820,7 @@
     vec[1:2, :] = load_vector(flat, ATTN_BPROJ, ROW_D)
     bias_query = load_vector(flat, ATTN_BQ + place.core * ROW_HALF, ROW_HALF)
     bias_value = load_vector(flat, ATTN_BV + place.core * ROW_HALF, ROW_HALF)
-    pump(PUMP[2])
+    both.until(FORWARD_START + 7)
     for j in range(2):
         for kind in range(2):
             arrival(place.other_block(j), kind).wait_recv()
@@ -790,28 +837,30 @@
         value = dot_nn(low, wqkv[2]) + bias_value
         for result, across, heads in ((query, qt, qh), (key, kt, kh), (value, vt, vh)):
             across[:, rows] = result.T.astype(bf16)
-            rounded = result.astype(bf16)
-            for h in range(HALF_HEADS):
-                heads[h, rows, :] = rounded[:, h * HD : (h + 1) * HD]
+            split_heads(result.astype(bf16), heads, rows)
         return carry
 
     lax.fori_loop(0, seq_size, project, 0)
+    keep = [
+        pltpu.make_async_copy(src, dst, keep_sems.at[i])
+        for i, (src, dst) in enumerate(
+            [(n1, n1_out), (wqkv, wqkv_out), (qt, qt_out), (kt, kt_out), (qh, qh_out), (kh, kh_out), (vh, vh_out)]
+        )
+    ]
+    for copy in keep:
+        copy.start()
     lse[...] = jnp.zeros_like(lse)
-
-    rest = len(m_events) - pumped[0]
-    per_head = -(-rest // HALF_HEADS)
+    unit = HEAD_FORWARD / (seq_size * (seq_size + 1) // 2)
+    points = [((h, i), unit * (i + 1)) for h in range(HALF_HEADS) for i in range(seq_size)]
+    plan = both.plan(FORWARD_START + 12, points)
 
     def one_head(h, carry):
-        for c in range(HALF_HEADS):
-
-            @pl.when(h == c)
-            def _():
-                pump(per_head)
-
         head_rows = pl.ds(pl.multiple_of(h * HD, HD), HD)
+        pair_rows = pl.ds(pl.multiple_of(h // 2 * LANES, LANES), LANES)
         for i in range(seq_size):
+            handle([plan[c, i] for c in range(HALF_HEADS)], h)
             columns = slice(i * block, (i + 1) * block)
-            query = qt[head_rows, columns]
+            query = qt[pair_rows, columns]
             top = jnp.full((1, block), -jnp.inf, f32)
             for b in range(i + 1):
                 rows = slice(b * block, (b + 1) * block)
@@ -834,6 +883,7 @@
         return carry
 
     lax.fori_loop(0, HALF_HEADS, one_head, 0)
+    both.until(math.inf)
 
     for j in range(2):
         columns = pl.ds(pl.multiple_of(place.other_block(j) * block, block), block)
@@ -850,8 +900,10 @@
         ref = att.at[1 - place.core, j]
         remote(ref, ref, swap_sems.at[0, j], swap_sems.at[1, j], place.sibling).wait_recv()
         ref = cot_own.at[j]
-        remote(ref, ref, cot_sems.at[0, j], cot_sems.at[1, j], place.sibling).wait_recv()
+        remote(ref, ref, cot_sems.at[0, j], cot_sems.at[1, j], place.sibling).wait()
     own_copies[1].wait()
+    for copy in keep:
+        copy.wait()
     gm.finish_sibling()
     for copy in sent:
         copy.wait_send()
@@ -862,8 +914,8 @@
 def mlp_kernel(
     m_rows,
     m_slots, x_own, cot, att, w_proj, vec,
-    out, d_mid, d_att, g_slots, g_proj, g_bias,
-    flat, w_up, w_down, mid, n2, d_n2, total, b_up, gb_up, sem,
+    g_out, out, d_mid, d_att, g_proj, g_bias,
+    g_slots, flat, w_up, w_down, mid, n2, d_n2, total, b_up, gb_up, sem, out_sems,
 ):
     rows_all = x_own.shape[0]
     half = rows_all // 2
@@ -952,21 +1004,49 @@
     store_vector(flat, MLP_BDOWN, down_sum)
     used = MLP_BDOWN + ROW_D
     flat[used:, :] = jnp.zeros((flat.shape[0] - used, LANES), f32)
-    flatten(flat, g_slots, m_rows)
+    group = g_slots.shape[0] // 4
+    flush = []
+    for part in range(4):
+        slots = pl.ds(part * group, group)
+
+        def body(s, carry, part=part):
+            s = s + part * group
+            g_slots[s, :m_rows, :] = flat[pl.ds(s * m_rows, m_rows), :].astype(bf16)
+            return carry
+
+        lax.fori_loop(0, group, body, 0)
+        copy = pltpu.make_async_copy(g_slots.at[slots], g_out.at[slots], out_sems.at[part])
+        copy.start()
+        flush.append(copy)
+    for copy in flush:
+        copy.wait()
 
 
 def backward_kernel(
     dp_size, seq_size, a_rows,
-    out_own, m_grads, d_mid, d_att, g_proj, g_bias, x_own, n1, wqkv, vec, qt, kt, qh, kh, vh, seg_all, lse,
+    out_own, m_grads, g_proj, n1_in, wqkv_in, qt_in, kt_in, qh_in, kh_in, vh_in, d_mid_in, x_own_in,
+    d_att, g_bias, vec, seg_all, lse,
     out_back, grad_back, a_out, m_out,
-    flat, d_all, dt, dh, seg_col, p_piece, d_piece, dk, dv, dqt, dm, d_n1, d_n1_in, g_out, core_out,
-    move_sems, swap_sems, norm_sems, proj_sem, *refs,
+    n1, wqkv, qt, kt, qh, kh, vh, d_mid, x_own,
+    flat, d_all, dt, dh, seg_col, p_piece, d_piece, dk, dv, dqt, dm, d_n1, d_n1_in,
+    move_sems, swap_sems, norm_sems, proj_sem, load_sems, *refs,
 ):
     place = Place(seq_size)
-    block = x_own.shape[1]
+    block = x_own_in.shape[1]
     count = len(refs) // 2
     sm = make_scatter(dp_size, seq_size, m_out, refs[:count])
     sa = make_scatter(dp_size, seq_size, a_out, refs[count:])
+    loads = [
+        pltpu.make_async_copy(src, dst, load_sems.at[i])
+        for i, (src, dst) in enumerate(
+            [
+                (qt_in, qt), (kt_in, kt), (qh_in, qh), (kh_in, kh), (vh_in, vh),
+                (n1_in, n1), (wqkv_in, wqkv), (d_mid_in, d_mid), (x_own_in, x_own),
+            ]
+        )
+    ]
+    for copy in loads:
+        copy.start()
     greet(place.line_peers() + [(place.dp ^ (1 << b), place.z) for b in sm.bits])
     sent = []
     for j in range(2):
@@ -997,40 +1077,35 @@
         rows = pl.ds(pl.multiple_of(t * block, block), block)
         piece = d_all[t]
         dt[:, rows] = piece.astype(f32).T.astype(bf16)
-        for h in range(HALF_HEADS):
-            dh[h, rows, :] = piece[:, h * HD : (h + 1) * HD]
+        split_heads(piece, dh, rows)
         return carry
 
     lax.fori_loop(0, seq_size, spread, 0)
 
-    m_events = sm.events()
-    first = len(m_events) - len([e for e in m_events if e[0] != "c"])
-    pumped = [0]
-
-    def pump(count):
-        for event in m_events[pumped[0] : pumped[0] + count]:
-            sm.step(event)
-        pumped[0] += count
-
-    pump(first)
-    per_head = -(-(len(m_events) - first) // HALF_HEADS)
-
-    def one_pair(pair, carry):
-        for side in range(2):
-            for c in range(HALF_HEADS // 2):
-
-                @pl.when(pair == c)
-                def _():
-                    begin = first + (2 * c + side) * per_head
-                    for event in m_events[begin : begin + per_head]:
-                        sm.step(event)
-
-            h = 2 * pair + side
-            head_rows = pl.ds(pl.multiple_of(h * HD, HD), HD)
-            for i in range(seq_size):
-                columns = slice(i * block, (i + 1) * block)
-                query = qt[head_rows, columns]
-                d_query = dt[head_rows, columns]
+    steps = Steps([(time, (sm, event)) for time, event in sm.events()])
+    steps.until(BACKWARD_START)
+    unit = HEAD_BACKWARD / (seq_size * (seq_size + 1) // 2)
+    points = [
+        ((i, side, pair), unit * (i + 1))
+        for i in reversed(range(seq_size))
+        for pair in range(HALF_HEADS // 2)
+        for side in range(2)
+    ]
+    plan = steps.plan(BACKWARD_START, points)
+    for copy in loads[:5]:
+        copy.wait()
+
+    def query_block(i):
+        columns = slice(i * block, (i + 1) * block)
+
+        def one_pair(pair, carry):
+            pair_rows = pl.ds(pl.multiple_of(pair * LANES, LANES), LANES)
+            for side in range(2):
+                handle([plan[i, side, turn] for turn in range(HALF_HEADS // 2)], pair)
+                h = 2 * pair + side
+                head_rows = pl.ds(pl.multiple_of(h * HD, HD), HD)
+                query = qt[pair_rows, columns]
+                d_query = dt[pair_rows, columns]
                 level = lse[pl.ds(h, 1), columns]
                 delta = jnp.zeros((1, block), f32)
                 for b in range(i + 1):
@@ -1049,70 +1124,74 @@
                     d_scores = (probs * (d_piece[rows, :] - delta)).astype(bf16)
                     key_part = dot_nn(d_scores, qh[h, columns, :])
                     value_part = dot_nn(probs.astype(bf16), dh[h, columns, :])
-                    if b == i:
-                        dk[side, rows, :] = key_part
-                        dv[side, rows, :] = value_part
+                    if i == seq_size - 1 and side == 0:
+                        dk[pair, rows, :] = key_part
+                        dv[pair, rows, :] = value_part
                     else:
-                        dk[side, rows, :] += key_part
-                        dv[side, rows, :] += value_part
+                        dk[pair, rows, :] += key_part
+                        dv[pair, rows, :] += value_part
                     result = result + dot_nn(kt[head_rows, rows], d_scores)
                 dqt[head_rows, columns] = result * (1.0 / math.sqrt(HD))
-        lanes = pl.ds(pl.multiple_of(pair * LANES, LANES), LANES)
+            return carry
+
+        lax.fori_loop(0, HALF_HEADS // 2, one_pair, 0)
+        dm[0, columns, :] = dqt[:, columns].T.astype(bf16)
         for section, part in ((1, dk), (2, dv)):
-            dm[section, :, lanes] = jnp.concatenate([part[0], part[1]], axis=1).astype(bf16)
-        return carry
-
-    lax.fori_loop(0, HALF_HEADS // 2, one_pair, 0)
-    pumped[0] = len(m_events)
-
-    query_sum = jnp.zeros((1, HALF_COLS), f32)
-    value_sum = jnp.zeros((1, HALF_COLS), f32)
-    for t in range(seq_size):
-        rows = slice(t * block, (t + 1) * block)
-        low = dqt[:, rows].T.astype(bf16)
-        dm[0, rows, :] = low
-        query_sum += jnp.sum(low.astype(f32), axis=0, keepdims=True)
-        value_sum += jnp.sum(dm[2, rows, :].astype(f32), axis=0, keepdims=True)
+            for pair in range(HALF_HEADS // 2):
+                dm[section, columns, pair * LANES : (pair + 1) * LANES] = part[pair, columns, :].astype(bf16)
 
     def to_norm(t):
         rows = pl.ds(pl.multiple_of(t * block, block), block)
         return dot_nt(dm[0, rows, :], wqkv[0]) + dot_nt(dm[1, rows, :], wqkv[1]) + dot_nt(dm[2, rows, :], wqkv[2])
 
-    for j in range(2):
+    def share_norm(j):
         d_n1[j] = to_norm(place.other_block(j))
         copy = remote(d_n1.at[j], d_n1_in.at[j], norm_sems.at[0, j], norm_sems.at[1, j], place.sibling)
         copy.start()
         sent.append(copy)
+        d_n1[2] = to_norm(place.own_block(j))
+
+    def finish_input(j):
+        ref = d_n1_in.at[j]
+        remote(ref, ref, norm_sems.at[0, j], norm_sems.at[1, j], place.sibling).wait_recv()
+        grad = d_n1[2] + d_n1_in[j]
+        normal, scale = norm_parts(x_own[j].astype(f32))
+        x_own[j] = (d_mid[j * block : (j + 1) * block, :] + norm_back(normal, scale, grad, gain)).astype(bf16)
+        to, micro = place.home(j)
+        copy = remote(x_own.at[j], grad_back.at[micro], move_sems.at[2, j], move_sems.at[3, micro], to)
+        copy.start()
+        sent.append(copy)
+        return jnp.sum(grad * normal, axis=0, keepdims=True), jnp.sum(grad, axis=0, keepdims=True)
+
+    gain = vec[0:1, :]
+    query_block(3)
+    query_block(2)
+    for copy in loads[5:]:
+        copy.wait()
+    share_norm(1)
+    query_block(1)
+    gain_sum, shift_sum = finish_input(1)
+    query_block(0)
+    share_norm(0)
+    now = BACKWARD_START + HALF_HEADS * HEAD_BACKWARD
+    steps.until(now)
     proj_copy.wait()
     for section in range(3):
         part = dot_tn(n1[...], dm[section])
         for j in range(ROW_HALF):
             start = ATTN_QKV + section * ROW_D + place.core * ROW_HALF + j
             flat[pl.ds(start, D, stride=ROW_QKV), :] = part[:, j * LANES : (j + 1) * LANES]
-    store_vector(flat, ATTN_BQ + place.core * ROW_HALF, query_sum)
-    store_vector(flat, ATTN_BV + place.core * ROW_HALF, value_sum)
+    steps.until(now + 5)
+    more_gain, more_shift = finish_input(0)
+    store_vector(flat, 0, gain_sum + more_gain)
+    store_vector(flat, ROW_D, shift_sum + more_shift)
+    for section, start in ((0, ATTN_BQ), (2, ATTN_BV)):
+        total = jnp.sum(dm[section].astype(f32), axis=0, keepdims=True)
+        store_vector(flat, start + place.core * ROW_HALF, total)
     store_vector(flat, ATTN_BPROJ, g_bias[...])
-    gain = vec[0:1, :]
-    gain_sum = jnp.zeros((1, D), f32)
-    shift_sum = jnp.zeros((1, D), f32)
-    for j in range(2):
-        grad = to_norm(place.own_block(j))
-        ref = d_n1_in.at[j]
-        remote(ref, ref, norm_sems.at[0, j], norm_sems.at[1, j], place.sibling).wait_recv()
-        grad = grad + d_n1_in[j]
-        normal, scale = norm_parts(x_own[j].astype(f32))
-        gain_sum += jnp.sum(grad * normal, axis=0, keepdims=True)
-        shift_sum += jnp.sum(grad, axis=0, keepdims=True)
-        g_out[j] = (d_mid[j * block : (j + 1) * block, :] + norm_back(normal, scale, grad, gain)).astype(bf16)
-    store_vector(flat, 0, gain_sum)
-    store_vector(flat, ROW_D, shift_sum)
-    sa.begin_flat(flat, a_rows, core_out)
-    for j in range(2):
-        to, micro = place.home(j)
-        copy = remote(g_out.at[j], grad_back.at[micro], move_sems.at[2, j], move_sems.at[3, micro], to)
-        copy.start()
-        sent.append(copy)
-    for event in sa.events():
+    sa.begin_flat(flat, a_rows, sm.core_in)
+    steps.until(math.inf)
+    for _, event in sa.events():
         sa.step(event)
     sm.finish()
     sa.finish()
@@ -1126,7 +1205,7 @@
 
 
 class Scatter:
-    def __init__(self, dp_size, seq_size, out, acc, core_in, level_in, seq_in, load_sems, send_sems, recv_sems):
+    def __init__(self, dp_size, seq_size, out, acc, core_in, level_in, seq_in, load_sems, send_sems, recv_sems, seq_sems):
         self.n = seq_size
         self.bits = list(range(1, dp_size.bit_length() - 1))
         self.masks = [m << 1 for m in range(1 << len(self.bits))]
@@ -1139,7 +1218,7 @@
         half = rows // 32 * 16
         self.parts = [(0, half), (half, rows - half)]
         self.orders = [self.bits[::-1], self.bits]
-        self.load_sems, self.send_sems, self.recv_sems = load_sems, send_sems, recv_sems
+        self.load_sems, self.send_sems, self.recv_sems, self.seq_sems = load_sems, send_sems, recv_sems, seq_sems
         self.started = []
         self.indices = {}
 
@@ -1147,17 +1226,18 @@
         return self.indices.setdefault(key, len(self.indices))
 
     def slot(self, mask, k):
-        return (self.dp ^ mask) * self.n + lax.rem(self.z + k, self.n)
+        return (self.dp ^ mask) * self.n + nearest(self.z, self.n, k)
 
     def send(self, src, dst, to, key, part=None):
-        remote(src, dst, self.send_sems.at[len(self.started)], self.recv_sems.at[self.index(*key)], to).start()
+        sem = self.recv_sems.at[self.index(*key)] if isinstance(key, tuple) else key
+        remote(src, dst, self.send_sems.at[len(self.started)], sem, to).start()
         self.started.append(part)
 
     def wait(self, ref, key):
         remote(ref, ref, self.send_sems.at[0], self.recv_sems.at[self.index(*key)], (self.dp, self.z)).wait_recv()
 
     def turn(self):
-        return list(range(1, self.n)) + [0]
+        return list(range(self.n))[::-1]
 
     def begin(self, slots):
         for k in self.turn():
@@ -1173,13 +1253,14 @@
                 )
 
     def begin_flat(self, flat, rows, core_out):
+        whole = self.acc.shape[2]
         for k in self.turn():
             for mask in self.masks[::-1]:
                 i = self.masks.index(mask)
                 for target, which in ((core_out, mask ^ 1), (self.acc, mask)):
                     target[i, k, :rows, :] = flat[pl.ds(self.slot(which, k) * rows, rows), :].astype(bf16)
-                    target[i, k, rows:, :] = jnp.zeros((target.shape[2] - rows, LANES), bf16)
-                self.send(core_out.at[i, k], self.core_in.at[i, k], (self.dp ^ 1, self.z), ("c", i, k))
+                    target[i, k, rows:whole, :] = jnp.zeros((whole - rows, LANES), bf16)
+                self.send(core_out.at[i, k, pl.ds(0, whole)], self.core_in.at[i, k], (self.dp ^ 1, self.z), ("c", i, k))
 
     def cell(self, part, level, mask):
         free = [b for b in self.bits if b not in self.orders[part][: level + 1]]
@@ -1191,9 +1272,6 @@
         start, size = self.parts[part]
         src = self.acc.at[i, k, pl.ds(start, size)]
         if level == len(order):
-            if k:
-                to = (self.dp, lax.rem(self.z + k, self.n))
-                self.send(src, self.seq_in[part].at[k - 1], to, ("z", part, k), part)
             return
         bit = 1 << order[level]
         if mask & bit:
@@ -1201,19 +1279,23 @@
             dst = self.level_in[part][level].at[self.cell(part, level, rest), k]
             self.send(src, dst, (self.dp ^ bit, self.z), ("l", part, level, rest, k), part)
 
-    def events(self):
+    def events(self, begin=6.0, gap=9.6, level_gap=(9.0, 19.0), seq_gap=0.5):
         out = []
         for turn, k in enumerate(self.turn()):
+            at = begin + max(0, turn - 1) * gap
             for mask in self.masks[::-1]:
-                out.append((turn * 0.1, ("c", mask, k)))
+                out.append((at, ("c", mask, k)))
+            at = begin + turn * gap
             for level in range(len(self.bits)):
                 for part in (0, 1):
                     past = self.orders[part][: level + 1]
                     for mask in self.masks[::-1]:
                         if not any(mask >> b & 1 for b in past):
-                            out.append((turn + (level + 1) * 1.0 + 0.5, ("l", part, level, mask, k)))
-        out.sort(key=lambda e: e[0])
-        return [e[1] for e in out]
+                            out.append((at + level_gap[min(level, 1)], ("l", part, level, mask, k)))
+            if k:
+                for part in (0, 1):
+                    out.append((at + level_gap[min(len(self.bits) - 1, 1)] + seq_gap, ("z", part, k)))
+        return sorted(out, key=lambda e: e[0])
 
     def step(self, event):
         if event[0] == "c":
@@ -1226,6 +1308,10 @@
             for part in (0, 1):
                 self.pass_on(part, 0, mask, k)
             return
+        if event[0] == "z":
+            _, part, k = event
+            self.along(part, k)
+            return
         _, part, level, mask, k = event
         i = self.masks.index(mask)
         start, size = self.parts[part]
@@ -1235,16 +1321,41 @@
         self.acc[i, k, rows] = (self.acc[i, k, rows].astype(f32) + cell[...].astype(f32)).astype(bf16)
         self.pass_on(part, level + 1, mask, k)
 
+    def from_side(self, part, place, side):
+        index = place if side == 0 else self.n
+        ref = self.seq_in[part].at[index]
+        remote(ref, ref, self.send_sems.at[0], self.seq_sems.at[part, index], (self.dp, self.z)).wait_recv()
+        return self.seq_in[part][index].astype(f32)
+
+    def along(self, part, k):
+        place = nearest(self.z, self.n, k)
+        up = place > self.z
+        start, size = self.parts[part]
+        rows = pl.ds(start, size)
+
+        @pl.when((up & (self.z > 0)) | (jnp.logical_not(up) & (self.z < self.n - 1)))
+        def _():
+            self.acc[0, k, rows] = (self.acc[0, k, rows].astype(f32) + self.from_side(part, place, 0)).astype(bf16)
+
+        to = jnp.where(up, self.z + 1, self.z - 1)
+        index = jnp.where((to == place) & jnp.logical_not(up), self.n, place)
+        self.send(
+            self.acc.at[0, k, rows], self.seq_in[part].at[index], (self.dp, to), self.seq_sems.at[part, index], part
+        )
+
     def finish(self):
         used = self.out.shape[0]
         for part in (0, 1):
             start, size = self.parts[part]
-            size = min(size, used - start)
-            total = self.acc[0, 0, pl.ds(start, size)].astype(f32)
-            for k in range(1, self.n):
-                self.wait(self.seq_in[part].at[k - 1], ("z", part, k))
-                total = total + self.seq_in[part][k - 1, :size].astype(f32)
-            self.out[start : start + size, :] = total
+            kept = min(size, used - start)
+            rows = slice(start, start + kept)
+            self.out[rows, :] = self.acc[0, 0, pl.ds(start, kept)].astype(f32)
+            for side, there in ((0, self.z > 0), (1, self.z < self.n - 1)):
+
+                @pl.when(there)
+                def _():
+                    self.out[rows, :] += self.from_side(part, self.z, side)[:kept]
+
         for index, part in enumerate(self.started):
             start, size = (0, self.acc.shape[2]) if part is None else self.parts[part]
             ref = self.acc.at[0, 0, pl.ds(start, size)]
@@ -1264,12 +1375,13 @@
         for level in range(bits):
             shapes.append(pltpu.VMEM((masks >> (level + 1), seq_size, size, LANES), bf16))
     for size in sizes:
-        shapes.append(pltpu.VMEM((seq_size - 1, size, LANES), bf16))
+        shapes.append(pltpu.VMEM((seq_size + 1, size, LANES), bf16))
     count = masks * seq_size + 2 * (masks - 1) * seq_size + 2 * (seq_size - 1)
     shapes += [
         pltpu.SemaphoreType.DMA((masks, seq_size)),
         pltpu.SemaphoreType.DMA((count,)),
         pltpu.SemaphoreType.DMA((count,)),
+        pltpu.SemaphoreType.DMA((2, seq_size + 1)),
     ]
     return shapes
 
@@ -1302,21 +1414,25 @@
     send, recv = gather_counts(dp_size, n)
     dma = pltpu.SemaphoreType.DMA
     across = shape_of((HALF_COLS, length), bf16)
-    heads = shape_of((HALF_HEADS, length, HD), bf16)
+    heads = shape_of((HALF_HEADS, length, LANES), bf16)
     own = shape_of((2, block, D), bf16)
+    kept = [
+        shape_of((length, D), bf16), shape_of((3, D, HALF_COLS), bf16), across, across, heads, heads, heads,
+    ]
     (
-        m_slots, cot_own, x_own, n1, wqkv, w_proj, vec, qt, kt, qh, kh, vh, seg_all, lse, att,
+        m_slots, cot_own, n1, wqkv, qt, kt, qh, kh, vh, x_own, w_proj, vec, seg_all, lse, att,
     ) = pl.pallas_call(
         functools.partial(forward_kernel, dp_size, n, a_rows),
-        out_shape=[
-            shape_of((devices, m_pad, LANES), bf16), own, own, shape_of((length, D), bf16),
-            shape_of((3, D, HALF_COLS), bf16), shape_of((D, D), bf16), shape_of((8, D), f32),
-            across, across, heads, heads, heads,
+        out_shape=[shape_of((devices, m_pad, LANES), bf16), own]
+        + kept
+        + [
+            own, shape_of((D, D), bf16), shape_of((8, D), f32),
             shape_of((n, 8, LANES), jnp.int32), shape_of((8, length), f32), shape_of((2, 2, block, HALF_COLS), bf16),
         ],
         in_specs=[ANY] * 5,
-        out_specs=[ANY] * 2 + [LOCAL] * 13,
-        scratch_shapes=[
+        out_specs=[ANY] * 9 + [LOCAL] * 6,
+        scratch_shapes=[pltpu.VMEM(like.shape, like.dtype) for like in kept]
+        + [
             pltpu.VMEM((devices, a_pad, LANES), bf16),
             pltpu.VMEM((devices * a_rows, LANES), f32),
             pltpu.VMEM((n, block, D), bf16),
@@ -1326,59 +1442,64 @@
             pltpu.VMEM((HALF_COLS, length), f32),
             pltpu.VMEM((2, block, HALF_COLS), bf16),
             dma((send,)), dma((recv,)), dma((send,)), dma((recv,)), dma((2,)),
-            dma((2, 4)), dma((2, n)), dma((2, 2)), dma((2, 2)),
+            dma((2, 4)), dma((2, n)), dma((2, 2)), dma((2, 2)), dma((len(kept),)),
         ],
         compiler_params=pltpu.CompilerParams(collective_id=0, has_side_effects=True, vmem_limit_bytes=VMEM_LIMIT),
     )(inputs[:, 0], seg_rows, cotangent[:, 0], a_own, m_own)
 
     tokens = 2 * block
-    out_own, d_mid, d_att, m_grads, g_proj, g_bias = pl.pallas_call(
+    m_grads, out_own, d_mid, d_att, g_proj, g_bias = pl.pallas_call(
         functools.partial(mlp_kernel, m_rows),
         out_shape=[
+            shape_of((devices, m_pad, LANES), bf16),
             shape_of((tokens, D), bf16), shape_of((tokens, D), f32), shape_of((2, tokens, HALF_COLS), bf16),
-            shape_of((devices, m_pad, LANES), bf16), shape_of((D * ROW_D, LANES), f32), shape_of((1, D), f32),
+            shape_of((D * ROW_D, LANES), f32), shape_of((1, D), f32),
         ],
         in_specs=[ANY] + [LOCAL] * 5,
-        out_specs=[LOCAL] * 6,
+        out_specs=[ANY] + [LOCAL] * 5,
         scratch_shapes=[
+            pltpu.VMEM((devices, m_pad, LANES), bf16),
             pltpu.VMEM((devices * m_rows, LANES), f32),
             pltpu.VMEM((D, FF), bf16), pltpu.VMEM((FF, D), bf16),
             pltpu.VMEM((tokens, D), f32), pltpu.VMEM((tokens, D), bf16),
             pltpu.VMEM((tokens, D), f32), pltpu.VMEM((tokens, D), f32),
             pltpu.VMEM((1, FF), f32), pltpu.VMEM((1, FF), f32),
-            dma(()),
+            dma(()), dma((4,)),
         ],
         compiler_params=pltpu.CompilerParams(vmem_limit_bytes=VMEM_LIMIT),
     )(m_slots, x_own.reshape(tokens, D), cot_own.reshape(tokens, D), att.reshape(2, tokens, HALF_COLS), w_proj, vec)
 
-    masks = dp_size // 2
     out_back, grad_back, a_sum, m_sum = pl.pallas_call(
         functools.partial(backward_kernel, dp_size, n, a_rows),
         out_shape=[own, own, shape_of((a_rows, LANES), f32), shape_of((m_rows, LANES), f32)],
-        in_specs=[ANY] * 2 + [LOCAL] * 2 + [ANY] + [LOCAL] * 12,
+        in_specs=[ANY] * 12 + [LOCAL] * 5,
         out_specs=[ANY] * 2 + [LOCAL] * 2,
-        scratch_shapes=[
+        scratch_shapes=[pltpu.VMEM(like.shape, like.dtype) for like in kept]
+        + [
+            pltpu.VMEM((tokens, D), f32),
+            pltpu.VMEM((2, block, D), bf16),
             pltpu.VMEM((devices * a_rows, LANES), f32),
             pltpu.VMEM((n, block, HALF_COLS), bf16),
             pltpu.VMEM((HALF_COLS, length), bf16),
-            pltpu.VMEM((HALF_HEADS, length, HD), bf16),
+            pltpu.VMEM((HALF_HEADS, length, LANES), bf16),
             pltpu.VMEM((length, LANES), jnp.int32),
             pltpu.VMEM((length, block), f32),
             pltpu.VMEM((length, block), f32),
-            pltpu.VMEM((2, length, HD), f32),
-            pltpu.VMEM((2, length, HD), f32),
+            pltpu.VMEM((HALF_HEADS // 2, length, LANES), f32),
+            pltpu.VMEM((HALF_HEADS // 2, length, LANES), f32),
             pltpu.VMEM((HALF_COLS, length), f32),
             pltpu.VMEM((3, length, HALF_COLS), bf16),
+            pltpu.VMEM((3, block, D), f32),
             pltpu.VMEM((2, block, D), f32),
-            pltpu.VMEM((2, block, D), f32),
-            pltpu.VMEM((2, block, D), bf16),
-            pltpu.VMEM((masks, n, a_pad, LANES), bf16),
-            dma((4, 2)), dma((2, 2)), dma((2, 2)), dma(()),
+            dma((4, 2)), dma((2, 2)), dma((2, 2)), dma(()), dma((9,)),
         ]
         + scatter_scratch(dp_size, n, m_pad)
         + scatter_scratch(dp_size, n, a_pad),
         compiler_params=pltpu.CompilerParams(collective_id=1, has_side_effects=True, vmem_limit_bytes=VMEM_LIMIT),
-    )(out_own, m_grads, d_mid, d_att, g_proj, g_bias, x_own, n1, wqkv, vec, qt, kt, qh, kh, vh, seg_all, lse)
+    )(
+        out_own, m_grads, g_proj, n1, wqkv, qt, kt, qh, kh, vh, d_mid, x_own,
+        d_att, g_bias, vec, seg_all, lse,
+    )
     return (
         out_back[:, None],
         grad_back.astype(f32)[:, None],

time: 252 us -> 220 us (0.87)
  Pallas kernels: 242 us -> 209 us
    pallas_call x1, Pallas kernels: 109 us -> 86.4 us  [per_chip_sequence(): pl.pallas_call(functools.partial(backward_kernel, dp_size, n, a_rows), ou...]
    pallas_call x1, Pallas kernels: 95.8 us -> 86.4 us  [per_chip_sequence(): pl.pallas_call(functools.partial(forward_kernel, dp_size, n, a_rows), out...]
where the time goes in v2:
time: 220 us; the launch traced here: 219 us
  Pallas kernels  209 us (95%)
  local copies, waits for them, and re-layouts  7.05 us (3%)
  other arithmetic  2.47 us (1%)
    pallas_call x1, Pallas kernels, per_chip_sequence(): pl.pallas_call(functools.partial(backward_kernel, dp_size, n, a_rows), ou...  86.4 us
    pallas_call x1, Pallas kernels, per_chip_sequence(): pl.pallas_call(functools.partial(forward_kernel, dp_size, n, a_rows), out...  86.4 us
    pallas_call x1, Pallas kernels, per_chip_sequence(): pl.pallas_call(functools.partial(mlp_kernel, m_rows), out_shape=[shape_of...  36.4 us

profile of v2, /device:TPU:0, one launch (start us, length us, event | category | flops | bytes accessed | tf_op | source)
XLA Modules:
  0.0 219.5 jit_solution(8387181083702976986)
XLA Ops:
  0.6 1.3 pad.12.seg_in
  1.9 1.6 pad.13.a_own
  3.5 1.7 pad.14.m_own
  5.2 86.4 %shard_map.84 = (bf16[32,1168,128]{2,1,0:T(8,128)(2,1)}, bf16[2,256,768]{2,1,0:T(8,128)(2,1)}, bf16[1024,768]{1,0:T(8,128)(2,1)}, bf16[3,768,384]{2,1,0:T(8,128)...) custom-call(bf16[2,256,768]{2,1,0:T(8,128)(2,1)} %bitcast.23, ...), custom_call_target="tpu_custom_call" | custom-call | tf_op jit(solution)/shard_map/pallas_call | solution.py:1424
  91.6 36.4 %shard_map.85 = (bf16[32,1168,128]{2,1,0:T(8,128)(2,1)}, bf16[512,768]{1,0:T(8,128)(2,1)}, f32[512,768]{1,0:T(8,128)}, bf16[2,512,384]{2,1,0:T(8,128)(2,1)}, f32[4608,128]{1,0:T(8,128)}, /*index=5*/f32[1,768]{1,0:T(1,128)}) custom-call(bf16[32,1168,128]{2,1,0:T(8,128)(2,1)} %get-tuple-element.29.m_slots, bf16[512,768]{1,0:T(8,128)(2,1)} %bitcast.19, ...), custom_call_target="tpu_custom_call" | custom-call | tf_op jit(solution)/shard_map/pallas_call | solution.py:1451
  128.1 86.4 %shard_map.86 = (bf16[2,256,768]{2,1,0:T(8,128)(2,1)}, bf16[2,256,768]{2,1,0:T(8,128)(2,1)}, f32[577,128]{1,0:T(8,128)}, f32[1154,128]{1,0:T(8,128)}) custom-call(bf16[512,768]{1,0:T(8,128)(2,1)} %get-tuple-element.35.out_own, bf16[32,1168,128]{2,1,0:T(8,128)(2,1)} %get-tuple-element.36.m_grads, f32[4608,128]{1,0:T(8,128)} %get-tuple-element.37.g_proj, ...), custom_call_target="tpu_custom_call" | custom-call | tf_op jit(solution)/shard_map/pallas_call | solution.py:1472
  214.5 0.0 copy-start
  214.5 0.0 copy-start.2
  214.5 2.5 %bitcast_convert_fusion = f32[2,1,256,768]{3,2,1,0:T(8,128)} fusion(bf16[2,256,768]{2,1,0:T(8,128)(2,1)} %get-tuple-element.51), kind=kLoop, calls=%fused_computation | loop fusion | flops 393216 | bytes 2359296
  217.0 0.0 copy-done
  217.0 0.0 copy-start.1
  217.0 0.9 copy.14
  217.9 0.0 copy-done.2
  217.9 0.7 copy.15
  218.6 0.0 copy-done.1
  218.6 0.9 copy.16
Async XLA Ops:
  214.5 2.5 %copy-start = (bf16[2,256,768]{2,1,0:T(8,128)(2,1)S(1)}, bf16[2,256,768]{2,1,0:T(8,128)(2,1)}, u32[]{:S(2)}) copy-start(bf16[2,256,768]{2,1,0:T(8,128)(2,1)} %get-tuple-element.50) | copy-start | bytes 2359300
  214.5 3.4 %copy-start.2 = (f32[577,128]{1,0:T(8,128)S(1)}, f32[577,128]{1,0:T(8,128)}, u32[]{:S(2)}) copy-start(f32[577,128]{1,0:T(8,128)} %get-tuple-element.52) | copy-start | bytes 886276
  217.0 1.6 copy-start.1

commit v3 on v2

--- a/solution.py
+++ b/solution.py
@@ -548,6 +548,8 @@
 ROW_QKV = 3 * ROW_D
 ROW_HALF = HALF_COLS // LANES
 FF_STEP = 512
+HEAD = 16
+MARGIN = 32
 VMEM_LIMIT = 63 * 2**20
 
 A_TIMES = (3.0, 6.0, 4.0)
@@ -555,12 +557,14 @@
 M_OWN = 8.0
 M_SEQ = 0.0
 M_BITS = 4.0
-SEND_X = 6.0
+SEND_X = (6.0, 6.0, 6.0, 6.0)
 SHARE_X = 28.0
-SEND_COT = 45.0
+SEND_COT = (45.0, 45.0)
 FORWARD_START = 30.0
 HEAD_FORWARD = 3.3
+BACKWARD_FIRST = 6.5
 BACKWARD_START = 8.0
+A_BACK = (6.0, 5.0, (5.0, 10.0), 1.0)
 HEAD_BACKWARD = 5.8
 
 ATTN_QKV = 2 * ROW_D
@@ -674,32 +678,139 @@
     pl.semaphore_wait(barrier, len(peers))
 
 
-def unflatten(slots, flat, rows):
+class Layout:
+    def __init__(self, rows, devices, matrices, tail):
+        self.rows, self.tail = rows, tail
+        self.whole = sum(count * columns for _, count, columns in matrices) // devices
+        self.slot_rows = self.whole + HEAD + tail
+        self.regions = []
+        first = 0
+        for start, count, columns in matrices:
+            shards = count * columns // self.whole
+            self.regions.append((start, columns, self.whole // columns, first, shards))
+            first += shards
+        assert first == devices
+        for s in range(devices):
+            start, columns, height, first, _ = self.region(s)
+            shift = start + self.whole * (s - first) - rows * s
+            assert shift <= HEAD and shift + self.whole >= rows - tail and shift >= -MARGIN
+
+    def region(self, s):
+        return [r for r in self.regions if r[3] <= s < r[3] + r[4]][0]
+
+    def shift(self, s, region):
+        start, _, _, first, _ = region
+        return start - self.whole * first + (self.whole - self.rows) * s
+
+    def piece(self, row):
+        s, q = row // self.rows, row % self.rows
+        if q < HEAD:
+            return s, self.whole + q
+        assert q >= self.rows - self.tail
+        return s, self.whole + HEAD + q - (self.rows - self.tail)
+
+    def lacking(self, region):
+        out = []
+        start, columns, height, first, shards = region
+        for s in range(first, first + shards):
+            shift = self.shift(s, region)
+            for q in range(self.whole):
+                if not 0 <= shift + q < self.rows:
+                    out.append(((s - first) * height + q // columns, q % columns) + self.piece(s * self.rows + shift + q))
+        return out
+
+    def beyond(self):
+        out = []
+        for s in range(sum(r[4] for r in self.regions)):
+            shift = self.shift(s, self.region(s))
+            for q in list(range(max(shift, 0))) + list(range(shift + self.whole, self.rows)):
+                row = s * self.rows + q
+                for start, columns, height, first, shards in self.regions:
+                    if start <= row < start + shards * self.whole:
+                        i, j = (row - start) // columns, (row - start) % columns
+                        out.append(self.piece(row) + (first + i // height, j * height + i % height))
+        return out
+
+    def branch(self, s, action):
+        for region in self.regions:
+            pl.when((s >= region[3]) & (s < region[3] + region[4]))(functools.partial(action, region))
+
+    def pack(self, own, wide, slot, s):
+        edge = jnp.zeros((MARGIN, LANES), f32)
+        wide[:MARGIN, :] = edge
+        wide[MARGIN + own.shape[0] :, :] = edge
+        wide[MARGIN : MARGIN + own.shape[0], :] = own[...].astype(f32)
+
+        def fill(region):
+            _, columns, height, _, _ = region
+            for j in range(columns):
+                piece = wide[pl.ds(MARGIN + self.shift(s, region) + j, height, stride=columns), :]
+                slot[j * height : (j + 1) * height, :] = piece.astype(bf16)
+
+        self.branch(s, fill)
+        slot[self.whole : self.whole + HEAD, :] = own[:HEAD, :]
+        last = wide[MARGIN + self.rows - self.tail : MARGIN + self.rows, :]
+        slot[self.whole + HEAD :, :] = last.astype(bf16)
+
+    def unpack(self, slot, wide, out, s):
+        def fill(region):
+            _, columns, height, _, _ = region
+            shift = self.shift(s, region)
+            for j in range(columns):
+                wide[pl.ds(MARGIN + shift + j, height, stride=columns), :] = slot[j * height : (j + 1) * height, :]
+            out[...] = wide[MARGIN : MARGIN + self.rows, :]
+            row = lax.broadcasted_iota(jnp.int32, (HEAD, LANES), 0)
+            out[:HEAD, :] = jnp.where(row < shift, slot[self.whole : self.whole + HEAD, :], out[:HEAD, :])
+            begin = self.rows - self.tail
+            row = lax.broadcasted_iota(jnp.int32, (self.tail, LANES), 0) + begin
+            last = slot[self.whole + HEAD :, :]
+            out[begin:, :] = jnp.where(row >= shift + self.whole, last, out[begin:, :])
+
+        self.branch(s, fill)
+
+    def vector(self, slots, row, blocks):
+        parts = []
+        for j in range(blocks):
+            s, q = self.piece(row + j)
+            aligned = q // 16 * 16
+            parts.append(slots[s, aligned : aligned + 16, :].astype(f32)[q - aligned : q - aligned + 1, :])
+        return jnp.concatenate(parts, axis=1)
+
+    def put_vectors(self, slots, entries):
+        areas = {}
+        for row, value in entries:
+            for j in range(value.shape[1] // LANES):
+                s, at = self.piece(row + j)
+                begin = self.whole if at < self.whole + HEAD else self.whole + HEAD
+                areas.setdefault((s, begin), {})[at - begin] = value[:, j * LANES : (j + 1) * LANES]
+        zero = jnp.zeros((1, LANES), f32)
+        for (s, begin), rows in areas.items():
+            size = HEAD if begin == self.whole else self.tail
+            tile = jnp.concatenate([rows.get(n, zero) for n in range(size)], axis=0)
+            slots[s, begin : begin + size, :] = tile.astype(bf16)
+
+
+def load_matrix(slots, layout, which, base, out):
+    region = layout.regions[which]
+    _, columns, height, first, shards = region
+
     def body(s, carry):
-        flat[pl.ds(s * rows, rows), :] = slots[s, :rows, :].astype(f32)
+        rows = pl.ds(pl.multiple_of(s * height, height), height)
+        for j in range(columns):
+            out[rows, j * LANES : (j + 1) * LANES] = slots[s + first - base, j * height : (j + 1) * height, :]
         return carry
 
-    lax.fori_loop(0, slots.shape[0], body, 0)
-
-
-def load_matrix(flat, start, stride, columns, out, step):
-    def body(i, carry):
-        rows = pl.ds(pl.multiple_of(i * step, step), step)
-        for j in range(columns):
-            piece = flat[pl.ds(start + j + i * (step * stride), step, stride=stride), :]
-            out[rows, j * LANES : (j + 1) * LANES] = piece.astype(bf16)
-        return carry
-
-    lax.fori_loop(0, out.shape[0] // step, body, 0)
-
-
-def load_vector(flat, start, blocks):
-    return jnp.concatenate([flat[pl.ds(start + j, 1), :] for j in range(blocks)], axis=1)
-
-
-def store_vector(flat, start, value):
-    for j in range(value.shape[1] // LANES):
-        flat[pl.ds(start + j, 1), :] = value[:, j * LANES : (j + 1) * LANES]
+    lax.fori_loop(0, shards, body, 0)
+    for i, j, s, q in layout.lacking(region):
+        out[i : i + 1, j * LANES : (j + 1) * LANES] = slots[s - base, q : q + 1, :]
+
+
+def attn_layout(rows, devices):
+    return Layout(rows, devices, [(ATTN_QKV, D, ROW_QKV), (ATTN_PROJ, D, ROW_D)], 16)
+
+
+def mlp_layout_of(rows, devices):
+    return Layout(rows, devices, [(MLP_UP, D, ROW_FF), (MLP_DOWN, FF, ROW_D)], 32)
 
 
 def norm_parts(values):
@@ -740,26 +851,28 @@
 
 
 def forward_kernel(
-    dp_size, seq_size, a_rows,
-    x_in, seg_in, cot_in, a_own, m_own,
+    dp_size, seq_size, a_layout, m_layout,
+    x_in, seg_in, cot_in, a_raw, m_raw,
     m_slots, cot_own, n1_out, wqkv_out, qt_out, kt_out, qh_out, kh_out, vh_out,
     x_own, w_proj, vec, seg_all, lse, att,
     n1, wqkv, qt, kt, qh, kh, vh,
-    a_slots, flat, x_all, vt, seg_col, scores, ot, att_out,
+    a_slots, a_own, m_own, a_wide, m_wide, x_all, vt, seg_col, scores, ot, att_out,
     a_send, a_recv, m_send, m_recv, own_sems, move_send, move_recv, cot_sems, swap_sems, keep_sems,
 ):
     place = Place(seq_size)
     block = x_in.shape[1]
     ga = Gather(dp_size, seq_size, a_own, a_slots, a_send, a_recv)
     gm = Gather(dp_size, seq_size, m_own, m_slots, m_send, m_recv)
+    mine = place.dp * seq_size + place.z
+    a_layout.pack(a_raw, a_wide, a_own, mine)
     greet(place.line_peers() + [(place.dp ^ (1 << b), place.z) for b in ga.bits])
 
-    mine = place.dp * seq_size + place.z
     own_copies = [
         pltpu.make_async_copy(a_own, a_slots.at[mine], own_sems.at[0]),
         pltpu.make_async_copy(m_own, m_slots.at[mine], own_sems.at[1]),
     ]
     ga.begin()
+    m_layout.pack(m_raw, m_wide, m_own, mine)
     for copy in own_copies:
         copy.start()
     sent = []
@@ -768,61 +881,96 @@
         copy.start()
         sent.append(copy)
 
-    def send_inputs():
+    def send_segments():
         for micro in range(2):
-            to = place.worker(micro)
-            launch(remote(seg_in.at[micro], seg_all.at[place.z], move_send.at[1, micro], move_recv.at[1, place.z], to))
-            launch(remote(x_in.at[micro], x_all.at[place.z], move_send.at[0, micro], move_recv.at[0, place.z], to))
+            launch(
+                remote(
+                    seg_in.at[micro], seg_all.at[place.z], move_send.at[2, micro], move_recv.at[2, place.z],
+                    place.worker(micro),
+                )
+            )
+
+    def send_inputs(micro, half):
+        rows = pl.ds(half * (block // 2), block // 2)
+        launch(
+            remote(
+                x_in.at[micro, rows], x_all.at[place.z, rows], move_send.at[half, micro], move_recv.at[half, place.z],
+                place.worker(micro),
+            )
+        )
+
+    def moved(t, kind):
+        return seg_all.at[t] if kind == 2 else x_all.at[t, pl.ds(kind * (block // 2), block // 2)]
 
     def arrival(t, kind):
-        ref = (x_all, seg_all)[kind].at[t]
+        ref = moved(t, kind)
         return remote(ref, ref, move_send.at[kind, 0], move_recv.at[kind, t], place.sibling)
 
     def share_inputs():
         for j in range(2):
             t = place.own_block(j)
-            for kind in range(2):
-                ref = (x_all, seg_all)[kind].at[t]
+            for kind in range(3):
+                ref = moved(t, kind)
                 arrival(t, kind).wait_recv()
                 launch(remote(ref, ref, move_send.at[kind, 2 + j], move_recv.at[kind, t], place.sibling))
 
-    def send_cotangent():
-        for micro in range(2):
-            remote(
-                cot_in.at[micro], cot_own.at[place.z // 2], cot_sems.at[0, micro], cot_sems.at[1, place.z // 2],
-                place.worker(micro),
-            ).start()
+    def send_cotangent(micro):
+        remote(
+            cot_in.at[micro], cot_own.at[place.z // 2], cot_sems.at[0, micro], cot_sems.at[1, place.z // 2],
+            place.worker(micro),
+        ).start()
 
     timed = [(time, (ga, event)) for time, event in ga.events(*A_TIMES)]
     timed += [(time + (0 if event[2] else M_OWN), (gm, event)) for time, event in gm.events(*M_TIMES)]
     timed += [
         (at, (Action(), action))
         for at, action in (
-            (SEND_X, send_inputs), (SHARE_X, share_inputs), (SEND_COT, send_cotangent),
-            (M_SEQ, gm.begin_seq), (M_BITS, gm.begin_bits),
+            (SEND_X[0], send_segments), (SHARE_X, share_inputs), (M_SEQ, gm.begin_seq), (M_BITS, gm.begin_bits),
         )
     ]
+    timed += [
+        (SEND_X[n], (Action(), functools.partial(send_inputs, 1 - n // 2, n % 2))) for n in range(4)
+    ]
+    timed += [(SEND_COT[n], (Action(), functools.partial(send_cotangent, 1 - n))) for n in range(2)]
     both = Steps(timed)
     both.until(FORWARD_START)
     own_copies[0].wait()
     ga.finish_sibling()
-    unflatten(a_slots, flat, a_rows)
-    both.until(FORWARD_START + 3)
-    for section in range(3):
-        load_matrix(
-            flat, ATTN_QKV + section * ROW_D + place.core * ROW_HALF, ROW_QKV, ROW_HALF, wqkv.at[section], LANES
-        )
-    load_matrix(flat, ATTN_PROJ, ROW_D, ROW_D, w_proj, LANES)
-    gain = load_vector(flat, 0, ROW_D)
-    shift = load_vector(flat, ROW_D, ROW_D)
+    height = a_layout.regions[0][2]
+
+    def take_columns(s, carry):
+        rows = pl.ds(pl.multiple_of(s * height, height), height)
+        for section in range(3):
+            for j in range(ROW_HALF):
+                block_at = section * ROW_D + place.core * ROW_HALF + j
+                piece = a_slots[s, pl.ds(pl.multiple_of(block_at * height, height), height), :]
+                wqkv[section, rows, j * LANES : (j + 1) * LANES] = piece
+        return carry
+
+    lax.fori_loop(0, a_layout.regions[0][4], take_columns, 0)
+    for core in range(2):
+
+        @pl.when(place.core == core)
+        def _():
+            for i, j, s, q in a_layout.lacking(a_layout.regions[0]):
+                section, at = j // ROW_D, j % ROW_D - core * ROW_HALF
+                if 0 <= at < ROW_HALF:
+                    wqkv[section, i : i + 1, at * LANES : (at + 1) * LANES] = a_slots[s, q : q + 1, :]
+
+    load_matrix(a_slots, a_layout, 1, 0, w_proj)
+    gain = a_layout.vector(a_slots, 0, ROW_D)
+    shift = a_layout.vector(a_slots, ROW_D, ROW_D)
     vec[...] = jnp.zeros_like(vec)
     vec[0:1, :] = gain
-    vec[1:2, :] = load_vector(flat, ATTN_BPROJ, ROW_D)
-    bias_query = load_vector(flat, ATTN_BQ + place.core * ROW_HALF, ROW_HALF)
-    bias_value = load_vector(flat, ATTN_BV + place.core * ROW_HALF, ROW_HALF)
-    both.until(FORWARD_START + 7)
+    vec[1:2, :] = a_layout.vector(a_slots, ATTN_BPROJ, ROW_D)
+    first_half = place.core == 0
+    bias_query = a_layout.vector(a_slots, ATTN_BQ, ROW_D)
+    bias_query = jnp.where(first_half, bias_query[:, :HALF_COLS], bias_query[:, HALF_COLS:])
+    bias_value = a_layout.vector(a_slots, ATTN_BV, ROW_D)
+    bias_value = jnp.where(first_half, bias_value[:, :HALF_COLS], bias_value[:, HALF_COLS:])
+    both.until(FORWARD_START + 2)
     for j in range(2):
-        for kind in range(2):
+        for kind in range(3):
             arrival(place.other_block(j), kind).wait_recv()
         x_own[j] = x_all[place.own_block(j)]
     segment_columns(seg_all, seg_col, block)
@@ -852,7 +1000,7 @@
     lse[...] = jnp.zeros_like(lse)
     unit = HEAD_FORWARD / (seq_size * (seq_size + 1) // 2)
     points = [((h, i), unit * (i + 1)) for h in range(HALF_HEADS) for i in range(seq_size)]
-    plan = both.plan(FORWARD_START + 12, points)
+    plan = both.plan(FORWARD_START + 7, points)
 
     def one_head(h, carry):
         head_rows = pl.ds(pl.multiple_of(h * HD, HD), HD)
@@ -911,314 +1059,348 @@
     gm.finish_sends()
 
 
-def mlp_kernel(
-    m_rows,
-    m_slots, x_own, cot, att, w_proj, vec,
-    g_out, out, d_mid, d_att, g_proj, g_bias,
-    g_slots, flat, w_up, w_down, mid, n2, d_n2, total, b_up, gb_up, sem, out_sems,
-):
-    rows_all = x_own.shape[0]
-    half = rows_all // 2
-    copy = pltpu.make_async_copy(m_slots, g_slots, sem)
-    copy.start()
-    blocks = [slice(0, half), slice(half, rows_all)]
-    for rows in blocks:
-        mid[rows, :] = (
-            x_own[rows, :].astype(f32)
-            + dot_nn(att[0, rows, :], w_proj[:HALF_COLS, :])
-            + dot_nn(att[1, rows, :], w_proj[HALF_COLS:, :])
-            + vec[1:2, :]
-        )
-    copy.wait()
-    unflatten(g_slots, flat, m_rows)
-    load_matrix(flat, MLP_UP, ROW_FF, ROW_FF, w_up, 64)
-    load_matrix(flat, MLP_DOWN, ROW_D, ROW_D, w_down, LANES)
-    gain = load_vector(flat, 0, ROW_D)
-    shift = load_vector(flat, ROW_D, ROW_D)
-    b_down = load_vector(flat, MLP_BDOWN, ROW_D)
-    b_up[...] = load_vector(flat, MLP_BUP, ROW_FF)
-    for rows in blocks:
-        normal, _ = norm_parts(mid[rows, :])
-        n2[rows, :] = (normal * gain + shift).astype(bf16)
-    total[...] = jnp.zeros_like(total)
-    d_n2[...] = jnp.zeros_like(d_n2)
-    inner = math.sqrt(2.0 / math.pi)
-
-    def step(f, carry):
-        start = pl.multiple_of(f * FF_STEP, FF_STEP)
-        columns = pl.ds(start, FF_STEP)
-        hidden = dot_nn(n2[...], w_up[:, columns]) + b_up[:, columns]
-        square = hidden * hidden
-        tanh = jnp.tanh(inner * (hidden + 0.044715 * (square * hidden)))
-        cdf = 0.5 * (1.0 + tanh)
-        active = (hidden * cdf).astype(bf16)
-        slope = cdf + (0.5 * inner) * hidden * (1.0 - tanh * tanh) * (1.0 + (3 * 0.044715) * square)
-        d_hidden = dot_nt(cot[...], w_down[columns, :]) * slope
-        low = d_hidden.astype(bf16)
-        gb_up[:, columns] = jnp.sum(low.astype(f32), axis=0, keepdims=True)
-        total[...] += dot_nn(active, w_down[columns, :])
-        d_n2[...] += dot_nt(low, w_up[:, columns])
-        g_down = dot_tn(active, cot[...])
-        for j in range(ROW_D):
-            flat[pl.ds(MLP_DOWN + j + f * (FF_STEP * ROW_D), FF_STEP, stride=ROW_D), :] = g_down[
-                :, j * LANES : (j + 1) * LANES
-            ]
-        g_up = dot_tn(n2[...], low)
-        for j in range(FF_STEP // LANES):
-            flat[pl.ds(MLP_UP + j + f * (FF_STEP // LANES), D, stride=ROW_FF), :] = g_up[
-                :, j * LANES : (j + 1) * LANES
-            ]
-        return carry
-
-    lax.fori_loop(0, FF // FF_STEP, step, 0)
-
-    gain_sum = jnp.zeros((1, D), f32)
-    shift_sum = jnp.zeros((1, D), f32)
-    down_sum = jnp.zeros((1, D), f32)
-    proj_sum = jnp.zeros((1, D), f32)
-    for rows in blocks:
-        out[rows, :] = (mid[rows, :] + total[rows, :] + b_down).astype(bf16)
-        normal, scale = norm_parts(mid[rows, :])
-        grad = d_n2[rows, :]
-        cot_rows = cot[rows, :].astype(f32)
-        gain_sum += jnp.sum(grad * normal, axis=0, keepdims=True)
-        shift_sum += jnp.sum(grad, axis=0, keepdims=True)
-        down_sum += jnp.sum(cot_rows, axis=0, keepdims=True)
-        d_rows = cot_rows + norm_back(normal, scale, grad, gain)
-        d_mid[rows, :] = d_rows
-        low = d_rows.astype(bf16)
-        n2[rows, :] = low
-        proj_sum += jnp.sum(low.astype(f32), axis=0, keepdims=True)
-        for c in range(2):
-            d_att[c, rows, :] = dot_nt(low, w_proj[c * HALF_COLS : (c + 1) * HALF_COLS, :]).astype(bf16)
-    for c in range(2):
-        g_part = dot_tn(att[c], n2[...])
-        for j in range(ROW_D):
-            g_proj[pl.ds(c * HALF_COLS * ROW_D + j, HALF_COLS, stride=ROW_D), :] = g_part[
-                :, j * LANES : (j + 1) * LANES
-            ]
-    g_bias[...] = proj_sum
-    store_vector(flat, 0, gain_sum)
-    store_vector(flat, ROW_D, shift_sum)
-    store_vector(flat, MLP_BUP, gb_up[...])
-    store_vector(flat, MLP_BDOWN, down_sum)
-    used = MLP_BDOWN + ROW_D
-    flat[used:, :] = jnp.zeros((flat.shape[0] - used, LANES), f32)
-    group = g_slots.shape[0] // 4
-    flush = []
-    for part in range(4):
-        slots = pl.ds(part * group, group)
-
-        def body(s, carry, part=part):
-            s = s + part * group
-            g_slots[s, :m_rows, :] = flat[pl.ds(s * m_rows, m_rows), :].astype(bf16)
-            return carry
-
-        lax.fori_loop(0, group, body, 0)
-        copy = pltpu.make_async_copy(g_slots.at[slots], g_out.at[slots], out_sems.at[part])
-        copy.start()
-        flush.append(copy)
-    for copy in flush:
-        copy.wait()
-
-
 def backward_kernel(
-    dp_size, seq_size, a_rows,
-    out_own, m_grads, g_proj, n1_in, wqkv_in, qt_in, kt_in, qh_in, kh_in, vh_in, d_mid_in, x_own_in,
-    d_att, g_bias, vec, seg_all, lse,
+    dp_size, seq_size, a_layout, m_layout,
+    m_slots, x_own_in, n1_in, wqkv_in, qt_in, kt_in, qh_in, kh_in, vh_in, cot_in, att_in, w_proj_in,
+    vec, seg_all, lse,
     out_back, grad_back, a_out, m_out,
-    n1, wqkv, qt, kt, qh, kh, vh, d_mid, x_own,
-    flat, d_all, dt, dh, seg_col, p_piece, d_piece, dk, dv, dqt, dm, d_n1, d_n1_in,
-    move_sems, swap_sems, norm_sems, proj_sem, load_sems, *refs,
+    g_slots, a_slots, x_own, out_own, d_mid, d_att, d_all, d_n1_in, g_bias, a_wide, m_wide,
+    move_sems, swap_sems, norm_sems, load_sems, *refs,
 ):
     place = Place(seq_size)
-    block = x_own_in.shape[1]
+    block = x_own.shape[1]
+    length = seq_size * block
+    mine = place.dp * seq_size + place.z
     count = len(refs) // 2
-    sm = make_scatter(dp_size, seq_size, m_out, refs[:count])
-    sa = make_scatter(dp_size, seq_size, a_out, refs[count:])
-    loads = [
-        pltpu.make_async_copy(src, dst, load_sems.at[i])
-        for i, (src, dst) in enumerate(
+    sm = make_scatter(dp_size, seq_size, g_slots, refs[:count])
+    sa = make_scatter(dp_size, seq_size, a_slots, refs[count:])
+    slots_copy = pltpu.make_async_copy(m_slots, g_slots, load_sems.at[1])
+    slots_copy.start()
+    greet(place.line_peers() + [(place.dp ^ (1 << b), place.z) for b in sm.bits])
+    a_slots[...] = jnp.zeros_like(a_slots)
+    def mlp(cot, att, w_proj, w_up, w_down, mid, n2, d_n2, total, b_up, gb_up):
+        blocks = [slice(j * block, (j + 1) * block) for j in range(2)]
+        first_loads = [
+            pltpu.make_async_copy(src, dst, load_sems.at[i])
+            for i, src, dst in ((0, x_own_in, x_own), (9, att_in, att), (10, w_proj_in, w_proj), (11, cot_in, cot))
+        ]
+        for copy in first_loads:
+            copy.start()
+        for copy in first_loads:
+            copy.wait()
+        for j, rows in enumerate(blocks):
+            mid[rows, :] = (
+                x_own[j].astype(f32)
+                + dot_nn(att[0, rows, :], w_proj[:HALF_COLS, :])
+                + dot_nn(att[1, rows, :], w_proj[HALF_COLS:, :])
+                + vec[1:2, :]
+            )
+        slots_copy.wait()
+        load_matrix(g_slots, m_layout, 0, 0, w_up)
+        load_matrix(g_slots, m_layout, 1, 0, w_down)
+        gain = m_layout.vector(g_slots, 0, ROW_D)
+        shift = m_layout.vector(g_slots, ROW_D, ROW_D)
+        b_down = m_layout.vector(g_slots, MLP_BDOWN, ROW_D)
+        b_up[...] = m_layout.vector(g_slots, MLP_BUP, ROW_FF)
+        for rows in blocks:
+            normal, _ = norm_parts(mid[rows, :])
+            n2[rows, :] = (normal * gain + shift).astype(bf16)
+        total[...] = jnp.zeros_like(total)
+        d_n2[...] = jnp.zeros_like(d_n2)
+        inner = math.sqrt(2.0 / math.pi)
+        _, _, up_height, up_first, up_shards = m_layout.regions[0]
+        _, _, down_height, down_first, _ = m_layout.regions[1]
+        turns = FF // FF_STEP // 2
+
+        def step(u, carry):
+            for v in range(turns):
+                start = pl.multiple_of((u * turns + v) * FF_STEP, FF_STEP)
+                columns = pl.ds(start, FF_STEP)
+                hidden = dot_nn(n2[...], w_up[:, columns]) + b_up[:, columns]
+                square = hidden * hidden
+                tanh = jnp.tanh(inner * (hidden + 0.044715 * (square * hidden)))
+                cdf = 0.5 * (1.0 + tanh)
+                active = (hidden * cdf).astype(bf16)
+                slope = cdf + (0.5 * inner) * hidden * (1.0 - tanh * tanh) * (1.0 + (3 * 0.044715) * square)
+                low = (dot_nt(cot[...], w_down[columns, :]) * slope).astype(bf16)
+                gb_up[:, columns] = jnp.sum(low.astype(f32), axis=0, keepdims=True)
+                total[...] += dot_nn(active, w_down[columns, :])
+                d_n2[...] += dot_nt(low, w_up[:, columns])
+                g_down = dot_tn(active, cot[...]).astype(bf16)
+                begin = v * FF_STEP
+                for t in range(begin // down_height, (begin + FF_STEP - 1) // down_height + 1):
+                    top = max(begin, t * down_height)
+                    end = min(begin + FF_STEP, (t + 1) * down_height)
+                    slot = down_first + u * (turns * FF_STEP // down_height) + t
+                    for j in range(ROW_D):
+                        at = j * down_height + top - t * down_height
+                        g_slots[slot, at : at + end - top, :] = g_down[
+                            top - begin : end - begin, j * LANES : (j + 1) * LANES
+                        ]
+                g_up = dot_tn(n2[...], low).astype(bf16)
+                for j in range(FF_STEP // LANES):
+                    at = ((u * turns + v) * (FF_STEP // LANES) + j) * up_height
+                    rows = pl.ds(pl.multiple_of(at, up_height), up_height)
+                    for s in range(up_shards):
+                        g_slots[up_first + s, rows, :] = g_up[
+                            s * up_height : (s + 1) * up_height, j * LANES : (j + 1) * LANES
+                        ]
+            return carry
+
+        lax.fori_loop(0, 2, step, 0)
+
+        gain_sum = jnp.zeros((1, D), f32)
+        shift_sum = jnp.zeros((1, D), f32)
+        down_sum = jnp.zeros((1, D), f32)
+        proj_sum = jnp.zeros((1, D), f32)
+        for rows in blocks:
+            normal, scale = norm_parts(mid[rows, :])
+            grad = d_n2[rows, :]
+            cot_rows = cot[rows, :].astype(f32)
+            gain_sum += jnp.sum(grad * normal, axis=0, keepdims=True)
+            shift_sum += jnp.sum(grad, axis=0, keepdims=True)
+            down_sum += jnp.sum(cot_rows, axis=0, keepdims=True)
+            d_rows = cot_rows + norm_back(normal, scale, grad, gain)
+            d_mid[rows, :] = d_rows
+            low = d_rows.astype(bf16)
+            n2[rows, :] = low
+            proj_sum += jnp.sum(low.astype(f32), axis=0, keepdims=True)
+        m_layout.put_vectors(
+            g_slots, [(0, gain_sum), (ROW_D, shift_sum), (MLP_BUP, gb_up[...]), (MLP_BDOWN, down_sum)]
+        )
+        for s, q, there, at in m_layout.beyond():
+            g_slots[s, q : q + 1, :] = g_slots[there, at : at + 1, :]
+        sm.begin()
+        for c in range(2):
+            for rows in blocks:
+                d_att[c, rows, :] = dot_nt(n2[rows, :], w_proj[c * HALF_COLS : (c + 1) * HALF_COLS, :]).astype(bf16)
+        for j in range(2):
+            src = d_att.at[1 - place.core, pl.ds(j * block, block)]
+            remote(
+                src, d_all.at[place.own_block(j)], swap_sems.at[0, j], swap_sems.at[1, j], place.sibling
+            ).start()
+        steps.until(BACKWARD_FIRST)
+        for j, rows in enumerate(blocks):
+            out_own[rows, :] = (mid[rows, :] + total[rows, :] + b_down).astype(bf16)
+            to, micro = place.home(j)
+            remote(
+                out_own.at[pl.ds(j * block, block)], out_back.at[micro], move_sems.at[0, j], move_sems.at[1, micro], to
+            ).start()
+        g_bias[...] = proj_sum
+        _, _, height, first, shards = a_layout.regions[1]
+        for c in range(2):
+            g_part = dot_tn(att[c], n2[...]).astype(bf16)
+            for t in range(shards // 2):
+                for j in range(ROW_D):
+                    a_slots[first + c * (shards // 2) + t, j * height : (j + 1) * height, :] = g_part[
+                        t * height : (t + 1) * height, j * LANES : (j + 1) * LANES
+                    ]
+
+    tokens = 2 * block
+    steps = Steps([(time, (sm, event)) for time, event in sm.events()])
+    pl.run_scoped(
+        mlp,
+        pltpu.VMEM((tokens, D), bf16), pltpu.VMEM((2, tokens, HALF_COLS), bf16), pltpu.VMEM((D, D), bf16),
+        pltpu.VMEM((D, FF), bf16), pltpu.VMEM((FF, D), bf16),
+        pltpu.VMEM((tokens, D), f32), pltpu.VMEM((tokens, D), bf16),
+        pltpu.VMEM((tokens, D), f32), pltpu.VMEM((tokens, D), f32),
+        pltpu.VMEM((1, FF), f32), pltpu.VMEM((1, FF), f32),
+    )
+
+    def attention(
+        n1, wqkv, qt, kt, qh, kh, vh, dt, dh, seg_col, p_piece, d_piece, dk, dv, dqt, dm, d_n1
+    ):
+        loads = [
+            pltpu.make_async_copy(src, dst, load_sems.at[2 + i])
+            for i, (src, dst) in enumerate(
+                [(qt_in, qt), (kt_in, kt), (qh_in, qh), (kh_in, kh), (vh_in, vh), (n1_in, n1), (wqkv_in, wqkv)]
+            )
+        ]
+        for copy in loads:
+            copy.start()
+        for j in range(2):
+            d_all[place.own_block(j)] = d_att[place.core, j * block : (j + 1) * block, :]
+        segment_columns(seg_all, seg_col, block)
+        steps.until(BACKWARD_START - 3)
+        for j in range(2):
+            ref = d_all.at[place.other_block(j)]
+            remote(ref, ref, swap_sems.at[0, j], swap_sems.at[1, j], place.sibling).wait_recv()
+
+        def spread(t, carry):
+            rows = pl.ds(pl.multiple_of(t * block, block), block)
+            piece = d_all[t]
+            dt[:, rows] = piece.astype(f32).T.astype(bf16)
+            split_heads(piece, dh, rows)
+            return carry
+
+        lax.fori_loop(0, seq_size, spread, 0)
+        steps.until(BACKWARD_START)
+        unit = HEAD_BACKWARD / (seq_size * (seq_size + 1) // 2)
+        points = [
+            ((i, side, pair), unit * (i + 1))
+            for i in reversed(range(seq_size))
+            for pair in range(HALF_HEADS // 2)
+            for side in range(2)
+        ]
+        plan = steps.plan(BACKWARD_START, points)
+        for copy in loads[:5]:
+            copy.wait()
+
+        def query_block(i):
+            columns = slice(i * block, (i + 1) * block)
+
+            def one_pair(pair, carry):
+                pair_rows = pl.ds(pl.multiple_of(pair * LANES, LANES), LANES)
+                for side in range(2):
+                    handle([plan[i, side, turn] for turn in range(HALF_HEADS // 2)], pair)
+                    h = 2 * pair + side
+                    head_rows = pl.ds(pl.multiple_of(h * HD, HD), HD)
+                    query = qt[pair_rows, columns]
+                    d_query = dt[pair_rows, columns]
+                    level = lse[pl.ds(h, 1), columns]
+                    delta = jnp.zeros((1, block), f32)
+                    for b in range(i + 1):
+                        rows = slice(b * block, (b + 1) * block)
+                        probs = jnp.exp(
+                            keep_allowed(dot_nn(kh[h, rows, :], query), seg_col, seg_all, b, i, block) - level
+                        )
+                        d_probs = dot_nn(vh[h, rows, :], d_query)
+                        delta = delta + jnp.sum(probs * d_probs, axis=0, keepdims=True)
+                        p_piece[rows, :] = probs
+                        d_piece[rows, :] = d_probs
+                    result = jnp.zeros((HD, block), f32)
+                    for b in range(i + 1):
+                        rows = slice(b * block, (b + 1) * block)
+                        probs = p_piece[rows, :]
+                        d_scores = (probs * (d_piece[rows, :] - delta)).astype(bf16)
+                        key_part = dot_nn(d_scores, qh[h, columns, :])
+                        value_part = dot_nn(probs.astype(bf16), dh[h, columns, :])
+                        if i == seq_size - 1 and side == 0:
+                            dk[pair, rows, :] = key_part
+                            dv[pair, rows, :] = value_part
+                        else:
+                            dk[pair, rows, :] += key_part
+                            dv[pair, rows, :] += value_part
+                        result = result + dot_nn(kt[head_rows, rows], d_scores)
+                    dqt[head_rows, :] = result * (1.0 / math.sqrt(HD))
+                return carry
+
+            lax.fori_loop(0, HALF_HEADS // 2, one_pair, 0)
+            dm[0, columns, :] = dqt[...].T.astype(bf16)
+            for section, part in ((1, dk), (2, dv)):
+                for pair in range(HALF_HEADS // 2):
+                    dm[section, columns, pair * LANES : (pair + 1) * LANES] = part[pair, columns, :].astype(bf16)
+
+        def to_norm(t):
+            rows = pl.ds(pl.multiple_of(t * block, block), block)
+            return (
+                dot_nt(dm[0, rows, :], wqkv[0]) + dot_nt(dm[1, rows, :], wqkv[1]) + dot_nt(dm[2, rows, :], wqkv[2])
+            )
+
+        def share_norm(j):
+            d_n1[j] = to_norm(place.other_block(j))
+            remote(d_n1.at[j], d_n1_in.at[j], norm_sems.at[0, j], norm_sems.at[1, j], place.sibling).start()
+
+        def finish_input(j):
+            ref = d_n1_in.at[j]
+            remote(ref, ref, norm_sems.at[0, j], norm_sems.at[1, j], place.sibling).wait_recv()
+            grad = to_norm(place.own_block(j)) + d_n1_in[j]
+            normal, scale = norm_parts(x_own[j].astype(f32))
+            x_own[j] = (d_mid[j * block : (j + 1) * block, :] + norm_back(normal, scale, grad, gain)).astype(bf16)
+            to, micro = place.home(j)
+            remote(x_own.at[j], grad_back.at[micro], move_sems.at[2, j], move_sems.at[3, micro], to).start()
+            return jnp.sum(grad * normal, axis=0, keepdims=True), jnp.sum(grad, axis=0, keepdims=True)
+
+        gain = vec[0:1, :]
+        query_block(3)
+        query_block(2)
+        for copy in loads[5:]:
+            copy.wait()
+        share_norm(1)
+        query_block(1)
+        gain_sum, shift_sum = finish_input(1)
+        query_block(0)
+        share_norm(0)
+        now = BACKWARD_START + HALF_HEADS * HEAD_BACKWARD
+        steps.until(now)
+        _, _, height, first, shards = a_layout.regions[0]
+        for section in range(3):
+            part = dot_tn(n1[...], dm[section]).astype(bf16)
+            for j in range(ROW_HALF):
+                at = (section * ROW_D + place.core * ROW_HALF + j) * height
+                rows = pl.ds(pl.multiple_of(at, height), height)
+                for s in range(shards):
+                    a_slots[first + s, rows, :] = part[s * height : (s + 1) * height, j * LANES : (j + 1) * LANES]
+        steps.until(now + 4)
+        more_gain, more_shift = finish_input(0)
+        sums = []
+        for section in (0, 2):
+            half = jnp.sum(dm[section].astype(f32), axis=0, keepdims=True)
+            zero = jnp.zeros_like(half)
+            first_half = place.core == 0
+            sums.append(
+                jnp.concatenate([jnp.where(first_half, half, zero), jnp.where(first_half, zero, half)], axis=1)
+            )
+        a_layout.put_vectors(
+            a_slots,
             [
-                (qt_in, qt), (kt_in, kt), (qh_in, qh), (kh_in, kh), (vh_in, vh),
-                (n1_in, n1), (wqkv_in, wqkv), (d_mid_in, d_mid), (x_own_in, x_own),
-            ]
-        )
-    ]
-    for copy in loads:
-        copy.start()
-    greet(place.line_peers() + [(place.dp ^ (1 << b), place.z) for b in sm.bits])
-    sent = []
-    for j in range(2):
-        t = place.own_block(j)
-        src = d_att.at[1 - place.core, pl.ds(j * block, block)]
-        copy = remote(src, d_all.at[t], swap_sems.at[0, j], swap_sems.at[1, j], place.sibling)
-        copy.start()
-        sent.append(copy)
-    sm.begin(m_grads)
-    for j in range(2):
-        to, micro = place.home(j)
-        copy = remote(
-            out_own.at[pl.ds(j * block, block)], out_back.at[micro], move_sems.at[0, j], move_sems.at[1, micro], to
-        )
-        copy.start()
-        sent.append(copy)
-    flat[...] = jnp.zeros_like(flat)
-    proj_copy = pltpu.make_async_copy(g_proj, flat.at[pl.ds(ATTN_PROJ, D * ROW_D)], proj_sem)
-    proj_copy.start()
-    for j in range(2):
-        d_all[place.own_block(j)] = d_att[place.core, j * block : (j + 1) * block, :]
-    segment_columns(seg_all, seg_col, block)
-    for j in range(2):
-        ref = d_all.at[place.other_block(j)]
-        remote(ref, ref, swap_sems.at[0, j], swap_sems.at[1, j], place.sibling).wait_recv()
-
-    def spread(t, carry):
-        rows = pl.ds(pl.multiple_of(t * block, block), block)
-        piece = d_all[t]
-        dt[:, rows] = piece.astype(f32).T.astype(bf16)
-        split_heads(piece, dh, rows)
-        return carry
-
-    lax.fori_loop(0, seq_size, spread, 0)
-
-    steps = Steps([(time, (sm, event)) for time, event in sm.events()])
-    steps.until(BACKWARD_START)
-    unit = HEAD_BACKWARD / (seq_size * (seq_size + 1) // 2)
-    points = [
-        ((i, side, pair), unit * (i + 1))
-        for i in reversed(range(seq_size))
-        for pair in range(HALF_HEADS // 2)
-        for side in range(2)
-    ]
-    plan = steps.plan(BACKWARD_START, points)
-    for copy in loads[:5]:
-        copy.wait()
-
-    def query_block(i):
-        columns = slice(i * block, (i + 1) * block)
-
-        def one_pair(pair, carry):
-            pair_rows = pl.ds(pl.multiple_of(pair * LANES, LANES), LANES)
-            for side in range(2):
-                handle([plan[i, side, turn] for turn in range(HALF_HEADS // 2)], pair)
-                h = 2 * pair + side
-                head_rows = pl.ds(pl.multiple_of(h * HD, HD), HD)
-                query = qt[pair_rows, columns]
-                d_query = dt[pair_rows, columns]
-                level = lse[pl.ds(h, 1), columns]
-                delta = jnp.zeros((1, block), f32)
-                for b in range(i + 1):
-                    rows = slice(b * block, (b + 1) * block)
-                    probs = jnp.exp(
-                        keep_allowed(dot_nn(kh[h, rows, :], query), seg_col, seg_all, b, i, block) - level
-                    )
-                    d_probs = dot_nn(vh[h, rows, :], d_query)
-                    delta = delta + jnp.sum(probs * d_probs, axis=0, keepdims=True)
-                    p_piece[rows, :] = probs
-                    d_piece[rows, :] = d_probs
-                result = jnp.zeros((HD, block), f32)
-                for b in range(i + 1):
-                    rows = slice(b * block, (b + 1) * block)
-                    probs = p_piece[rows, :]
-                    d_scores = (probs * (d_piece[rows, :] - delta)).astype(bf16)
-                    key_part = dot_nn(d_scores, qh[h, columns, :])
-                    value_part = dot_nn(probs.astype(bf16), dh[h, columns, :])
-                    if i == seq_size - 1 and side == 0:
-                        dk[pair, rows, :] = key_part
-                        dv[pair, rows, :] = value_part
-                    else:
-                        dk[pair, rows, :] += key_part
-                        dv[pair, rows, :] += value_part
-                    result = result + dot_nn(kt[head_rows, rows], d_scores)
-                dqt[head_rows, columns] = result * (1.0 / math.sqrt(HD))
-            return carry
-
-        lax.fori_loop(0, HALF_HEADS // 2, one_pair, 0)
-        dm[0, columns, :] = dqt[:, columns].T.astype(bf16)
-        for section, part in ((1, dk), (2, dv)):
-            for pair in range(HALF_HEADS // 2):
-                dm[section, columns, pair * LANES : (pair + 1) * LANES] = part[pair, columns, :].astype(bf16)
-
-    def to_norm(t):
-        rows = pl.ds(pl.multiple_of(t * block, block), block)
-        return dot_nt(dm[0, rows, :], wqkv[0]) + dot_nt(dm[1, rows, :], wqkv[1]) + dot_nt(dm[2, rows, :], wqkv[2])
-
-    def share_norm(j):
-        d_n1[j] = to_norm(place.other_block(j))
-        copy = remote(d_n1.at[j], d_n1_in.at[j], norm_sems.at[0, j], norm_sems.at[1, j], place.sibling)
-        copy.start()
-        sent.append(copy)
-        d_n1[2] = to_norm(place.own_block(j))
-
-    def finish_input(j):
-        ref = d_n1_in.at[j]
-        remote(ref, ref, norm_sems.at[0, j], norm_sems.at[1, j], place.sibling).wait_recv()
-        grad = d_n1[2] + d_n1_in[j]
-        normal, scale = norm_parts(x_own[j].astype(f32))
-        x_own[j] = (d_mid[j * block : (j + 1) * block, :] + norm_back(normal, scale, grad, gain)).astype(bf16)
-        to, micro = place.home(j)
-        copy = remote(x_own.at[j], grad_back.at[micro], move_sems.at[2, j], move_sems.at[3, micro], to)
-        copy.start()
-        sent.append(copy)
-        return jnp.sum(grad * normal, axis=0, keepdims=True), jnp.sum(grad, axis=0, keepdims=True)
-
-    gain = vec[0:1, :]
-    query_block(3)
-    query_block(2)
-    for copy in loads[5:]:
-        copy.wait()
-    share_norm(1)
-    query_block(1)
-    gain_sum, shift_sum = finish_input(1)
-    query_block(0)
-    share_norm(0)
-    now = BACKWARD_START + HALF_HEADS * HEAD_BACKWARD
-    steps.until(now)
-    proj_copy.wait()
-    for section in range(3):
-        part = dot_tn(n1[...], dm[section])
-        for j in range(ROW_HALF):
-            start = ATTN_QKV + section * ROW_D + place.core * ROW_HALF + j
-            flat[pl.ds(start, D, stride=ROW_QKV), :] = part[:, j * LANES : (j + 1) * LANES]
-    steps.until(now + 5)
-    more_gain, more_shift = finish_input(0)
-    store_vector(flat, 0, gain_sum + more_gain)
-    store_vector(flat, ROW_D, shift_sum + more_shift)
-    for section, start in ((0, ATTN_BQ), (2, ATTN_BV)):
-        total = jnp.sum(dm[section].astype(f32), axis=0, keepdims=True)
-        store_vector(flat, start + place.core * ROW_HALF, total)
-    store_vector(flat, ATTN_BPROJ, g_bias[...])
-    sa.begin_flat(flat, a_rows, sm.core_in)
-    steps.until(math.inf)
-    for _, event in sa.events():
-        sa.step(event)
-    sm.finish()
-    sa.finish()
-    for micro in range(2):
-        for kind, ref in ((1, out_back), (3, grad_back)):
-            remote(
-                ref.at[micro], ref.at[micro], move_sems.at[0, micro], move_sems.at[kind, micro], place.sibling
-            ).wait_recv()
-    for copy in sent:
-        copy.wait_send()
+                (0, gain_sum + more_gain), (ROW_D, shift_sum + more_shift),
+                (ATTN_BQ, sums[0]), (ATTN_BV, sums[1]), (ATTN_BPROJ, g_bias[...]),
+            ],
+        )
+        for s, q, there, at in a_layout.beyond():
+            a_slots[s, q : q + 1, :] = a_slots[there, at : at + 1, :]
+        sa.begin()
+        Steps(steps.queue + [(now + time, (sa, event)) for time, event in sa.events(*A_BACK)]).until(math.inf)
+        sm.finish()
+        m_layout.unpack(sm.out, m_wide, m_out, mine)
+        sa.finish()
+        a_layout.unpack(sa.out, a_wide, a_out, mine)
+        for micro in range(2):
+            for kind, ref in ((1, out_back), (3, grad_back)):
+                remote(
+                    ref.at[micro], ref.at[micro], move_sems.at[0, micro], move_sems.at[kind, micro], place.sibling
+                ).wait_recv()
+        for j in range(2):
+            for ref, sem in (
+                (d_all, swap_sems.at[0, j]), (out_back, move_sems.at[0, j]),
+                (d_n1_in, norm_sems.at[0, j]), (grad_back, move_sems.at[2, j]),
+            ):
+                remote(ref.at[0], ref.at[0], sem, sem, place.sibling).wait_send()
+
+    pl.run_scoped(
+        attention,
+        *[
+            pltpu.VMEM(ref.shape, ref.dtype)
+            for ref in (n1_in, wqkv_in, qt_in, kt_in, qh_in, kh_in, vh_in)
+        ],
+        pltpu.VMEM((HALF_COLS, length), bf16),
+        pltpu.VMEM((HALF_HEADS, length, LANES), bf16),
+        pltpu.VMEM((length, LANES), jnp.int32),
+        pltpu.VMEM((length, block), f32),
+        pltpu.VMEM((length, block), f32),
+        pltpu.VMEM((HALF_HEADS // 2, length, LANES), f32),
+        pltpu.VMEM((HALF_HEADS // 2, length, LANES), f32),
+        pltpu.VMEM((HALF_COLS, block), f32),
+        pltpu.VMEM((3, length, HALF_COLS), bf16),
+        pltpu.VMEM((2, block, D), f32),
+    )
 
 
 class Scatter:
-    def __init__(self, dp_size, seq_size, out, acc, core_in, level_in, seq_in, load_sems, send_sems, recv_sems, seq_sems):
+    def __init__(self, dp_size, seq_size, slots, out, core_in, level_in, seq_in, send_sems, recv_sems, seq_sems):
         self.n = seq_size
         self.bits = list(range(1, dp_size.bit_length() - 1))
         self.masks = [m << 1 for m in range(1 << len(self.bits))]
         self.dp = lax.axis_index("dp")
         self.z = lax.axis_index("seq")
-        self.out, self.acc = out, acc
-        self.loads = []
+        self.slots, self.out = slots, out
         self.core_in, self.level_in, self.seq_in = core_in, level_in, seq_in
-        rows = acc.shape[2]
+        rows = slots.shape[1]
         half = rows // 32 * 16
         self.parts = [(0, half), (half, rows - half)]
         self.orders = [self.bits[::-1], self.bits]
-        self.load_sems, self.send_sems, self.recv_sems, self.seq_sems = load_sems, send_sems, recv_sems, seq_sems
+        self.send_sems, self.recv_sems, self.seq_sems = send_sems, recv_sems, seq_sems
         self.started = []
         self.indices = {}
 
@@ -1239,28 +1421,23 @@
     def turn(self):
         return list(range(self.n))[::-1]
 
-    def begin(self, slots):
+    def begin(self):
         for k in self.turn():
             for mask in self.masks[::-1]:
                 i = self.masks.index(mask)
-                load = pltpu.make_async_copy(
-                    slots.at[self.slot(mask, k)], self.acc.at[i, k], self.load_sems.at[i, k]
+                self.send(
+                    self.slots.at[self.slot(mask ^ 1, k)], self.core_in.at[i, k], (self.dp ^ 1, self.z), ("c", i, k)
                 )
-                load.start()
-                self.loads.append(load)
-                self.send(
-                    slots.at[self.slot(mask ^ 1, k)], self.core_in.at[i, k], (self.dp ^ 1, self.z), ("c", i, k)
-                )
-
-    def begin_flat(self, flat, rows, core_out):
-        whole = self.acc.shape[2]
-        for k in self.turn():
-            for mask in self.masks[::-1]:
-                i = self.masks.index(mask)
-                for target, which in ((core_out, mask ^ 1), (self.acc, mask)):
-                    target[i, k, :rows, :] = flat[pl.ds(self.slot(which, k) * rows, rows), :].astype(bf16)
-                    target[i, k, rows:whole, :] = jnp.zeros((whole - rows, LANES), bf16)
-                self.send(core_out.at[i, k, pl.ds(0, whole)], self.core_in.at[i, k], (self.dp ^ 1, self.z), ("c", i, k))
+
+    def add(self, mask, k, part, term):
+        start, size = (0, self.slots.shape[1]) if part is None else self.parts[part]
+        rows = pl.ds(start, size)
+        index = self.slot(mask, k)
+        self.slots[index, rows, :] = (self.slots[index, rows, :].astype(f32) + term.astype(f32)).astype(bf16)
+
+    def view(self, mask, k, part):
+        start, size = self.parts[part]
+        return self.slots.at[self.slot(mask, k), pl.ds(start, size)]
 
     def cell(self, part, level, mask):
         free = [b for b in self.bits if b not in self.orders[part][: level + 1]]
@@ -1268,9 +1445,7 @@
 
     def pass_on(self, part, level, mask, k):
         order = self.orders[part]
-        i = self.masks.index(mask)
-        start, size = self.parts[part]
-        src = self.acc.at[i, k, pl.ds(start, size)]
+        src = self.view(mask, k, part)
         if level == len(order):
             return
         bit = 1 << order[level]
@@ -1301,10 +1476,8 @@
         if event[0] == "c":
             _, mask, k = event
             i = self.masks.index(mask)
-            if self.loads:
-                pltpu.make_async_copy(self.acc.at[i, k], self.acc.at[i, k], self.load_sems.at[i, k]).wait()
             self.wait(self.core_in.at[i, k], ("c", i, k))
-            self.acc[i, k] = (self.acc[i, k].astype(f32) + self.core_in[i, k].astype(f32)).astype(bf16)
+            self.add(mask, k, None, self.core_in[i, k])
             for part in (0, 1):
                 self.pass_on(part, 0, mask, k)
             return
@@ -1313,12 +1486,9 @@
             self.along(part, k)
             return
         _, part, level, mask, k = event
-        i = self.masks.index(mask)
-        start, size = self.parts[part]
-        cell = self.level_in[part][level].at[self.cell(part, level, mask), k]
-        self.wait(cell, ("l", part, level, mask, k))
-        rows = pl.ds(start, size)
-        self.acc[i, k, rows] = (self.acc[i, k, rows].astype(f32) + cell[...].astype(f32)).astype(bf16)
+        index = self.cell(part, level, mask)
+        self.wait(self.level_in[part][level].at[index, k], ("l", part, level, mask, k))
+        self.add(mask, k, part, self.level_in[part][level][index, k])
         self.pass_on(part, level + 1, mask, k)
 
     def from_side(self, part, place, side):
@@ -1330,35 +1500,32 @@
     def along(self, part, k):
         place = nearest(self.z, self.n, k)
         up = place > self.z
-        start, size = self.parts[part]
-        rows = pl.ds(start, size)
 
         @pl.when((up & (self.z > 0)) | (jnp.logical_not(up) & (self.z < self.n - 1)))
         def _():
-            self.acc[0, k, rows] = (self.acc[0, k, rows].astype(f32) + self.from_side(part, place, 0)).astype(bf16)
+            self.add(0, k, part, self.from_side(part, place, 0))
 
         to = jnp.where(up, self.z + 1, self.z - 1)
         index = jnp.where((to == place) & jnp.logical_not(up), self.n, place)
         self.send(
-            self.acc.at[0, k, rows], self.seq_in[part].at[index], (self.dp, to), self.seq_sems.at[part, index], part
+            self.view(0, k, part), self.seq_in[part].at[index], (self.dp, to), self.seq_sems.at[part, index], part
         )
 
     def finish(self):
-        used = self.out.shape[0]
+        index = self.slot(0, 0)
         for part in (0, 1):
             start, size = self.parts[part]
-            kept = min(size, used - start)
-            rows = slice(start, start + kept)
-            self.out[rows, :] = self.acc[0, 0, pl.ds(start, kept)].astype(f32)
+            rows = slice(start, start + size)
+            self.out[rows, :] = self.slots[index, rows, :].astype(f32)
             for side, there in ((0, self.z > 0), (1, self.z < self.n - 1)):
 
                 @pl.when(there)
                 def _():
-                    self.out[rows, :] += self.from_side(part, self.z, side)[:kept]
+                    self.out[rows, :] += self.from_side(part, self.z, side)
 
         for index, part in enumerate(self.started):
-            start, size = (0, self.acc.shape[2]) if part is None else self.parts[part]
-            ref = self.acc.at[0, 0, pl.ds(start, size)]
+            start, size = (0, self.slots.shape[1]) if part is None else self.parts[part]
+            ref = self.slots.at[0, pl.ds(start, size)]
             remote(ref, ref, self.send_sems.at[index], self.recv_sems.at[0], (self.dp, self.z)).wait_send()
 
 
@@ -1367,10 +1534,7 @@
     masks = 1 << bits
     half = rows // 32 * 16
     sizes = [half, rows - half]
-    shapes = [
-        pltpu.VMEM((masks, seq_size, rows, LANES), bf16),
-        pltpu.VMEM((masks, seq_size, rows, LANES), bf16),
-    ]
+    shapes = [pltpu.VMEM((masks, seq_size, rows, LANES), bf16), pltpu.VMEM((rows, LANES), f32)]
     for size in sizes:
         for level in range(bits):
             shapes.append(pltpu.VMEM((masks >> (level + 1), seq_size, size, LANES), bf16))
@@ -1378,7 +1542,6 @@
         shapes.append(pltpu.VMEM((seq_size + 1, size, LANES), bf16))
     count = masks * seq_size + 2 * (masks - 1) * seq_size + 2 * (seq_size - 1)
     shapes += [
-        pltpu.SemaphoreType.DMA((masks, seq_size)),
         pltpu.SemaphoreType.DMA((count,)),
         pltpu.SemaphoreType.DMA((count,)),
         pltpu.SemaphoreType.DMA((2, seq_size + 1)),
@@ -1386,12 +1549,12 @@
     return shapes
 
 
-def make_scatter(dp_size, seq_size, out, refs):
+def make_scatter(dp_size, seq_size, slots, refs):
     bits = dp_size.bit_length() - 2
-    acc, core_in, *rest = refs
+    core_in, total, *rest = refs
     level_in = [rest[:bits], rest[bits : 2 * bits]]
     rest = rest[2 * bits :]
-    return Scatter(dp_size, seq_size, out, acc, core_in, level_in, rest[:2], *rest[2:])
+    return Scatter(dp_size, seq_size, slots, total, core_in, level_in, rest[:2], *rest[2:])
 
 
 ANY = pl.BlockSpec(memory_space=pl.ANY)
@@ -1407,9 +1570,12 @@
     devices = dp_size * n
     block = inputs.shape[2]
     length = n * block
-    a_rows, m_rows = attn_params.shape[0] // LANES, mlp_params.shape[0] // LANES
-    a_own, m_own = to_rows(attn_params), to_rows(mlp_params)
-    a_pad, m_pad = a_own.shape[0], m_own.shape[0]
+    tokens = 2 * block
+    a_layout = attn_layout(attn_params.shape[0] // LANES, devices)
+    m_layout = mlp_layout_of(mlp_params.shape[0] // LANES, devices)
+    a_raw, m_raw = to_rows(attn_params), to_rows(mlp_params)
+    a_rows, m_rows = a_layout.slot_rows, m_layout.slot_rows
+    wide = [pltpu.VMEM((raw.shape[0] + 2 * MARGIN, LANES), f32) for raw in (a_raw, m_raw)]
     seg_rows = jnp.pad(segments.reshape(2, block // LANES, LANES), ((0, 0), (0, 8 - block // LANES), (0, 0)))
     send, recv = gather_counts(dp_size, n)
     dma = pltpu.SemaphoreType.DMA
@@ -1422,19 +1588,23 @@
     (
         m_slots, cot_own, n1, wqkv, qt, kt, qh, kh, vh, x_own, w_proj, vec, seg_all, lse, att,
     ) = pl.pallas_call(
-        functools.partial(forward_kernel, dp_size, n, a_rows),
-        out_shape=[shape_of((devices, m_pad, LANES), bf16), own]
+        functools.partial(forward_kernel, dp_size, n, a_layout, m_layout),
+        out_shape=[shape_of((devices, m_rows, LANES), bf16), own]
         + kept
         + [
             own, shape_of((D, D), bf16), shape_of((8, D), f32),
             shape_of((n, 8, LANES), jnp.int32), shape_of((8, length), f32), shape_of((2, 2, block, HALF_COLS), bf16),
         ],
-        in_specs=[ANY] * 5,
+        in_specs=[ANY] * 3 + [LOCAL] * 2,
         out_specs=[ANY] * 9 + [LOCAL] * 6,
         scratch_shapes=[pltpu.VMEM(like.shape, like.dtype) for like in kept]
         + [
-            pltpu.VMEM((devices, a_pad, LANES), bf16),
-            pltpu.VMEM((devices * a_rows, LANES), f32),
+            pltpu.VMEM((devices, a_rows, LANES), bf16),
+            pltpu.VMEM((a_rows, LANES), bf16),
+            pltpu.VMEM((m_rows, LANES), bf16),
+        ]
+        + wide
+        + [
             pltpu.VMEM((n, block, D), bf16),
             pltpu.VMEM((HALF_COLS, length), bf16),
             pltpu.VMEM((length, LANES), jnp.int32),
@@ -1442,63 +1612,35 @@
             pltpu.VMEM((HALF_COLS, length), f32),
             pltpu.VMEM((2, block, HALF_COLS), bf16),
             dma((send,)), dma((recv,)), dma((send,)), dma((recv,)), dma((2,)),
-            dma((2, 4)), dma((2, n)), dma((2, 2)), dma((2, 2)), dma((len(kept),)),
+            dma((3, 4)), dma((3, n)), dma((2, 2)), dma((2, 2)), dma((len(kept),)),
         ],
         compiler_params=pltpu.CompilerParams(collective_id=0, has_side_effects=True, vmem_limit_bytes=VMEM_LIMIT),
-    )(inputs[:, 0], seg_rows, cotangent[:, 0], a_own, m_own)
-
-    tokens = 2 * block
-    m_grads, out_own, d_mid, d_att, g_proj, g_bias = pl.pallas_call(
-        functools.partial(mlp_kernel, m_rows),
-        out_shape=[
-            shape_of((devices, m_pad, LANES), bf16),
-            shape_of((tokens, D), bf16), shape_of((tokens, D), f32), shape_of((2, tokens, HALF_COLS), bf16),
-            shape_of((D * ROW_D, LANES), f32), shape_of((1, D), f32),
-        ],
-        in_specs=[ANY] + [LOCAL] * 5,
-        out_specs=[ANY] + [LOCAL] * 5,
+    )(inputs[:, 0], seg_rows, cotangent[:, 0], a_raw, m_raw)
+
+    out_back, grad_back, a_sum, m_sum = pl.pallas_call(
+        functools.partial(backward_kernel, dp_size, n, a_layout, m_layout),
+        out_shape=[own, own, shape_of((a_layout.rows, LANES), f32), shape_of((m_layout.rows, LANES), f32)],
+        in_specs=[ANY] * 12 + [LOCAL] * 3,
+        out_specs=[ANY] * 2 + [LOCAL] * 2,
         scratch_shapes=[
-            pltpu.VMEM((devices, m_pad, LANES), bf16),
-            pltpu.VMEM((devices * m_rows, LANES), f32),
-            pltpu.VMEM((D, FF), bf16), pltpu.VMEM((FF, D), bf16),
-            pltpu.VMEM((tokens, D), f32), pltpu.VMEM((tokens, D), bf16),
-            pltpu.VMEM((tokens, D), f32), pltpu.VMEM((tokens, D), f32),
-            pltpu.VMEM((1, FF), f32), pltpu.VMEM((1, FF), f32),
-            dma(()), dma((4,)),
-        ],
-        compiler_params=pltpu.CompilerParams(vmem_limit_bytes=VMEM_LIMIT),
-    )(m_slots, x_own.reshape(tokens, D), cot_own.reshape(tokens, D), att.reshape(2, tokens, HALF_COLS), w_proj, vec)
-
-    out_back, grad_back, a_sum, m_sum = pl.pallas_call(
-        functools.partial(backward_kernel, dp_size, n, a_rows),
-        out_shape=[own, own, shape_of((a_rows, LANES), f32), shape_of((m_rows, LANES), f32)],
-        in_specs=[ANY] * 12 + [LOCAL] * 5,
-        out_specs=[ANY] * 2 + [LOCAL] * 2,
-        scratch_shapes=[pltpu.VMEM(like.shape, like.dtype) for like in kept]
-        + [
+            pltpu.VMEM((devices, m_rows, LANES), bf16),
+            pltpu.VMEM((devices, a_rows, LANES), bf16),
+            pltpu.VMEM((2, block, D), bf16),
+            pltpu.VMEM((tokens, D), bf16),
             pltpu.VMEM((tokens, D), f32),
-            pltpu.VMEM((2, block, D), bf16),
-            pltpu.VMEM((devices * a_rows, LANES), f32),
+            pltpu.VMEM((2, tokens, HALF_COLS), bf16),
             pltpu.VMEM((n, block, HALF_COLS), bf16),
-            pltpu.VMEM((HALF_COLS, length), bf16),
-            pltpu.VMEM((HALF_HEADS, length, LANES), bf16),
-            pltpu.VMEM((length, LANES), jnp.int32),
-            pltpu.VMEM((length, block), f32),
-            pltpu.VMEM((length, block), f32),
-            pltpu.VMEM((HALF_HEADS // 2, length, LANES), f32),
-            pltpu.VMEM((HALF_HEADS // 2, length, LANES), f32),
-            pltpu.VMEM((HALF_COLS, length), f32),
-            pltpu.VMEM((3, length, HALF_COLS), bf16),
-            pltpu.VMEM((3, block, D), f32),
             pltpu.VMEM((2, block, D), f32),
-            dma((4, 2)), dma((2, 2)), dma((2, 2)), dma(()), dma((9,)),
+            pltpu.VMEM((1, D), f32),
         ]
-        + scatter_scratch(dp_size, n, m_pad)
-        + scatter_scratch(dp_size, n, a_pad),
+        + wide
+        + [dma((4, 2)), dma((2, 2)), dma((2, 2)), dma((12,))]
+        + scatter_scratch(dp_size, n, m_rows)
+        + scatter_scratch(dp_size, n, a_rows),
         compiler_params=pltpu.CompilerParams(collective_id=1, has_side_effects=True, vmem_limit_bytes=VMEM_LIMIT),
     )(
-        out_own, m_grads, g_proj, n1, wqkv, qt, kt, qh, kh, vh, d_mid, x_own,
-        d_att, g_bias, vec, seg_all, lse,
+        m_slots, x_own, n1, wqkv, qt, kt, qh, kh, vh,
+        cot_own.reshape(tokens, D), att.reshape(2, tokens, HALF_COLS), w_proj, vec, seg_all, lse,
     )
     return (
         out_back[:, None],

time: 220 us -> 214 us (0.973)
  Pallas kernels: 209 us -> 203 us
    pallas_call x3 -> x2, Pallas kernels: 209 us -> 203 us  [the longest x1 108 us: per_chip_sequence(): pl.pallas_call(functools.partial(backward_kernel, dp_size, n, a_layout, m...]
where the time goes in v3:
time: 214 us; the launch traced here: 213 us
  Pallas kernels  203 us (95%)
  local copies, waits for them, and re-layouts  7.05 us (3%)
  other arithmetic  2.47 us (1%)
    pallas_call x1, Pallas kernels, per_chip_sequence(): pl.pallas_call(functools.partial(backward_kernel, dp_size, n, a_layout, m...  108 us
    pallas_call x1, Pallas kernels, per_chip_sequence(): pl.pallas_call(functools.partial(forward_kernel, dp_size, n, a_layout, m_...  95.6 us

profile of v3, /device:TPU:0, one launch (start us, length us, event | category | flops | bytes accessed | tf_op | source)
XLA Modules:
  0.0 213.4 jit_solution(2629920145885656835)
XLA Ops:
  0.6 1.3 pad.12.seg_in
  1.9 1.6 pad.13.a_raw
  3.5 1.7 pad.14.m_raw
  5.2 95.6 %shard_map.84 = (bf16[32,1200,128]{2,1,0:T(8,128)(2,1)}, bf16[2,256,768]{2,1,0:T(8,128)(2,1)}, bf16[1024,768]{1,0:T(8,128)(2,1)}, bf16[3,768,384]{2,1,0:T(8,128)...) custom-call(bf16[2,256,768]{2,1,0:T(8,128)(2,1)} %bitcast.19, ...), custom_call_target="tpu_custom_call" | custom-call | tf_op jit(solution)/shard_map/pallas_call | solution.py:1590
  100.8 107.6 %shard_map.85 = (bf16[2,256,768]{2,1,0:T(8,128)(2,1)}, bf16[2,256,768]{2,1,0:T(8,128)(2,1)}, f32[577,128]{1,0:T(8,128)}, f32[1154,128]{1,0:T(8,128)}) custom-call(bf16[32,1200,128]{2,1,0:T(8,128)(2,1)} %get-tuple-element.23.m_slots, bf16[2,256,768]{2,1,0:T(8,128)(2,1)} %get-tuple-element.24.x_own_in, bf16[1024,768]{1,0:T(8,128)(2,1)} %get-tuple-element.25.n1_in, ...), custom_call_target="tpu_custom_call" | custom-call | tf_op jit(solution)/shard_map/pallas_call | solution.py:1620
  208.5 0.0 copy-start
  208.5 0.0 copy-start.2
  208.5 2.5 %bitcast_convert_fusion = f32[2,1,256,768]{3,2,1,0:T(8,128)} fusion(bf16[2,256,768]{2,1,0:T(8,128)(2,1)} %get-tuple-element.39), kind=kLoop, calls=%fused_computation | loop fusion | flops 393216 | bytes 2359296
  210.9 0.0 copy-done
  210.9 0.0 copy-start.1
  210.9 0.9 copy.14
  211.8 0.0 copy-done.2
  211.8 0.7 copy.15
  212.6 0.0 copy-done.1
  212.6 0.9 copy.16
Async XLA Ops:
  208.5 2.5 %copy-start = (bf16[2,256,768]{2,1,0:T(8,128)(2,1)S(1)}, bf16[2,256,768]{2,1,0:T(8,128)(2,1)}, u32[]{:S(2)}) copy-start(bf16[2,256,768]{2,1,0:T(8,128)(2,1)} %get-tuple-element.38) | copy-start | bytes 2359300
  208.5 3.4 %copy-start.2 = (f32[577,128]{1,0:T(8,128)S(1)}, f32[577,128]{1,0:T(8,128)}, u32[]{:S(2)}) copy-start(f32[577,128]{1,0:T(8,128)} %get-tuple-element.40) | copy-start | bytes 886276
  210.9 1.6 copy-start.1

commit v4 on v3

--- a/solution.py
+++ b/solution.py
@@ -212,10 +212,9 @@
                 self.send(mask, i, part, (self.dp ^ bit, self.z), self.recv_sem(0, part, mask | bit, i))
         self.send(mask, i, part, (self.dp ^ 1, self.z), self.recv_sem(1, part, mask, i))
 
-    def begin_seq(self):
-        for part in (0, 1):
-            for up in (True, False):
-                self.along(0, part, up)
+    def begin_seq(self, part):
+        for up in (True, False):
+            self.along(0, part, up)
 
     def begin_bits(self):
         for level in range(len(self.bits)):
@@ -226,14 +225,17 @@
             self.send(0, 0, part, (self.dp ^ 1, self.z), self.recv_sem(1, part, 0, 0))
 
     def begin(self):
-        self.begin_seq()
+        self.begin_seq(0)
+        self.begin_seq(1)
         self.begin_bits()
 
-    def events(self, begin=0, seq_gap=1, level_gap=1):
+    def events(self, seq_times=None, own=0.0, level_gap=1.0):
+        if seq_times is None:
+            seq_times = [(i + 1.0, i + 1.5) for i in range(self.n - 1)]
         out = []
         for i in range(self.n):
             for part in (0, 1):
-                at = begin + (i + 0.5 * part - 0.5) * seq_gap if i else 0
+                at = seq_times[i - 1][part] if i else own
                 if i:
                     out.append((at, (part, 0, i)))
                 order = self.orders[part]
@@ -552,18 +554,20 @@
 MARGIN = 32
 VMEM_LIMIT = 63 * 2**20
 
-A_TIMES = (3.0, 6.0, 4.0)
-M_TIMES = (12.0, 9.0, 6.0)
-M_OWN = 8.0
-M_SEQ = 0.0
-M_BITS = 4.0
+A_SEQ = ((6.0, 9.0), (12.0, 15.0), (18.0, 21.0))
+A_OWN = (1.0, 6.1)
+M_SEQ = ((16.5, 21.0), (25.5, 30.0), (34.5, 39.0))
+M_OWN = (8.0, 8.6)
+M_BEGIN = (0.0, -1.1, 4.0)
 SEND_X = (6.0, 6.0, 6.0, 6.0)
-SHARE_X = 28.0
+SHARE_X = 24.5
 SEND_COT = (45.0, 45.0)
-FORWARD_START = 30.0
-HEAD_FORWARD = 3.3
+FORWARD_START = 36.1
+PROJECT = 4.0
+HEAD_FORWARD = 2.9
 BACKWARD_FIRST = 6.5
 BACKWARD_START = 8.0
+M_BACK = (6.0, 9.6, (9.0, 19.0), 0.5)
 A_BACK = (6.0, 5.0, (5.0, 10.0), 1.0)
 HEAD_BACKWARD = 5.8
 
@@ -856,7 +860,7 @@
     m_slots, cot_own, n1_out, wqkv_out, qt_out, kt_out, qh_out, kh_out, vh_out,
     x_own, w_proj, vec, seg_all, lse, att,
     n1, wqkv, qt, kt, qh, kh, vh,
-    a_slots, a_own, m_own, a_wide, m_wide, x_all, vt, seg_col, scores, ot, att_out,
+    a_slots, a_own, m_own, a_wide, m_wide, x_all, plain, vt, seg_col, scores, ot, att_out,
     a_send, a_recv, m_send, m_recv, own_sems, move_send, move_recv, cot_sems, swap_sems, keep_sems,
 ):
     place = Place(seq_size)
@@ -920,12 +924,13 @@
             place.worker(micro),
         ).start()
 
-    timed = [(time, (ga, event)) for time, event in ga.events(*A_TIMES)]
-    timed += [(time + (0 if event[2] else M_OWN), (gm, event)) for time, event in gm.events(*M_TIMES)]
+    timed = [(time, (ga, event)) for time, event in ga.events(A_SEQ, *A_OWN)]
+    timed += [(time, (gm, event)) for time, event in gm.events(M_SEQ, *M_OWN)]
     timed += [
         (at, (Action(), action))
         for at, action in (
-            (SEND_X[0], send_segments), (SHARE_X, share_inputs), (M_SEQ, gm.begin_seq), (M_BITS, gm.begin_bits),
+            (SEND_X[0], send_segments), (SHARE_X, share_inputs), (M_BEGIN[2], gm.begin_bits),
+            (M_BEGIN[0], functools.partial(gm.begin_seq, 0)), (M_BEGIN[1], functools.partial(gm.begin_seq, 1)),
         )
     ]
     timed += [
@@ -975,32 +980,43 @@
         x_own[j] = x_all[place.own_block(j)]
     segment_columns(seg_all, seg_col, block)
 
+    project_plan = both.plan(FORWARD_START + 2, [(t, PROJECT / seq_size) for t in range(seq_size)])
+
     def project(t, carry):
+        handle([project_plan[turn] for turn in range(seq_size)], t)
         rows = pl.ds(pl.multiple_of(t * block, block), block)
         normal, _ = norm_parts(x_all[t].astype(f32))
         low = (normal * gain + shift).astype(bf16)
         n1[rows, :] = low
         query = (dot_nn(low, wqkv[0]) + bias_query).astype(bf16).astype(f32) * (1.0 / math.sqrt(HD))
-        key = dot_nn(low, wqkv[1])
+        key = dot_nn(low, wqkv[1]).astype(bf16)
         value = dot_nn(low, wqkv[2]) + bias_value
-        for result, across, heads in ((query, qt, qh), (key, kt, kh), (value, vt, vh)):
-            across[:, rows] = result.T.astype(bf16)
-            split_heads(result.astype(bf16), heads, rows)
+        qt[:, rows] = query.T.astype(bf16)
+        split_heads(key, kh, rows)
+        vt[:, rows] = value.T.astype(bf16)
+        plain[0, rows, :] = query.astype(bf16)
+        plain[1, rows, :] = key
+        plain[2, rows, :] = value.astype(bf16)
+        return carry
+
+    def other_forms(t, carry):
+        rows = pl.ds(pl.multiple_of(t * block, block), block)
+        split_heads(plain[0, rows, :], qh, rows)
+        split_heads(plain[2, rows, :], vh, rows)
+        kt[:, rows] = plain[1, rows, :].astype(f32).T.astype(bf16)
         return carry
 
     lax.fori_loop(0, seq_size, project, 0)
     keep = [
         pltpu.make_async_copy(src, dst, keep_sems.at[i])
-        for i, (src, dst) in enumerate(
-            [(n1, n1_out), (wqkv, wqkv_out), (qt, qt_out), (kt, kt_out), (qh, qh_out), (kh, kh_out), (vh, vh_out)]
-        )
+        for i, (src, dst) in enumerate([(n1, n1_out), (wqkv, wqkv_out), (qt, qt_out), (kh, kh_out)])
     ]
     for copy in keep:
         copy.start()
     lse[...] = jnp.zeros_like(lse)
     unit = HEAD_FORWARD / (seq_size * (seq_size + 1) // 2)
     points = [((h, i), unit * (i + 1)) for h in range(HALF_HEADS) for i in range(seq_size)]
-    plan = both.plan(FORWARD_START + 7, points)
+    plan = both.plan(FORWARD_START + 2 + PROJECT, points)
 
     def one_head(h, carry):
         head_rows = pl.ds(pl.multiple_of(h * HD, HD), HD)
@@ -1031,7 +1047,7 @@
         return carry
 
     lax.fori_loop(0, HALF_HEADS, one_head, 0)
-    both.until(math.inf)
+    both.until(FORWARD_START + 3 + PROJECT + HALF_HEADS * HEAD_FORWARD)
 
     for j in range(2):
         columns = pl.ds(pl.multiple_of(place.other_block(j) * block, block), block)
@@ -1044,6 +1060,14 @@
     for j in range(2):
         columns = pl.ds(pl.multiple_of(place.own_block(j) * block, block), block)
         att[place.core, j] = ot[:, columns].T.astype(bf16)
+    lax.fori_loop(0, seq_size, other_forms, 0)
+    keep += [
+        pltpu.make_async_copy(src, dst, keep_sems.at[4 + i])
+        for i, (src, dst) in enumerate([(kt, kt_out), (qh, qh_out), (vh, vh_out)])
+    ]
+    for copy in keep[4:]:
+        copy.start()
+    both.until(math.inf)
     for j in range(2):
         ref = att.at[1 - place.core, j]
         remote(ref, ref, swap_sems.at[0, j], swap_sems.at[1, j], place.sibling).wait_recv()
@@ -1197,7 +1221,7 @@
                     ]
 
     tokens = 2 * block
-    steps = Steps([(time, (sm, event)) for time, event in sm.events()])
+    steps = Steps([(time, (sm, event)) for time, event in sm.events(*M_BACK)])
     pl.run_scoped(
         mlp,
         pltpu.VMEM((tokens, D), bf16), pltpu.VMEM((2, tokens, HALF_COLS), bf16), pltpu.VMEM((D, D), bf16),
@@ -1557,6 +1581,18 @@
     return Scatter(dp_size, seq_size, slots, total, core_in, level_in, rest[:2], *rest[2:])
 
 
+def deliver_kernel(out_in, grad_in, a_in, m_in, out, grad, a_out, m_out, sems):
+    copies = [
+        pltpu.make_async_copy(src, dst, sems.at[i])
+        for i, (src, dst) in enumerate([(out_in, out), (a_in, a_out), (m_in, m_out)])
+    ]
+    for copy in copies:
+        copy.start()
+    grad[...] = grad_in[...].astype(f32)
+    for copy in copies:
+        copy.wait()
+
+
 ANY = pl.BlockSpec(memory_space=pl.ANY)
 LOCAL = pl.BlockSpec(memory_space=pltpu.VMEM)
 
@@ -1573,10 +1609,10 @@
     tokens = 2 * block
     a_layout = attn_layout(attn_params.shape[0] // LANES, devices)
     m_layout = mlp_layout_of(mlp_params.shape[0] // LANES, devices)
-    a_raw, m_raw = to_rows(attn_params), to_rows(mlp_params)
+    a_raw, m_raw = attn_params.reshape(-1, LANES), mlp_params.reshape(-1, LANES)
     a_rows, m_rows = a_layout.slot_rows, m_layout.slot_rows
     wide = [pltpu.VMEM((raw.shape[0] + 2 * MARGIN, LANES), f32) for raw in (a_raw, m_raw)]
-    seg_rows = jnp.pad(segments.reshape(2, block // LANES, LANES), ((0, 0), (0, 8 - block // LANES), (0, 0)))
+    seg_rows = segments.reshape(2, block // LANES, LANES)
     send, recv = gather_counts(dp_size, n)
     dma = pltpu.SemaphoreType.DMA
     across = shape_of((HALF_COLS, length), bf16)
@@ -1593,7 +1629,7 @@
         + kept
         + [
             own, shape_of((D, D), bf16), shape_of((8, D), f32),
-            shape_of((n, 8, LANES), jnp.int32), shape_of((8, length), f32), shape_of((2, 2, block, HALF_COLS), bf16),
+            shape_of((n, block // LANES, LANES), jnp.int32), shape_of((8, length), f32), shape_of((2, 2, block, HALF_COLS), bf16),
         ],
         in_specs=[ANY] * 3 + [LOCAL] * 2,
         out_specs=[ANY] * 9 + [LOCAL] * 6,
@@ -1606,6 +1642,7 @@
         + wide
         + [
             pltpu.VMEM((n, block, D), bf16),
+            pltpu.VMEM((3, length, HALF_COLS), bf16),
             pltpu.VMEM((HALF_COLS, length), bf16),
             pltpu.VMEM((length, LANES), jnp.int32),
             pltpu.VMEM((length, block), f32),
@@ -1642,12 +1679,15 @@
         m_slots, x_own, n1, wqkv, qt, kt, qh, kh, vh,
         cot_own.reshape(tokens, D), att.reshape(2, tokens, HALF_COLS), w_proj, vec, seg_all, lse,
     )
-    return (
-        out_back[:, None],
-        grad_back.astype(f32)[:, None],
-        a_sum.reshape(-1),
-        m_sum.reshape(-1),
-    )
+    out, grad, a_sum, m_sum = pl.pallas_call(
+        deliver_kernel,
+        out_shape=[own, shape_of(own.shape, f32), shape_of(a_sum.shape, f32), shape_of(m_sum.shape, f32)],
+        in_specs=[ANY, LOCAL, ANY, ANY],
+        out_specs=[ANY, LOCAL, ANY, ANY],
+        scratch_shapes=[dma((3,))],
+        compiler_params=pltpu.CompilerParams(vmem_limit_bytes=16 * 2**20),
+    )(out_back, grad_back, a_sum, m_sum)
+    return out[:, None], grad[:, None], a_sum.reshape(-1), m_sum.reshape(-1)
 
 
 def solution(mesh):

time: 214 us -> 204 us (0.953)
  Pallas kernels: 203 us -> 199 us
  local copies, waits for them, and re-layouts: 7.05 us -> 4.29 us
  other arithmetic: 2.47 us -> 0 us
    pallas_call x1, Pallas kernels: 95.6 us -> 88.2 us  [per_chip_sequence(): pl.pallas_call(functools.partial(forward_kernel, dp_size, n, a_layout, m_...]
    pad x3 -> x0, local copies, waits for them, and re-layouts: 4.57 us -> none  [the longest x2 3.28 us: to_rows(): jnp.pad(flat.reshape(rows, LANES), ((0, pad_rows(rows) - rows), (0, 0)))]
    unnamed x1 -> x0, other arithmetic: 2.47 us -> none
    pallas_call x0 -> x1, Pallas kernels: none -> 2.34 us  [per_chip_sequence(): pl.pallas_call(deliver_kernel, out_shape=[own, shape_of(own.shape, f32),...]
    unnamed x9 -> x8, local copies, waits for them, and re-layouts: 2.48 us -> 4.29 us
where the time goes in v4:
time: 204 us
  Pallas kernels  199 us (98%)
  local copies, waits for them, and re-layouts  4.29 us (2%)
    pallas_call x1, Pallas kernels, per_chip_sequence(): pl.pallas_call(functools.partial(backward_kernel, dp_size, n, a_layout, m...  108 us
    pallas_call x1, Pallas kernels, per_chip_sequence(): pl.pallas_call(functools.partial(forward_kernel, dp_size, n, a_layout, m_...  88.2 us
    unnamed x8, local copies, waits for them, and re-layouts  4.29 us

profile of v4, /device:TPU:0, one launch (start us, length us, event | category | flops | bytes accessed | tf_op | source)
XLA Modules:
  0.0 203.8 jit_solution(3688093561186911711)
XLA Ops:
  0.6 88.2 %shard_map.84 = (bf16[32,1200,128]{2,1,0:T(8,128)(2,1)}, bf16[2,256,768]{2,1,0:T(8,128)(2,1)}, bf16[1024,768]{1,0:T(8,128)(2,1)}, bf16[3,768,384]{2,1,0:T(8,128)...) custom-call(bf16[2,256,768]{2,1,0:T(8,128)(2,1)} %bitcast.17, ...), custom_call_target="tpu_custom_call" | custom-call | tf_op jit(solution)/shard_map/pallas_call | solution.py:1626
  88.8 108.1 %shard_map.85 = (bf16[2,256,768]{2,1,0:T(8,128)(2,1)}, bf16[2,256,768]{2,1,0:T(8,128)(2,1)}, f32[577,128]{1,0:T(8,128)}, f32[1154,128]{1,0:T(8,128)}) custom-call(bf16[32,1200,128]{2,1,0:T(8,128)(2,1)} %get-tuple-element.27.m_slots, bf16[2,256,768]{2,1,0:T(8,128)(2,1)} %get-tuple-element.28.x_own_in, bf16[1024,768]{1,0:T(8,128)(2,1)} %get-tuple-element.29.n1_in, ...), custom_call_target="tpu_custom_call" | custom-call | tf_op jit(solution)/shard_map/pallas_call | solution.py:1657
  196.9 0.0 copy-start
  196.9 1.1 copy-done
  198.1 0.0 copy-start.1
  198.1 1.1 copy-done.1
  199.2 0.0 copy-start.2
  199.2 1.1 copy-done.2
  200.3 0.0 copy-start.3
  200.3 1.0 copy-done.3
  201.2 2.3 %shard_map.86 = (bf16[2,256,768]{2,1,0:T(8,128)(2,1)}, f32[2,256,768]{2,1,0:T(8,128)}, f32[577,128]{1,0:T(8,128)}, f32[1154,128]{1,0:T(8,128)}) custom-call(bf16[2,256,768]{2,1,0:T(8,128)(2,1)S(1)} %copy-done, bf16[2,256,768]{2,1,0:T(8,128)(2,1)S(1)} %copy-done.1, f32[577,128]{1,0:T(8,128)S(1)} %copy-done.3, f32[1154,128]{1,0:T(8,128)S(1)} %copy-done.2), custom_call_target="tpu_custom_call" | custom-call | tf_op jit(solution)/shard_map/pallas_call | solution.py:1682
Async XLA Ops:
  196.9 1.1 copy-start
  198.1 1.1 copy-start.1
  199.2 1.1 copy-start.2
  200.3 1.0 copy-start.3

commit v5 on v4

--- a/solution.py
+++ b/solution.py
@@ -568,8 +568,8 @@
 BACKWARD_FIRST = 6.5
 BACKWARD_START = 8.0
 M_BACK = (6.0, 9.6, (9.0, 19.0), 0.5)
-A_BACK = (6.0, 5.0, (5.0, 10.0), 1.0)
-HEAD_BACKWARD = 5.8
+A_BACK = (-4.0, 4.0, (6.0, 13.0), 2.0)
+HEAD_BACKWARD = 5.4
 
 ATTN_QKV = 2 * ROW_D
 ATTN_BQ = ATTN_QKV + D * ROW_QKV
@@ -740,9 +740,8 @@
             pl.when((s >= region[3]) & (s < region[3] + region[4]))(functools.partial(action, region))
 
     def pack(self, own, wide, slot, s):
-        edge = jnp.zeros((MARGIN, LANES), f32)
-        wide[:MARGIN, :] = edge
-        wide[MARGIN + own.shape[0] :, :] = edge
+        wide[:MARGIN, :] = jnp.zeros((MARGIN, LANES), f32)
+        wide[MARGIN + own.shape[0] :, :] = jnp.zeros((2 * MARGIN, LANES), f32)
         wide[MARGIN : MARGIN + own.shape[0], :] = own[...].astype(f32)
 
         def fill(region):
@@ -1611,7 +1610,7 @@
     m_layout = mlp_layout_of(mlp_params.shape[0] // LANES, devices)
     a_raw, m_raw = attn_params.reshape(-1, LANES), mlp_params.reshape(-1, LANES)
     a_rows, m_rows = a_layout.slot_rows, m_layout.slot_rows
-    wide = [pltpu.VMEM((raw.shape[0] + 2 * MARGIN, LANES), f32) for raw in (a_raw, m_raw)]
+    wide = [pltpu.VMEM((raw.shape[0] + 3 * MARGIN, LANES), f32) for raw in (a_raw, m_raw)]
     seg_rows = segments.reshape(2, block // LANES, LANES)
     send, recv = gather_counts(dp_size, n)
     dma = pltpu.SemaphoreType.DMA

time: 204 us -> 203 us (level)
  no operation moved by 1% of the time
where the time goes in v5:
time: 203 us; the launch traced here: 202 us
  Pallas kernels  197 us (97%)
  local copies, waits for them, and re-layouts  4.29 us (2%)
    pallas_call x1, Pallas kernels, per_chip_sequence(): pl.pallas_call(functools.partial(backward_kernel, dp_size, n, a_layout, m...  107 us
    pallas_call x1, Pallas kernels, per_chip_sequence(): pl.pallas_call(functools.partial(forward_kernel, dp_size, n, a_layout, m_...  88.2 us
    unnamed x8, local copies, waits for them, and re-layouts  4.29 us

profile of v5, /device:TPU:0, one launch (start us, length us, event | category | flops | bytes accessed | tf_op | source)
XLA Modules:
  0.0 202.4 jit_solution(1032715691441878279)
XLA Ops:
  0.6 88.2 %shard_map.84 = (bf16[32,1200,128]{2,1,0:T(8,128)(2,1)}, bf16[2,256,768]{2,1,0:T(8,128)(2,1)}, bf16[1024,768]{1,0:T(8,128)(2,1)}, bf16[3,768,384]{2,1,0:T(8,128)...) custom-call(bf16[2,256,768]{2,1,0:T(8,128)(2,1)} %bitcast.17, ...), custom_call_target="tpu_custom_call" | custom-call | tf_op jit(solution)/shard_map/pallas_call | solution.py:1625
  88.8 106.8 %shard_map.85 = (bf16[2,256,768]{2,1,0:T(8,128)(2,1)}, bf16[2,256,768]{2,1,0:T(8,128)(2,1)}, f32[577,128]{1,0:T(8,128)}, f32[1154,128]{1,0:T(8,128)}) custom-call(bf16[32,1200,128]{2,1,0:T(8,128)(2,1)} %get-tuple-element.27.m_slots, bf16[2,256,768]{2,1,0:T(8,128)(2,1)} %get-tuple-element.28.x_own_in, bf16[1024,768]{1,0:T(8,128)(2,1)} %get-tuple-element.29.n1_in, ...), custom_call_target="tpu_custom_call" | custom-call | tf_op jit(solution)/shard_map/pallas_call | solution.py:1656
  195.6 0.0 copy-start
  195.6 1.1 copy-done
  196.7 0.0 copy-start.1
  196.7 1.1 copy-done.1
  197.9 0.0 copy-start.2
  197.9 1.1 copy-done.2
  198.9 0.0 copy-start.3
  198.9 1.0 copy-done.3
  199.9 2.3 %shard_map.86 = (bf16[2,256,768]{2,1,0:T(8,128)(2,1)}, f32[2,256,768]{2,1,0:T(8,128)}, f32[577,128]{1,0:T(8,128)}, f32[1154,128]{1,0:T(8,128)}) custom-call(bf16[2,256,768]{2,1,0:T(8,128)(2,1)S(1)} %copy-done, bf16[2,256,768]{2,1,0:T(8,128)(2,1)S(1)} %copy-done.1, f32[577,128]{1,0:T(8,128)S(1)} %copy-done.3, f32[1154,128]{1,0:T(8,128)S(1)} %copy-done.2), custom_call_target="tpu_custom_call" | custom-call | tf_op jit(solution)/shard_map/pallas_call | solution.py:1681
Async XLA Ops:
  195.6 1.1 copy-start
  196.7 1.1 copy-start.1
  197.9 1.1 copy-start.2
  198.9 1.0 copy-start.3
